TPU v7x, 32 devices: a whole 2x2x4 slice. The times are simulated.
32 devices in a mesh: field: 2 (over y), epoch: 4 (over z), sky: 4 (over x, core).
Axes of the slice: x: 2, y: 2, z: 4, core: 2. Of those that a mesh axis runs over, the one named last changes fastest.
Arguments:
- sky_scene: bfloat16 [4096, 2048], P(('field', 'epoch'), 'sky'), parts along dimension 0, may hold values from -6 to 6
- images: bfloat16 [16, 2048, 2048], P(('field', 'epoch'), None, 'sky'), parts along dimension 0, may hold values from -6 to 6
- psf_rows: bfloat16 [16, 25], P('field'), parts along dimension 0, may hold values from 0.0099487305 to 0.06982422
- psf_cols: bfloat16 [16, 25], P('field'), parts along dimension 0, may hold values from 0.0099487305 to 0.06982422
- offsets: int32 [16, 2], P('field'), parts along dimension 0, may hold values from -4 to 4, as said below
- epoch_weight: float32 [16], P('field'), parts along dimension 0, may hold values from 0.25 to 2
- column_mask: int32 [16, 2048], P('field', 'sky'), parts along dimension 0, may hold values 0 or 1
- coverage: int32 [16, 4, 4], P('field'), parts along dimension 0, may hold values from 0 to 1, as said below
Outputs:
- gradient: float32 [4096, 2048], P(('field', 'epoch'), 'sky'), parts along dimension 0
There are 2 independent parts, one for each index of `field`. A program takes and returns all parts, laid end to end along the dimension named above; each array names one. Nothing has to cross between parts.
Inputs may be any that keep to these rules, and one draw needn't show every extreme that they name: `offsets`: column 0 shifts rows and column 1 shifts columns. `coverage`: the tiles that one epoch covers form a rectangle of whole tiles that spans all tile rows or all but one of them, and all tile columns or all but one of them.
All inputs are finite; a program needn't handle non-finite values. No bound on the sum of `column_mask` on one device may be relied on, other than what follows from the above.
Results may differ from a plain program's by a relative error of at most 0.0045.
Values may be sent and summed in bfloat16 or wider, within the bound.
No kernel may reach another device: no remote copies, remote signals or barrier semaphores. Data moves between devices by JAX's collectives and lax.ppermute only.
A program may use at most 64 MiB of HBM per device.

v0:
```python
import jax
import jax.numpy as jnp
from jax import lax
from jax.sharding import PartitionSpec as P

TILE = 512
HALO = 16


def extended(value, sides, width):
    for axis, dim in sides:
        peers, length = (lax.axis_size(axis), value.shape[dim])
        up = [(i, (i + 1) % peers) for i in range(peers - 1)]
        down = [(j, i) for i, j in up]
        last = lax.slice_in_dim(value, length - width, length, axis=dim)
        initial = lax.slice_in_dim(value, 0, width, axis=dim)
        before = lax.ppermute(last, axis, up)
        after = lax.ppermute(initial, axis, down)
        value = jnp.concatenate([before, value, after], axis=dim)
    return value


def band_tables(kernels, shifts, count_in, count_out):
    row_index = lax.broadcasted_iota(jnp.int32, (count_in, count_out), 0)
    col_index = lax.broadcasted_iota(jnp.int32, (count_in, count_out), 1)
    spread = kernels.shape[1]
    half_width = (spread - 1) // 2
    position = (
        (row_index - col_index)[None]
        - shifts[:, None, None]
        + half_width
        - (count_in - count_out) // 2
    )
    band_table = jnp.zeros((kernels.shape[0], count_in, count_out), jnp.float32)
    for each_tap in range(spread):
        band_table = band_table + jnp.where(
            position == each_tap, kernels[:, each_tap, None, None].astype(jnp.float32), 0.0
        )
    return band_table.astype(jnp.bfloat16)


def epoch_block(window, row_table, col_table, image_block, factor):
    lifted = jnp.einsum("ki,kc->ic", row_table, window, preferred_element_type=jnp.float32).astype(
        jnp.bfloat16
    )
    modeled = jnp.dot(lifted, col_table, preferred_element_type=jnp.float32)
    residual = (factor * (modeled - image_block.astype(jnp.float32))).astype(jnp.bfloat16)
    pulled = jnp.einsum(
        "ic,kc->ik", residual, col_table, preferred_element_type=jnp.float32
    ).astype(jnp.bfloat16)
    return jnp.dot(row_table, pulled, preferred_element_type=jnp.float32)


def strip_plan(sky_scene, images, psf_rows, psf_cols, offsets, epoch_weight, column_mask, coverage):
    slab_cells = extended(sky_scene, (("sky", 1),), HALO)
    strip_cells = lax.all_gather(slab_cells, "epoch", axis=0, tiled=True)
    strip_cells = jnp.pad(strip_cells, ((HALO, HALO), (0, 0)))
    full_rows = strip_cells.shape[0] - 2 * HALO
    strip_width = sky_scene.shape[1]
    local_count = images.shape[0]
    epoch_base = lax.axis_index("epoch") * local_count
    tile_column = lax.axis_index("sky") * strip_width // TILE

    def per_epoch(local_epoch, running):
        epoch_now = epoch_base + local_epoch
        row_table = band_tables(
            psf_rows[epoch_now][None], offsets[epoch_now, 0][None], TILE + 2 * HALO, TILE
        )[0]
        col_table = band_tables(
            psf_cols[epoch_now][None],
            offsets[epoch_now, 1][None],
            strip_width + 2 * HALO,
            strip_width,
        )[0]
        observed = lax.dynamic_index_in_dim(images, local_epoch, 0, keepdims=False)
        weight = epoch_weight[epoch_now]
        mask_row = column_mask[epoch_now].astype(jnp.float32)
        for row_block in range(full_rows // TILE):
            covered_flag = coverage[epoch_now, row_block, tile_column]
            window = strip_cells[row_block * TILE : row_block * TILE + TILE + 2 * HALO]
            image_block = observed[row_block * TILE : (row_block + 1) * TILE]
            factor = 2.0 * weight * covered_flag.astype(jnp.float32) * mask_row

            def covered():
                return epoch_block(window, row_table, col_table, image_block, factor)

            def skipped():
                return jnp.zeros((TILE + 2 * HALO, strip_width + 2 * HALO), jnp.float32)

            grad_term = lax.cond(covered_flag > 0, covered, skipped)
            running = running.at[row_block * TILE : row_block * TILE + TILE + 2 * HALO].add(
                grad_term
            )
        return running

    running = lax.fori_loop(
        0,
        local_count,
        per_epoch,
        jnp.zeros((full_rows + 2 * HALO, strip_width + 2 * HALO), jnp.float32),
    )
    trimmed = running[HALO : HALO + full_rows]
    packed = jnp.concatenate([trimmed[:, :HALO], trimmed[:, strip_width + HALO :]], axis=1)
    center_raw = trimmed[:, HALO : HALO + strip_width]
    received = extended(packed, (("sky", 1),), HALO)
    center_cells = center_raw.at[:, :HALO].add(received[:, :HALO])
    center_cells = center_cells.at[:, strip_width - HALO :].add(received[:, 3 * HALO :])
    return lax.psum_scatter(center_cells, "epoch", scatter_dimension=0, tiled=True)


def on_device(sky_scene, images, psf_rows, psf_cols, offsets, epoch_weight, column_mask, coverage):
    return strip_plan(
        sky_scene, images, psf_rows, psf_cols, offsets, epoch_weight, column_mask, coverage
    )


def solution(mesh):
    return jax.shard_map(
        on_device,
        mesh=mesh,
        in_specs=(
            P(("field", "epoch"), "sky"),
            P(("field", "epoch"), None, "sky"),
            P("field", None),
            P("field", None),
            P("field", None),
            P("field"),
            P("field", "sky"),
            P("field", None, None),
        ),
        out_specs=P(("field", "epoch"), "sky"),
        check_vma=False,
    )
```

profile of v0, /device:TPU:0, one launch (start us, length us, event | category | flops | bytes accessed | tf_op | source)
XLA Modules:
  0.0 384.0 jit_solution(12242590850483263235)
XLA Ops:
  7.6 2.4 collective-permute-start
  11.3 4.0 %collective-permute-done.1 = bf16[512,16]{1,0:T(8,128)(2,1)S(1)} collective-permute-done((bf16[512,16]{1,0:T(8,128)(2,1)S(1)}, bf16[512,16]{1,0:T(8,128)(2,1)S(1)}, u32[]{:S(2)}, u32[]{:S(2)}) %collective-permute-start.1) | collective-permute-done | bytes 16416 | tf_op jit(solution)/shard_map/ppermute | solution.py:18
  15.3 2.2 pad_maximum_fusion
  17.7 58.4 %all-gather.2.cloned.1.call-done = bf16[2048,544]{1,0:T(8,128)(2,1)} async-done(((bf16[512,544]{1,0:T(8,128)(2,1)}), bf16[2048,544]{1,0:T(8,128)(2,1)}) %all-gather.2.cloned.1.call-update) | async-done | bytes 2228240 | tf_op jit(solution)/shard_map/all_gather | solution.py:56
  76.1 3.5 pad.24
  79.6 2.5 broadcast_in_dim.819
  82.0 166.3 %while.24 = (s32[]{:T(128)}, f32[2080,544]{0,1:T(8,128)}, s32[]{:T(128)}, s32[8,4,4]{0,2,1:T(4,128)}, s32[]{:T(128)}, /*index=5*/s32[8,2]{0,1:T(2,128)S(1)}, bf1...) while((s32[]{:T(128)}, f32[2080,544]{0,1:T(8,128)}, ...), condition=%wide.region_9.10_spmd, body=%wide.region_0.9_spmd.sunk | while | flops 4757068288 | bytes 58701516 | solution.py:96
  100.6 3.5 add_convert_fusion.5
  121.3 3.5 add_convert_fusion.4
  124.8 1.6 constant_dynamic-slice_fusion.13
  128.3 3.1 constant_dynamic-slice_fusion.16
  132.1 1.5 slice_add_fusion.8
  133.6 8.0 %scatter-add.40 = f32[2080,544]{0,1:T(8,128)} dynamic-update-slice(f32[2080,544]{0,1:T(8,128)} %get-tuple-element.1017, f32[544,544]{0,1:T(8,128)S(1)} %slice_add_fusion.8, s32[]{:T(128)} %constant.688.clone.1..sunk, s32[]{:T(128)} %constant.688.clone.1..sunk) | dynamic-update-slice | bytes 2367492 | tf_op jit(solution)/shard_map/while/body/eval_jaxpr/scatter-add | solution.py:91
  143.8 7.9 %scatter-add.41 = f32[2080,544]{0,1:T(8,128)} dynamic-update-slice(f32[2080,544]{0,1:T(8,128)} %scatter-add.40, f32[544,544]{0,1:T(8,128)S(1)} %slice_add_fusion.9, s32[]{:T(128)} %constant.694.clone.1..sunk, s32[]{:T(128)} %constant.688.clone.1..sunk) | dynamic-update-slice | bytes 2367492 | tf_op jit(solution)/shard_map/while/body/eval_jaxpr/scatter-add | solution.py:91
  152.5 1.5 slice_add_fusion.10
  154.0 7.8 %scatter-add.42 = f32[2080,544]{0,1:T(8,128)} dynamic-update-slice(f32[2080,544]{0,1:T(8,128)} %scatter-add.41, f32[544,544]{0,1:T(8,128)S(1)} %slice_add_fusion.10, s32[]{:T(128)} %constant.685.clone.1..sunk, s32[]{:T(128)} %constant.688.clone.1..sunk) | dynamic-update-slice | bytes 2367492 | tf_op jit(solution)/shard_map/while/body/eval_jaxpr/scatter-add | solution.py:91
  162.5 2.7 fusion.104
  183.8 3.5 add_convert_fusion.5
  204.5 3.5 add_convert_fusion.4
  208.0 1.6 constant_dynamic-slice_fusion.13
  211.5 3.1 constant_dynamic-slice_fusion.16
  216.8 8.0 %scatter-add.40 = f32[2080,544]{0,1:T(8,128)} dynamic-update-slice(f32[2080,544]{0,1:T(8,128)} %get-tuple-element.1017, f32[544,544]{0,1:T(8,128)S(1)} %slice_add_fusion.8, s32[]{:T(128)} %constant.688.clone.1..sunk, s32[]{:T(128)} %constant.688.clone.1..sunk) | dynamic-update-slice | bytes 2367492 | tf_op jit(solution)/shard_map/while/body/eval_jaxpr/scatter-add | solution.py:91
  225.5 1.5 slice_add_fusion.9
  227.0 7.9 %scatter-add.41 = f32[2080,544]{0,1:T(8,128)} dynamic-update-slice(f32[2080,544]{0,1:T(8,128)} %scatter-add.40, f32[544,544]{0,1:T(8,128)S(1)} %slice_add_fusion.9, s32[]{:T(128)} %constant.694.clone.1..sunk, s32[]{:T(128)} %constant.688.clone.1..sunk) | dynamic-update-slice | bytes 2367492 | tf_op jit(solution)/shard_map/while/body/eval_jaxpr/scatter-add | solution.py:91
  237.2 7.8 %scatter-add.42 = f32[2080,544]{0,1:T(8,128)} dynamic-update-slice(f32[2080,544]{0,1:T(8,128)} %scatter-add.41, f32[544,544]{0,1:T(8,128)S(1)} %slice_add_fusion.10, s32[]{:T(128)} %constant.685.clone.1..sunk, s32[]{:T(128)} %constant.688.clone.1..sunk) | dynamic-update-slice | bytes 2367492 | tf_op jit(solution)/shard_map/while/body/eval_jaxpr/scatter-add | solution.py:91
  245.7 2.7 fusion.104
  249.5 32.9 %collective-permute-start.2 = (f32[2048,16]{0,1:T(8,128)S(1)}, f32[2048,16]{0,1:T(8,128)S(1)}, u32[]{:S(2)}, u32[]{:S(2)}) collective-permute-start(f32[2048,16]{0,1:T(8,128)S(1)} %get-tuple-element.806), channel_id=1, source_target_pairs={{0,1},{1,2},{2,3},{4,5},{5,6},{6,7},{8,9},{9,10},{10,11},{12,13},{... | collective-permute-start | bytes 393224 | tf_op jit(solution)/shard_map/ppermute | solution.py:17
  283.0 5.4 %slice.992 = f32[2048,512]{0,1:T(8,128)} slice(f32[2080,544]{0,1:T(8,128)} %get-tuple-element.722), slice={[16:2064], [16:528]} | slice | bytes 8388608 | tf_op jit(solution)/shard_map/slice | solution.py:104
  289.8 2.3 fusion.67
  293.0 1.6 fusion.68
  294.6 80.0 %reduce-scatter.2.cloned.1.call-done = f32[512,512]{0,1:T(8,128)} async-done(((f32[2048,512]{0,1:T(8,128)}), f32[512,512]{0,1:T(8,128)}) %reduce-scatter.2.cloned.1.call-update) | async-done | bytes 1048592 | tf_op jit(solution)/shard_map/reduce_scatter | solution.py:108
  374.6 2.5 copy.13
  (55 shorter events, 23.3 us)
Async XLA Ops:
  6.5 69.5 %all-gather.2.cloned.1.call-start = ((), (), s32[]{:S(2)}) async-start(), calls=%async_computation.1 | async-start | bytes 3276800 | tf_op jit(solution)/shard_map/all_gather | solution.py:56
  7.6 3.7 collective-permute-start
  10.0 5.3 %collective-permute-start.1 = (bf16[512,16]{1,0:T(8,128)(2,1)S(1)}, bf16[512,16]{1,0:T(8,128)(2,1)S(1)}, u32[]{:S(2)}, u32[]{:S(2)}) collective-permute-start(bf16[512,16]{1,0:T(8,128)(2,1)S(1)} %get-tuple-element.808), channel_id=1, source_target_pairs={{1,0},{2,1},{3,2},{5,4},{6,5},{7,6},{9,8},{10,9},{11,10},{13,12},{... | collective-permute-start | bytes 49160 | tf_op jit(solution)/shard_map/ppermute | solution.py:18
  17.6 357.0 %reduce-scatter.2.cloned.1.call-start = ((), (), s32[]{:S(2)}) async-start(), calls=%async_computation.2 | async-start | bytes 5242880 | tf_op jit(solution)/shard_map/reduce_scatter | solution.py:108
  79.6 2.5 copy-start.4
  79.6 2.5 copy-start.5
  124.8 7.2 %copy-start = (bf16[544,512]{1,0:T(8,128)(2,1)}, bf16[544,512]{1,0:T(8,128)(2,1)S(1)}, u32[]{:S(2)}) copy-start(bf16[544,512]{1,0:T(8,128)(2,1)S(1)} %add_convert_fusion.4) | copy-start | bytes 1671172 | tf_op jit(solution)/shard_map/while
  208.0 7.2 %copy-start = (bf16[544,512]{1,0:T(8,128)(2,1)}, bf16[544,512]{1,0:T(8,128)(2,1)S(1)}, u32[]{:S(2)}) copy-start(bf16[544,512]{1,0:T(8,128)(2,1)S(1)} %add_convert_fusion.4) | copy-start | bytes 1671172 | tf_op jit(solution)/shard_map/while
  249.5 40.3 %collective-permute-start.2 = (f32[2048,16]{0,1:T(8,128)S(1)}, f32[2048,16]{0,1:T(8,128)S(1)}, u32[]{:S(2)}, u32[]{:S(2)}) collective-permute-start(f32[2048,16]{0,1:T(8,128)S(1)} %get-tuple-element.806), channel_id=1, source_target_pairs={{0,1},{1,2},{2,3},{4,5},{5,6},{6,7},{8,9},{9,10},{10,11},{12,13},{... | collective-permute-start | bytes 393224 | tf_op jit(solution)/shard_map/ppermute | solution.py:17
  288.5 4.5 %collective-permute-start.3 = (f32[2048,16]{0,1:T(8,128)S(1)}, f32[2048,16]{0,1:T(8,128)S(1)}, u32[]{:S(2)}, u32[]{:S(2)}) collective-permute-start(f32[2048,16]{0,1:T(8,128)S(1)} %get-tuple-element.805), channel_id=1, source_target_pairs={{1,0},{2,1},{3,2},{5,4},{6,5},{7,6},{9,8},{10,9},{11,10},{13,12},{... | collective-permute-start | bytes 393224 | tf_op jit(solution)/shard_map/ppermute | solution.py:18
Sparse Core Ops, SparseCore 0:
  17.7 58.3 all-gather.1
  294.7 79.8 reduce-scatter.1
where the time goes:
time: 388 us; the launch traced here: 384 us
  waiting for transfers between devices  143 us (37%)
  local copies, waits for them, and re-layouts  82.9 us (21%)
  loops' own time  69.7 us (18%)
  starting transfers between devices  37.9 us (10%)
  other arithmetic  36.6 us (9%)
  between operations  13.5 us (3%)
    reduce_scatter x1, waiting for transfers between devices, strip_plan(): lax.psum_scatter(center_cells, 'epoch', scatter_dimension=0, tiled=True)  80 us
    another operation x1, loops' own time, strip_plan(): lax.fori_loop(0, local_count, per_epoch, jnp.zeros((full_rows + 2 * HALO,...  69.6 us
    all_gather x1, waiting for transfers between devices, strip_plan(): strip_cells = lax.all_gather(slab_cells, 'epoch', axis=0, tiled=True)  58.4 us
    scatter-add x6, local copies, waits for them, and re-layouts, per_epoch(): running.at[row_block * TILE:row_block * TILE + TILE + 2 * HALO]  47.3 us
    ppermute x2, starting transfers between devices, extended(): before = lax.ppermute(last, axis, up)  35.3 us
    convert_element_type x4, other arithmetic, band_tables(): return band_table.astype(jnp.bfloat16)  14.1 us
    add x6, other arithmetic, per_epoch(): running.at[row_block * TILE:row_block * TILE + TILE + 2 * HALO]  8.93 us
  transfers between devices with their start and end apart: 6, of which 4 were waited for; matrix products, arithmetic and copies ran while one was open for 2% of the time, Pallas kernels for 0%

commit v1 on v0

v1 whole, which is shorter than its diff:
```python
import functools

import jax
import jax.numpy as jnp
from jax import lax
from jax.experimental import pallas as pl
from jax.experimental.pallas import tpu as pltpu
from jax.sharding import PartitionSpec as P

TILE = 512
HALO = 16
RIM = 2 * HALO
LANES = 128
SPAN = 256
STEP = SPAN - RIM
F32 = jnp.float32
BF16 = jnp.bfloat16
VMEM = pl.BlockSpec(memory_space=pltpu.VMEM)
SMEM = pl.BlockSpec(memory_space=pltpu.SMEM)
HBM = pl.BlockSpec(memory_space=pl.ANY)
PARAMS = pltpu.CompilerParams(vmem_limit_bytes=40 * 1024 * 1024)


def up_to(value, unit):
    return -(-value // unit) * unit


def dot(a, b, dims=((1,), (0,))):
    return lax.dot_general(a, b, (dims, ((), ())), preferred_element_type=F32)


def iota(shape, dim):
    return lax.broadcasted_iota(jnp.int32, shape, dim)


def selection(rows, cols, shift):
    return (iota((rows, cols), 1) == iota((rows, cols), 0) + shift).astype(BF16)


def toeplitz(taps, start, rows, width):
    line = jnp.concatenate([taps, jnp.zeros((1, width - LANES), F32)], axis=1)
    line = jnp.broadcast_to(line, (8, width))
    line = pltpu.roll(line, lax.rem(2 * width - start, width), 1)[0:1]
    line = jnp.broadcast_to(line, (rows, width))
    return pltpu.roll(line, 0, 1, stride=1, stride_axis=0).astype(BF16)


def stacked(taps, start):
    pair = toeplitz(taps, start, LANES, SPAN)
    return jnp.concatenate([pair[:, :LANES], pair[:, LANES:]], axis=0)


def row_of(values, index):
    return jnp.sum(jnp.where(iota(values.shape, 0) == index, values, 0), axis=0, keepdims=True)


def spans(length):
    return [(s, min(STEP, length - s)) for s in range(0, length, STEP)]


class Sizes:
    def __init__(self, images, sky_scene, psf_rows):
        self.local, self.height, self.width = images.shape
        self.rows = sky_scene.shape[0]
        self.epochs = psf_rows.shape[0]
        self.taps = psf_rows.shape[1]
        self.tile_rows = self.height // TILE
        self.wide = self.width + LANES
        self.line = up_to(self.height + RIM, LANES)
        self.chunk = up_to(self.rows, LANES)
        self.mask_rows = up_to(self.epochs, HALO)
        self.buffer_rows = HALO * (self.local + 1)
        self.blocks = self.height // self.rows


def cover_at(coverage_ref, epoch, row_tile, col_tile):
    last_row = coverage_ref.shape[1] - 1
    last_col = coverage_ref.shape[2] - 1
    inside = (row_tile >= 0) & (row_tile <= last_row) & (col_tile >= 0) & (col_tile <= last_col)
    value = coverage_ref[epoch, jnp.clip(row_tile, 0, last_row), jnp.clip(col_tile, 0, last_col)]
    return jnp.where(inside, value, 0).astype(F32)


def tile_of(position):
    return (position + TILE) // TILE - 1


def edges_kernel(sz, coverage_ref, images_ref, scene_ref, mask_ref, left_ref, right_ref, edge, sem):
    first = lax.axis_index("epoch") * sz.local
    column = lax.axis_index("sky") * sz.width
    places = (0, sz.width - LANES)
    copies = []
    for e in range(sz.local):
        for side in range(2):
            slot = 2 * e + side
            copies.append(
                pltpu.make_async_copy(
                    images_ref.at[e, :, pl.ds(places[side], LANES)],
                    edge.at[slot, pl.ds(HALO, sz.height), :],
                    sem.at[slot],
                )
            )
            copies[-1].start()
            edge[slot, 0:HALO] = jnp.zeros((HALO, LANES), BF16)
            tail = sz.line - sz.height - HALO
            edge[slot, sz.line - tail :] = jnp.zeros((tail, LANES), BF16)
    tail_at = HALO * sz.local
    for side, out in enumerate((left_ref, right_ref)):
        out[tail_at:, :] = jnp.zeros((HALO, sz.line), BF16)
        shift = 0 if side == 0 else LANES - RIM
        cells = dot(
            selection(RIM, LANES, shift),
            scene_ref[:, places[side] : places[side] + LANES],
            ((1,), (1,)),
        ).astype(BF16)
        for q in range(2):
            out[tail_at:, q * sz.chunk : q * sz.chunk + sz.rows] = cells[q * HALO : (q + 1) * HALO]
        good = mask_ref[:, places[side] : places[side] + LANES].astype(F32)
        if side == 1:
            good = pltpu.roll(good, HALO, 1)
        if sz.mask_rows > sz.epochs:
            good = jnp.concatenate(
                [good, jnp.zeros((sz.mask_rows - sz.epochs, LANES), F32)], axis=0
            )
        good = good.astype(BF16)
        for q in range(sz.mask_rows // HALO):
            at = 2 * sz.chunk + q * LANES
            out[tail_at:, at : at + LANES] = good[q * HALO : (q + 1) * HALO]
    for e in range(sz.local):
        for side, out in enumerate((left_ref, right_ref)):
            slot = 2 * e + side
            copies[slot].wait()
            for t in range(sz.tile_rows):
                here = slice(HALO + t * TILE, HALO + (t + 1) * TILE)
                factor = cover_at(coverage_ref, first + e, t, column // TILE)
                edge[slot, here] = edge[slot, here] * jnp.full((1, LANES), factor, F32).astype(BF16)
            good = row_of(mask_ref[:, places[side] : places[side] + LANES].astype(F32), first + e)
            shift = 0 if side == 0 else LANES - HALO
            pick = (iota((HALO, LANES), 1) == iota((HALO, LANES), 0) + shift) & (good > 0)
            out[HALO * e : HALO * (e + 1), :] = dot(
                pick.astype(F32).astype(BF16), edge[slot], ((1,), (1,))
            ).astype(BF16)


def edges(sz, coverage, images, scene, mask):
    shape = jax.ShapeDtypeStruct((sz.buffer_rows, sz.line), BF16)
    return pl.pallas_call(
        functools.partial(edges_kernel, sz),
        out_shape=(shape, shape),
        in_specs=[SMEM, HBM, VMEM, VMEM],
        out_specs=(VMEM, VMEM),
        scratch_shapes=[
            pltpu.VMEM((2 * sz.local, sz.line, LANES), BF16),
            pltpu.SemaphoreType.DMA((2 * sz.local,)),
        ],
        compiler_params=PARAMS,
        name="edges",
    )(coverage, images, scene, mask)


def widen_kernel(sz, scene_ref, mask_ref, before_ref, after_ref, wide_ref, good_ref):
    tail_at = HALO * sz.local

    def cells(ref):
        return jnp.concatenate(
            [ref[tail_at:, q * sz.chunk : q * sz.chunk + sz.rows] for q in range(2)], axis=0
        )

    def flags(ref):
        parts = []
        for q in range(sz.mask_rows // HALO):
            at = 2 * sz.chunk + q * LANES
            parts.append(ref[tail_at:, at : at + LANES])
        return jnp.concatenate(parts, axis=0) if len(parts) > 1 else parts[0]

    wide = dot(scene_ref[...], selection(sz.width, sz.wide, RIM))
    wide += dot(cells(before_ref), selection(RIM, sz.wide, 0), ((0,), (0,)))
    wide += dot(cells(after_ref), selection(RIM, sz.wide, sz.width + RIM), ((0,), (0,)))
    wide_ref[...] = wide.astype(BF16)
    own = mask_ref[...].astype(F32)
    if sz.mask_rows > sz.epochs:
        own = jnp.concatenate(
            [own, jnp.zeros((sz.mask_rows - sz.epochs, sz.width), F32)], axis=0
        )
    good = dot(own.astype(BF16), selection(sz.width, sz.wide, HALO))
    inner = iota((LANES, sz.wide), 0) < HALO
    zero = jnp.zeros((LANES, sz.wide), BF16)
    good += dot(flags(before_ref), jnp.where(inner, selection(LANES, sz.wide, 0), zero))
    good += dot(
        flags(after_ref), jnp.where(inner, selection(LANES, sz.wide, sz.width + HALO), zero)
    )
    good_ref[...] = good


def widen(sz, scene, mask, before, after):
    return pl.pallas_call(
        functools.partial(widen_kernel, sz),
        out_shape=(
            jax.ShapeDtypeStruct((sz.rows, sz.wide), BF16),
            jax.ShapeDtypeStruct((sz.mask_rows, sz.wide), F32),
        ),
        in_specs=[VMEM] * 4,
        out_specs=(VMEM, VMEM),
        compiler_params=PARAMS,
        name="widen",
    )(scene, mask, before, after)


def destination(slot, place):
    return (
        3 * (1 - place % 2),
        2 - place // 2,
        (2 * place + 1) % 5,
        place,
    )[slot]


def image_kernel(
    sz, slots, coverage_ref, offsets_ref, weight_ref,
    images_ref, mask_ref, taps_ref, before_ref, after_ref,
    out_ref, window, row_table, main_table, cross_table, rim_table, sem,
):
    step = pl.program_id(0)
    steps = pl.num_programs(0)
    place = lax.axis_index("epoch")
    first = place * sz.local
    column = lax.axis_index("sky") * sz.width

    def target(index):
        if slots is None:
            return index
        value = destination(slots[0], place)
        for i in range(1, len(slots)):
            value = jnp.where(index == i, destination(slots[i], place), value)
        return value

    def copies(index, slot):
        start = target(index) * sz.rows
        head = jnp.maximum(start - HALO, 0)
        foot = jnp.minimum(start + sz.rows, sz.height - HALO)
        made = []
        for e in range(sz.local):
            for n, (source, at, count) in enumerate(
                ((start, HALO, sz.rows), (head, 0, HALO), (foot, HALO + sz.rows, HALO))
            ):
                made.append(
                    pltpu.make_async_copy(
                        images_ref.at[e, pl.ds(pl.multiple_of(source, HALO), count), :],
                        window.at[slot, e, pl.ds(at, count), :],
                        sem.at[slot, e, n],
                    )
                )
        return made

    @pl.when(step == 0)
    def _():
        for copy in copies(0, 0):
            copy.start()
        for e in range(sz.local):
            epoch = first + e
            row_shift, col_shift = offsets_ref[epoch, 0], offsets_ref[epoch, 1]
            line = taps_ref[1, pl.ds(epoch, 1), :]
            row_table[e] = toeplitz(line, row_shift - 4, STEP, SPAN)
            line = taps_ref[2, pl.ds(epoch, 1), :]
            main = toeplitz(line, 12 - col_shift, SPAN, SPAN + LANES)[:, :SPAN]
            main_table[e] = main
            apart = (iota((SPAN, SPAN), 0) < LANES) != (iota((SPAN, SPAN), 1) < LANES)
            cross_table[e] = jnp.where(apart, main, jnp.zeros_like(main))
            enter = toeplitz(line, 28 - col_shift, HALO, SPAN)[:, :LANES]
            leave = toeplitz(line, SPAN + LANES - 116 - col_shift, HALO, SPAN + LANES)[:, :LANES]
            none = jnp.zeros((HALO, LANES), BF16)
            rim_table[e] = jnp.concatenate(
                [
                    jnp.concatenate([enter, none], axis=1),
                    jnp.concatenate([none, leave], axis=1),
                ],
                axis=0,
            )

    slot = step % 2

    @pl.when(step + 1 < steps)
    def _():
        for copy in copies(step + 1, (step + 1) % 2):
            copy.start()

    for copy in copies(step, slot):
        copy.wait()
    start = target(step) * sz.rows
    zones = (
        (0, HALO, tile_of(start - HALO)),
        (HALO, HALO + sz.rows, tile_of(start)),
        (HALO + sz.rows, RIM + sz.rows, tile_of(start + sz.rows)),
    )
    total = [None] * (sz.width // LANES)

    def add(at, value):
        for n in range(value.shape[1] // LANES):
            piece = value[:, n * LANES : (n + 1) * LANES]
            k = at + n
            total[k] = piece if total[k] is None else total[k] + piece

    for e in range(sz.local):
        epoch = first + e
        twice = -2.0 * weight_ref[epoch]
        good = row_of(mask_ref[...].astype(F32), epoch)
        for begin, end, tile in zones:
            factor = good * cover_at(coverage_ref, epoch, tile, column // TILE)
            window[slot, e, begin:end] = window[slot, e, begin:end] * factor.astype(BF16)
        parts = []
        for s, n in spans(sz.rows):
            parts.append(
                (dot(row_table[e, :n, : n + RIM], window[slot, e, s : s + n + RIM]) * twice).astype(
                    BF16
                )
            )
        rows_done = jnp.concatenate(parts, axis=0) if len(parts) > 1 else parts[0]
        for b in range(0, sz.width, SPAN):
            add(b // LANES, dot(rows_done[:, b : b + SPAN], main_table[e]))
        for b in range(LANES, sz.width - LANES, SPAN):
            add(b // LANES, dot(rows_done[:, b : b + SPAN], cross_table[e]))
        rims = []
        size = min(sz.rows, LANES)
        for s in range(0, sz.rows, size):
            at = start + s
            base = pl.multiple_of((at // LANES) * LANES, LANES)
            both = jnp.concatenate(
                [
                    ref[HALO * e : HALO * (e + 1), pl.ds(base, SPAN)]
                    for ref in (before_ref, after_ref)
                ],
                axis=0,
            )
            if size < LANES:
                both = pltpu.roll(both.astype(F32), lax.rem(SPAN - (at - base), SPAN), 1)
                both = both.astype(BF16)
            rims.append((dot(both, row_table[e, :size], ((1,), (1,))) * twice).astype(BF16))
        rim = jnp.concatenate(rims, axis=1) if len(rims) > 1 else rims[0]
        rim_part = dot(rim, rim_table[e], ((0,), (0,)))
        add(0, rim_part[:, :LANES])
        add(sz.width // LANES - 1, rim_part[:, LANES:])
    for k, piece in enumerate(total):
        out_ref[:, k * LANES : (k + 1) * LANES] = piece.astype(BF16)


def image_blocks(sz, slots, coverage, offsets, weight, images, mask, taps, before, after):
    count = sz.blocks if slots is None else len(slots)
    return pl.pallas_call(
        functools.partial(image_kernel, sz, slots),
        grid=(count,),
        out_shape=jax.ShapeDtypeStruct((count * sz.rows, sz.width), BF16),
        in_specs=[SMEM, SMEM, SMEM, HBM, VMEM, VMEM, VMEM, VMEM],
        out_specs=pl.BlockSpec((sz.rows, sz.width), lambda i: (i, 0)),
        scratch_shapes=[
            pltpu.VMEM((2, sz.local, sz.rows + RIM, sz.width), BF16),
            pltpu.VMEM((sz.local, STEP, SPAN), BF16),
            pltpu.VMEM((sz.local, SPAN, SPAN), BF16),
            pltpu.VMEM((sz.local, SPAN, SPAN), BF16),
            pltpu.VMEM((sz.local, RIM, SPAN), BF16),
            pltpu.SemaphoreType.DMA((2, sz.local, 3)),
        ],
        compiler_params=PARAMS,
        cost_estimate=pl.CostEstimate(
            flops=count * 1400000000, bytes_accessed=count * 2000000, transcendentals=0
        ),
        name="image_blocks",
    )(coverage, offsets, weight, images, mask, taps, before, after)


def model_kernel(
    sz, coverage_ref, offsets_ref, weight_ref,
    wide_ref, head_ref, foot_ref, good_ref, taps_ref,
    out_ref, scene, lifted, residual, pulled,
):
    epoch = pl.program_id(0)
    place = lax.axis_index("epoch")
    start = place * sz.rows
    column = lax.axis_index("sky") * sz.width

    @pl.when(epoch == 0)
    def _():
        scene[0:RIM] = head_ref[...]
        scene[RIM : RIM + sz.rows] = wide_ref[...]
        scene[RIM + sz.rows :] = foot_ref[...]

    row_shift, col_shift = offsets_ref[epoch, 0], offsets_ref[epoch, 1]
    row_in = toeplitz(taps_ref[0, pl.ds(epoch, 1), :], -4 - row_shift, STEP, SPAN)
    row_out = toeplitz(taps_ref[1, pl.ds(epoch, 1), :], row_shift - 4, STEP, SPAN)
    col_in = stacked(taps_ref[3, pl.ds(epoch, 1), :], 28 + col_shift)
    col_out = stacked(taps_ref[2, pl.ds(epoch, 1), :], 28 - col_shift)

    for s, n in spans(sz.rows + RIM):
        lifted[s : s + n] = dot(row_in[:n, : n + RIM], scene[s : s + n + RIM]).astype(BF16)

    twice = 2.0 * weight_ref[epoch]
    good = row_of(good_ref[...], epoch) * twice
    lane = iota((1, sz.wide), 1)
    factors = []
    for row_tile in (tile_of(start - HALO), tile_of(start), tile_of(start + sz.rows)):
        left, here, right = (
            cover_at(coverage_ref, epoch, row_tile, tile_of(c))
            for c in (column - HALO, column, column + sz.width)
        )
        factors.append(
            good * jnp.where(lane < HALO, left, jnp.where(lane < HALO + sz.width, here, right))
        )
    for b in range(0, sz.wide, LANES):
        if b < sz.width:
            modeled = dot(lifted[:, b : b + SPAN], col_in)
        else:
            modeled = dot(lifted[:, b : b + LANES], col_in[:LANES])
        low, mid, high = (f[:, b : b + LANES] for f in factors)
        edge = sz.rows + HALO
        residual[0:HALO, b : b + LANES] = (modeled[0:HALO] * low).astype(BF16)
        residual[HALO:edge, b : b + LANES] = (modeled[HALO:edge] * mid).astype(BF16)
        residual[edge:, b : b + LANES] = (modeled[edge:] * high).astype(BF16)
    for b in range(0, sz.width, LANES):
        pulled[:, b : b + LANES] = dot(residual[:, b : b + SPAN], col_out).astype(BF16)
    for s, n in spans(sz.rows):
        term = dot(row_out[:n, : n + RIM], pulled[s : s + n + RIM])

        @pl.when(epoch == 0)
        def _():
            out_ref[s : s + n] = term

        @pl.when(epoch > 0)
        def _():
            out_ref[s : s + n] += term


def model_term(sz, coverage, offsets, weight, wide, head, foot, good, taps):
    high = sz.rows + RIM
    return pl.pallas_call(
        functools.partial(model_kernel, sz),
        grid=(sz.epochs,),
        out_shape=jax.ShapeDtypeStruct((sz.rows, sz.width), F32),
        in_specs=[SMEM, SMEM, SMEM, VMEM, VMEM, VMEM, VMEM, VMEM],
        out_specs=VMEM,
        scratch_shapes=[
            pltpu.VMEM((sz.rows + 2 * RIM, sz.wide), BF16),
            pltpu.VMEM((high, sz.wide), BF16),
            pltpu.VMEM((high, sz.wide), BF16),
            pltpu.VMEM((high, sz.width), BF16),
        ],
        compiler_params=PARAMS,
        cost_estimate=pl.CostEstimate(
            flops=sz.epochs * 1300000000, bytes_accessed=2000000, transcendentals=0
        ),
        name="model_term",
    )(coverage, offsets, weight, wide, head, foot, good, taps)


def on_device(sky_scene, images, psf_rows, psf_cols, offsets, epoch_weight, column_mask, coverage):
    sz = Sizes(images, sky_scene, psf_rows)
    peers = lax.axis_size("sky")
    depth = lax.axis_size("epoch")
    rightward = [(i, i + 1) for i in range(peers - 1)]
    leftward = [(i + 1, i) for i in range(peers - 1)]
    downward = [(i, i + 1) for i in range(depth - 1)]
    upward = [(i + 1, i) for i in range(depth - 1)]
    taps = jnp.stack([psf_rows, psf_rows[:, ::-1], psf_cols, psf_cols[:, ::-1]]).astype(F32)
    taps = jnp.pad(taps, ((0, 0), (0, 0), (0, LANES - sz.taps)))

    to_left, to_right = edges(sz, coverage, images, sky_scene, column_mask)
    before = lax.ppermute(to_right, "sky", rightward)
    after = lax.ppermute(to_left, "sky", leftward)
    wide, good = widen(sz, sky_scene, column_mask, before, after)
    head = lax.ppermute(wide[-RIM:], "epoch", downward)
    foot = lax.ppermute(wide[:RIM], "epoch", upward)

    def blocks(slots):
        return image_blocks(
            sz, slots, coverage, offsets, epoch_weight, images, column_mask, taps, before, after
        )

    if depth == 4:
        place = lax.axis_index("epoch")
        outer = (place == 0) | (place == 3)
        one = blocks((0,))
        got_one = lax.ppermute(one, "epoch", [(0, 1), (1, 0), (2, 3), (3, 2)])
        rest = blocks((1, 2, 3))
        two, three, own = (rest[i * sz.rows : (i + 1) * sz.rows] for i in range(3))
        got_two = lax.ppermute(two, "epoch", [(1, 2), (2, 1)])
        got_three = lax.ppermute(three, "epoch", [(0, 1), (3, 2)])
        merged = jnp.where(outer, two, three + got_one)
        got_four = lax.ppermute(merged, "epoch", [(0, 2), (3, 1), (1, 3), (2, 0)])
        model = model_term(sz, coverage, offsets, epoch_weight, wide, head, foot, good, taps)
        last = jnp.where(outer, got_one.astype(F32), got_two.astype(F32) + got_three.astype(F32))
        return model + own.astype(F32) + got_four.astype(F32) + last
    model = model_term(sz, coverage, offsets, epoch_weight, wide, head, foot, good, taps)
    summed = lax.psum_scatter(
        blocks(None).astype(F32), "epoch", scatter_dimension=0, tiled=True
    )
    return model + summed


def solution(mesh):
    return jax.shard_map(
        on_device,
        mesh=mesh,
        in_specs=(
            P(("field", "epoch"), "sky"),
            P(("field", "epoch"), None, "sky"),
            P("field", None),
            P("field", None),
            P("field", None),
            P("field"),
            P("field", "sky"),
            P("field", None, None),
        ),
        out_specs=P(("field", "epoch"), "sky"),
        check_vma=False,
    )
```

time: 388 us -> 72.1 us (0.19)
  the two profiles are of different devices: /device:TPU:0 before, /device:TPU:9 now
where the time goes in v1:
time: 72.1 us; the launch traced here: 71.6 us
  Pallas kernels  27.4 us (38%)
  waiting for transfers between devices  18.5 us (26%)
  starting transfers between devices  16.8 us (23%)
  local copies, waits for them, and re-layouts  7.22 us (10%)
  other arithmetic  1.48 us (2%)
    pallas_call x1, Pallas kernels, model_term(): pl.pallas_call(functools.partial(model_kernel, sz), grid=(sz.epochs,), ou...  15.4 us
    ppermute x1, waiting for transfers between devices, on_device(): got_two = lax.ppermute(two, 'epoch', [(1, 2), (2, 1)])  9.77 us
    pallas_call x2, Pallas kernels, image_blocks(): pl.pallas_call(functools.partial(image_kernel, sz, slots), grid=(count,),...  8.45 us
    unnamed x24, local copies, waits for them, and re-layouts  7.04 us
    ppermute x1, waiting for transfers between devices, on_device(): after = lax.ppermute(to_left, 'sky', leftward)  4.4 us
    ppermute x1, starting transfers between devices, on_device(): before = lax.ppermute(to_right, 'sky', rightward)  3.68 us
    ppermute x1, starting transfers between devices, on_device(): foot = lax.ppermute(wide[:RIM], 'epoch', upward)  3.21 us
    ppermute x1, starting transfers between devices, on_device(): head = lax.ppermute(wide[-RIM:], 'epoch', downward)  3.05 us
  transfers between devices with their start and end apart: 8, of which 5 were waited for; matrix products, arithmetic and copies ran while one was open for 1% of the time, Pallas kernels for 31%

profile of v1, /device:TPU:9, one launch (start us, length us, event | category | flops | bytes accessed | tf_op | source)
XLA Modules:
  0.0 71.6 jit_solution(3096647113746608590)
XLA Ops:
  0.0 0.8 %copy.10.coverage_ref = s32[8,4,4]{2,1,0:T(4,128)S(1)} copy(s32[8,4,4]{0,2,1:T(4,128)} %param.15) | data formatting | bytes 1024 | tf_op args[7]
  0.8 2.2 %copy-done = bf16[2,2048,512]{2,1,0:T(8,128)(2,1)S(1)} copy-done((bf16[2,2048,512]{2,1,0:T(8,128)(2,1)S(1)}, bf16[2,2048,512]{2,1,0:T(8,128)(2,1)}, u32[]{:S(2)}) %copy-start) | copy-done | bytes 4194328
  3.0 1.0 %copy-done.3 = bf16[512,512]{1,0:T(8,128)(2,1)S(1)} copy-done((bf16[512,512]{1,0:T(8,128)(2,1)S(1)}, bf16[512,512]{1,0:T(8,128)(2,1)}, u32[]{:S(2)}) %copy-start.3) | copy-done | bytes 524312
  4.0 0.7 copy-done.5
  4.8 0.0 copy-start.7
  4.8 2.7 %edges.1 = (bf16[48,2176]{1,0:T(8,128)(2,1)S(1)}, bf16[48,2176]{1,0:T(8,128)(2,1)S(1)}) custom-call(s32[8,4,4]{2,1,0:T(4,128)S(1)} %copy.10.coverage_ref, bf16[2,2048,512]{2,1,0:T(8,128)(2,1)S(1)} %copy-done, bf16[512,512]{1,0:T(8,128)(2,1)S(1)} %copy-done.3, s32[8,512]{1,0:T(8,128)S(1)} %copy-done.5), custom_call_target="tpu_custom_call" | custom-call | tf_op jit(solution)/shard_map/edges/pallas_call | solution.py:147
  7.5 3.7 %collective-permute-start = (bf16[48,2176]{1,0:T(8,128)(2,1)S(1)}, bf16[48,2176]{1,0:T(8,128)(2,1)S(1)}, u32[]{:S(2)}, u32[]{:S(2)}) collective-permute-start(bf16[48,2176]{1,0:T(8,128)(2,1)S(1)} %get-tuple-element.9), channel_id=1, source_target_pairs={{0,1},{1,2},{2,3},{4,5},{5,6},{6,7},{8,9},{9,10},{10,11},{12,13},{... | collective-permute-start | bytes 626696 | tf_op jit(solution)/shard_map/ppermute | solution.py:465
  11.2 1.9 %collective-permute-start.1 = (bf16[48,2176]{1,0:T(8,128)(2,1)S(1)}, bf16[48,2176]{1,0:T(8,128)(2,1)S(1)}, u32[]{:S(2)}, u32[]{:S(2)}) collective-permute-start(bf16[48,2176]{1,0:T(8,128)(2,1)S(1)} %get-tuple-element.10), channel_id=1, source_target_pairs={{1,0},{2,1},{3,2},{5,4},{6,5},{7,6},{9,8},{10,9},{11,10},{13,12},{... | collective-permute-start | bytes 626696 | tf_op jit(solution)/shard_map/ppermute | solution.py:466
  13.1 0.1 rev.6
  13.2 0.1 rev.7
  13.3 0.1 copy.11.offsets_ref
  13.4 0.5 collective-permute-done.before_ref
  13.9 4.4 %collective-permute-done.1.after_ref = bf16[48,2176]{1,0:T(8,128)(2,1)S(1)} collective-permute-done((bf16[48,2176]{1,0:T(8,128)(2,1)S(1)}, bf16[48,2176]{1,0:T(8,128)(2,1)S(1)}, u32[]{:S(2)}, u32[]{:S(2)}) %collective-permute-start.1) | collective-permute-done | bytes 208928 | tf_op jit(solution)/shard_map/ppermute | solution.py:466
  18.3 2.2 %copy-done.1 = bf16[2,2048,512]{2,1,0:T(8,128)(2,1)S(1)} copy-done((bf16[2,2048,512]{2,1,0:T(8,128)(2,1)S(1)}, bf16[2,2048,512]{2,1,0:T(8,128)(2,1)}, u32[]{:S(2)}) %copy-start.1) | copy-done | bytes 4194328
  20.5 2.7 %image_blocks.3 = bf16[512,512]{1,0:T(8,128)(2,1)S(1)} custom-call(s32[8,4,4]{2,1,0:T(4,128)S(1)} %copy.10.coverage_ref, s32[8,2]{1,0:T(8,128)S(1)} %copy.11.offsets_ref, f32[8]{0:T(128)S(1)} %copy-done.7, bf16[2,2048,512]{2,1,0:T(8,128)(2,1)S(1)} %copy-done.1, s32[8,512]{1,0:T(8,128)S(1)} %copy-done.6, f32[4,8,128]{2,1,0:T(8,128)S(1)} %fusion.7.taps_ref, ...), custom_call_target="tpu_custom_call" | custom-call | flops 1400000000 | bytes 2000000 | tf_op jit(solution)/shard_map/image_blocks/pallas_call | solution.py:348
  23.2 0.2 collective-permute-start.4
  23.4 0.9 %widen.1 = (bf16[512,640]{1,0:T(8,128)(2,1)S(1)}, f32[16,640]{1,0:T(8,128)S(1)}) custom-call(bf16[512,512]{1,0:T(8,128)(2,1)S(1)} %copy-done.4, s32[8,512]{1,0:T(8,128)S(1)} %copy-done.6, bf16[48,2176]{1,0:T(8,128)(2,1)S(1)} %collective-permute-done.before_ref, bf16[48,2176]{1,0:T(8,128)(2,1)S(1)} %collective-permute-done.1.after_ref), custom_call_target="tpu_custom_call" | custom-call | tf_op jit(solution)/shard_map/widen/pallas_call | solution.py:196
  24.3 3.2 %collective-permute-start.3 = (bf16[32,640]{1,0:T(8,128)(2,1)S(1)}, bf16[32,640]{1,0:T(8,128)(2,1)S(1)}, u32[]{:S(2)}, u32[]{:S(2)}) collective-permute-start(bf16[32,640]{1,0:T(8,128)(2,1)S(1)} %get-tuple-element.16), channel_id=1, source_target_pairs={{4,0},{8,4},{12,8},{5,1},{9,5},{13,9},{6,2},{10,6},{14,10},{7,3},{... | collective-permute-start | bytes 122888 | tf_op jit(solution)/shard_map/ppermute | solution.py:469
  27.5 3.1 %collective-permute-start.2 = (bf16[32,640]{1,0:T(8,128)(2,1)S(1)}, bf16[32,640]{1,0:T(8,128)(2,1)S(1)}, u32[]{:S(2)}, u32[]{:S(2)}) collective-permute-start(bf16[32,640]{1,0:T(8,128)(2,1)S(1)} %get-tuple-element.17), channel_id=1, source_target_pairs={{0,4},{4,8},{8,12},{1,5},{5,9},{9,13},{2,6},{6,10},{10,14},{3,7},{... | collective-permute-start | bytes 122888 | tf_op jit(solution)/shard_map/ppermute | solution.py:468
  30.6 5.8 %image_blocks.2 = bf16[1536,512]{1,0:T(8,128)(2,1)S(1)} custom-call(s32[8,4,4]{2,1,0:T(4,128)S(1)} %copy.10.coverage_ref, s32[8,2]{1,0:T(8,128)S(1)} %copy.11.offsets_ref, f32[8]{0:T(128)S(1)} %copy-done.7, bf16[2,2048,512]{2,1,0:T(8,128)(2,1)S(1)} %copy-done.2, s32[8,512]{1,0:T(8,128)S(1)} %copy-done.6, f32[4,8,128]{2,1,0:T(8,128)S(1)} %fusion.7.taps_ref, ...), custom_call_target="tpu_custom_call" | custom-call | flops 4200000000 | bytes 6000000 | tf_op jit(solution)/shard_map/image_blocks/pallas_call | solution.py:348
  36.4 0.0 collective-permute-done.4
  36.4 0.1 add_select_fusion
  36.5 0.6 collective-permute-start.5
  37.1 1.3 %collective-permute-start.7 = (bf16[512,512]{1,0:T(8,128)(2,1)S(1)}, bf16[512,512]{1,0:T(8,128)(2,1)S(1)}, u32[]{:S(2)}, u32[]{:S(2)}) collective-permute-start(bf16[512,512]{1,0:T(8,128)(2,1)S(1)} %get-tuple-element.14), channel_id=1, source_target_pairs={{0,4},{12,8},{1,5},{13,9},{2,6},{14,10},{3,7},{15,11},{16,20},{28,... | collective-permute-start | bytes 1572872 | tf_op jit(solution)/shard_map/ppermute | solution.py:484
  38.4 2.9 %collective-permute-start.6 = (bf16[512,512]{1,0:T(8,128)(2,1)S(1)}, bf16[512,512]{1,0:T(8,128)(2,1)S(1)}, u32[]{:S(2)}, u32[]{:S(2)}) collective-permute-start(bf16[512,512]{1,0:T(8,128)(2,1)S(1)} %get-tuple-element.15), channel_id=1, source_target_pairs={{4,8},{8,4},{5,9},{9,5},{6,10},{10,6},{7,11},{11,7},{20,24},{24,20... | collective-permute-start | bytes 1572872 | tf_op jit(solution)/shard_map/ppermute | solution.py:483
  41.3 0.0 collective-permute-done.3.foot_ref
  41.3 0.0 collective-permute-done.2.head_ref
  41.3 15.4 %model_term.1 = f32[512,512]{1,0:T(8,128)S(1)} custom-call(s32[8,4,4]{2,1,0:T(4,128)S(1)} %copy.10.coverage_ref, s32[8,2]{1,0:T(8,128)S(1)} %copy.11.offsets_ref, f32[8]{0:T(128)S(1)} %copy-done.7, bf16[512,640]{1,0:T(8,128)(2,1)S(1)} %get-tuple-element.11.wide_ref, bf16[32,640]{1,0:T(8,128)(2,1)S(1)} %collective-permute-done.2.head_ref, ...), custom_call_target="tpu_custom_call" | custom-call | flops 10400000000 | bytes 2000000 | tf_op jit(solution)/shard_map/model_term/pallas_call | solution.py:433
  56.7 2.9 %collective-permute-done.5 = bf16[512,512]{1,0:T(8,128)(2,1)S(1)} collective-permute-done((bf16[512,512]{1,0:T(8,128)(2,1)S(1)}, bf16[512,512]{1,0:T(8,128)(2,1)S(1)}, u32[]{:S(2)}, u32[]{:S(2)}) %collective-permute-start.5) | collective-permute-done | bytes 524320 | tf_op jit(solution)/shard_map/ppermute | solution.py:486
  59.6 0.9 %collective-permute-done.7 = bf16[512,512]{1,0:T(8,128)(2,1)S(1)} collective-permute-done((bf16[512,512]{1,0:T(8,128)(2,1)S(1)}, bf16[512,512]{1,0:T(8,128)(2,1)S(1)}, u32[]{:S(2)}, u32[]{:S(2)}) %collective-permute-start.7) | collective-permute-done | bytes 524320 | tf_op jit(solution)/shard_map/ppermute | solution.py:484
  60.5 9.8 %collective-permute-done.6 = bf16[512,512]{1,0:T(8,128)(2,1)S(1)} collective-permute-done((bf16[512,512]{1,0:T(8,128)(2,1)S(1)}, bf16[512,512]{1,0:T(8,128)(2,1)S(1)}, u32[]{:S(2)}, u32[]{:S(2)}) %collective-permute-start.6) | collective-permute-done | bytes 524320 | tf_op jit(solution)/shard_map/ppermute | solution.py:483
  70.3 1.4 %select_add_fusion = f32[512,512]{1,0:T(8,128)} fusion(bf16[512,512]{1,0:T(8,128)(2,1)S(1)} %collective-permute-done.7, bf16[512,512]{1,0:T(8,128)(2,1)S(1)} %collective-permute-done.6, bf16[512,512]{1,0:T(8,128)(2,1)S(1)} %collective-permute-done.4, bf16[512,512]{1,0:T(8,128)(2,1)S(1)} %collective-permute-done.5, f32[512,512]{1,0:T(8,128)S(1)} %model_term.1, ...), kind=kLoop, calls=%fused_computation | loop fusion | flops 2621440 | bytes 4718593 | tf_op jit(solution)/shard_map/add | solution.py:489
  (19 shorter events, 0.0 us)
Async XLA Ops:
  0.8 2.2 %copy-start = (bf16[2,2048,512]{2,1,0:T(8,128)(2,1)S(1)}, bf16[2,2048,512]{2,1,0:T(8,128)(2,1)}, u32[]{:S(2)}) copy-start(bf16[2,2048,512]{2,1,0:T(8,128)(2,1)} %images_ref.5) | copy-start | bytes 12582916
  3.0 1.0 %copy-start.3 = (bf16[512,512]{1,0:T(8,128)(2,1)S(1)}, bf16[512,512]{1,0:T(8,128)(2,1)}, u32[]{:S(2)}) copy-start(bf16[512,512]{1,0:T(8,128)(2,1)} %scene_ref.3) | copy-start | bytes 1572868
  4.0 0.7 %copy-start.5 = (s32[8,512]{1,0:T(8,128)S(1)}, s32[8,512]{1,0:T(8,128)}, u32[]{:S(2)}) copy-start(s32[8,512]{1,0:T(8,128)} %mask_ref.7) | copy-start | bytes 49156
  4.7 8.4 %copy-start.9 = (bf16[8,25]{1,0:T(8,128)(2,1)S(1)}, bf16[8,25]{1,0:T(8,128)(2,1)}, u32[]{:S(2)}) copy-start(bf16[8,25]{1,0:T(8,128)(2,1)} %param.10) | copy-start | bytes 1204
  4.7 8.5 %copy-start.8 = (bf16[8,25]{1,0:T(8,128)(2,1)S(1)}, bf16[8,25]{1,0:T(8,128)(2,1)}, u32[]{:S(2)}) copy-start(bf16[8,25]{1,0:T(8,128)(2,1)} %param.11) | copy-start | bytes 1204
  4.7 8.5 %copy-start.10 = (s32[8,2]{0,1:T(2,128)S(1)}, s32[8,2]{0,1:T(2,128)}, u32[]{:S(2)}) copy-start(s32[8,2]{0,1:T(2,128)} %param.12) | copy-start | bytes 196
  4.8 13.5 %copy-start.6 = (s32[8,512]{1,0:T(8,128)S(1)}, s32[8,512]{1,0:T(8,128)}, u32[]{:S(2)}) copy-start(s32[8,512]{1,0:T(8,128)} %mask_ref.7) | copy-start | bytes 49156
  4.8 13.5 %copy-start.7 = (f32[8]{0:T(128)S(1)}, f32[8]{0:T(128)}, u32[]{:S(2)}) copy-start(f32[8]{0:T(128)} %weight_ref.5) | copy-start | bytes 100
  7.5 6.4 %collective-permute-start = (bf16[48,2176]{1,0:T(8,128)(2,1)S(1)}, bf16[48,2176]{1,0:T(8,128)(2,1)S(1)}, u32[]{:S(2)}, u32[]{:S(2)}) collective-permute-start(bf16[48,2176]{1,0:T(8,128)(2,1)S(1)} %get-tuple-element.9), channel_id=1, source_target_pairs={{0,1},{1,2},{2,3},{4,5},{5,6},{6,7},{8,9},{9,10},{10,11},{12,13},{... | collective-permute-start | bytes 626696 | tf_op jit(solution)/shard_map/ppermute | solution.py:465
  11.2 7.1 %collective-permute-start.1 = (bf16[48,2176]{1,0:T(8,128)(2,1)S(1)}, bf16[48,2176]{1,0:T(8,128)(2,1)S(1)}, u32[]{:S(2)}, u32[]{:S(2)}) collective-permute-start(bf16[48,2176]{1,0:T(8,128)(2,1)S(1)} %get-tuple-element.10), channel_id=1, source_target_pairs={{1,0},{2,1},{3,2},{5,4},{6,5},{7,6},{9,8},{10,9},{11,10},{13,12},{... | collective-permute-start | bytes 626696 | tf_op jit(solution)/shard_map/ppermute | solution.py:466
  18.3 2.2 %copy-start.1 = (bf16[2,2048,512]{2,1,0:T(8,128)(2,1)S(1)}, bf16[2,2048,512]{2,1,0:T(8,128)(2,1)}, u32[]{:S(2)}) copy-start(bf16[2,2048,512]{2,1,0:T(8,128)(2,1)} %images_ref.5) | copy-start | bytes 12582916
  20.5 2.9 %copy-start.4 = (bf16[512,512]{1,0:T(8,128)(2,1)S(1)}, bf16[512,512]{1,0:T(8,128)(2,1)}, u32[]{:S(2)}) copy-start(bf16[512,512]{1,0:T(8,128)(2,1)} %scene_ref.3) | copy-start | bytes 1572868
  20.5 10.1 %copy-start.2 = (bf16[2,2048,512]{2,1,0:T(8,128)(2,1)S(1)}, bf16[2,2048,512]{2,1,0:T(8,128)(2,1)}, u32[]{:S(2)}) copy-start(bf16[2,2048,512]{2,1,0:T(8,128)(2,1)} %images_ref.5) | copy-start | bytes 12582916
  23.2 13.2 %collective-permute-start.4 = (bf16[512,512]{1,0:T(8,128)(2,1)S(1)}, bf16[512,512]{1,0:T(8,128)(2,1)S(1)}, u32[]{:S(2)}, u32[]{:S(2)}) collective-permute-start(bf16[512,512]{1,0:T(8,128)(2,1)S(1)} %image_blocks.3), channel_id=1, source_target_pairs={{0,4},{4,0},{8,12},{12,8},{1,5},{5,1},{9,13},{13,9},{2,6},{6,2},{1... | collective-permute-start | bytes 1572872 | tf_op jit(solution)/shard_map/ppermute | solution.py:480
  24.3 17.0 %collective-permute-start.3 = (bf16[32,640]{1,0:T(8,128)(2,1)S(1)}, bf16[32,640]{1,0:T(8,128)(2,1)S(1)}, u32[]{:S(2)}, u32[]{:S(2)}) collective-permute-start(bf16[32,640]{1,0:T(8,128)(2,1)S(1)} %get-tuple-element.16), channel_id=1, source_target_pairs={{4,0},{8,4},{12,8},{5,1},{9,5},{13,9},{6,2},{10,6},{14,10},{7,3},{... | collective-permute-start | bytes 122888 | tf_op jit(solution)/shard_map/ppermute | solution.py:469
  27.5 13.7 %collective-permute-start.2 = (bf16[32,640]{1,0:T(8,128)(2,1)S(1)}, bf16[32,640]{1,0:T(8,128)(2,1)S(1)}, u32[]{:S(2)}, u32[]{:S(2)}) collective-permute-start(bf16[32,640]{1,0:T(8,128)(2,1)S(1)} %get-tuple-element.17), channel_id=1, source_target_pairs={{0,4},{4,8},{8,12},{1,5},{5,9},{9,13},{2,6},{6,10},{10,14},{3,7},{... | collective-permute-start | bytes 122888 | tf_op jit(solution)/shard_map/ppermute | solution.py:468
  36.5 23.1 %collective-permute-start.5 = (bf16[512,512]{1,0:T(8,128)(2,1)S(1)}, bf16[512,512]{1,0:T(8,128)(2,1)S(1)}, u32[]{:S(2)}, u32[]{:S(2)}) collective-permute-start(bf16[512,512]{1,0:T(8,128)(2,1)S(1)} %get-tuple-element.13), channel_id=1, source_target_pairs={{0,8},{12,4},{4,12},{8,0},{1,9},{13,5},{5,13},{9,1},{2,10},{14,6},... | collective-permute-start | bytes 1572872 | tf_op jit(solution)/shard_map/ppermute | solution.py:486
  37.1 23.4 %collective-permute-start.7 = (bf16[512,512]{1,0:T(8,128)(2,1)S(1)}, bf16[512,512]{1,0:T(8,128)(2,1)S(1)}, u32[]{:S(2)}, u32[]{:S(2)}) collective-permute-start(bf16[512,512]{1,0:T(8,128)(2,1)S(1)} %get-tuple-element.14), channel_id=1, source_target_pairs={{0,4},{12,8},{1,5},{13,9},{2,6},{14,10},{3,7},{15,11},{16,20},{28,... | collective-permute-start | bytes 1572872 | tf_op jit(solution)/shard_map/ppermute | solution.py:484
  38.4 31.9 %collective-permute-start.6 = (bf16[512,512]{1,0:T(8,128)(2,1)S(1)}, bf16[512,512]{1,0:T(8,128)(2,1)S(1)}, u32[]{:S(2)}, u32[]{:S(2)}) collective-permute-start(bf16[512,512]{1,0:T(8,128)(2,1)S(1)} %get-tuple-element.15), channel_id=1, source_target_pairs={{4,8},{8,4},{5,9},{9,5},{6,10},{10,6},{7,11},{11,7},{20,24},{24,20... | collective-permute-start | bytes 1572872 | tf_op jit(solution)/shard_map/ppermute | solution.py:483

commit v2 on v1

v2 whole, which is shorter than its diff:
```python
import functools

import jax
import jax.numpy as jnp
from jax import lax
from jax.experimental import pallas as pl
from jax.experimental.pallas import tpu as pltpu
from jax.sharding import PartitionSpec as P

TILE = 512
HALO = 16
RIM = 2 * HALO
LANES = 128
SPAN = 256
STEP = SPAN - RIM
F32 = jnp.float32
BF16 = jnp.bfloat16
VMEM = pl.BlockSpec(memory_space=pltpu.VMEM)
SMEM = pl.BlockSpec(memory_space=pltpu.SMEM)
HBM = pl.BlockSpec(memory_space=pltpu.HBM)
PARAMS = pltpu.CompilerParams(vmem_limit_bytes=40 * 1024 * 1024)
SHORT = pl.CostEstimate(flops=1000, bytes_accessed=1000, transcendentals=0)
WHOLE = pltpu.CompilerParams(vmem_limit_bytes=59 * 1024 * 1024)


def up_to(value, unit):
    return -(-value // unit) * unit


def dot(a, b, dims=((1,), (0,))):
    return lax.dot_general(a, b, (dims, ((), ())), preferred_element_type=F32)


def iota(shape, dim):
    return lax.broadcasted_iota(jnp.int32, shape, dim)


def selection(rows, cols, shift):
    return (iota((rows, cols), 1) == iota((rows, cols), 0) + shift).astype(BF16)


def toeplitz(taps, start, rows, width):
    line = jnp.concatenate([taps, jnp.zeros((1, width - LANES), F32)], axis=1)
    line = jnp.broadcast_to(line, (8, width))
    line = pltpu.roll(line, lax.rem(2 * width - start, width), 1)[0:1]
    line = jnp.broadcast_to(line, (rows, width))
    return pltpu.roll(line, 0, 1, stride=1, stride_axis=0).astype(BF16)


def stacked(taps, start):
    pair = toeplitz(taps, start, LANES, SPAN)
    return jnp.concatenate([pair[:, :LANES], pair[:, LANES:]], axis=0)


def row_of(values, index):
    return jnp.sum(jnp.where(iota(values.shape, 0) == index, values, 0), axis=0, keepdims=True)


def load_taps(psf_ref, lines, epochs, taps):
    lines[0] = jnp.zeros(lines.shape[1:], F32)
    lines[0, :epochs, :taps] = psf_ref[...].astype(F32)
    mirror = iota((LANES, LANES), 0) + iota((LANES, LANES), 1) == taps - 1
    lines[1] = dot(lines[0].astype(BF16), mirror.astype(F32).astype(BF16))


def spans(length):
    return [(s, min(STEP, length - s)) for s in range(0, length, STEP)]


class Sizes:
    def __init__(self, images, sky_scene, psf_rows):
        self.local, self.height, self.width = images.shape
        self.rows = sky_scene.shape[0]
        self.epochs = psf_rows.shape[0]
        self.taps = psf_rows.shape[1]
        self.tile_rows = self.height // TILE
        self.wide = self.width + LANES
        self.line = up_to(self.height + RIM, LANES)
        self.chunk = up_to(self.rows, LANES)
        self.mask_rows = up_to(self.epochs, HALO)
        self.buffer_rows = HALO * (self.local + 1)
        self.blocks = self.height // self.rows
        self.tap_rows = self.mask_rows


def cover_at(coverage_ref, epoch, row_tile, col_tile):
    last_row = coverage_ref.shape[0] - 1
    last_col = coverage_ref.shape[1] - 1
    inside = (row_tile >= 0) & (row_tile <= last_row) & (col_tile >= 0) & (col_tile <= last_col)
    value = coverage_ref[jnp.clip(row_tile, 0, last_row), jnp.clip(col_tile, 0, last_col), epoch]
    return jnp.where(inside, value, 0).astype(F32)


def tile_of(position):
    return (position + TILE) // TILE - 1


def edges_kernel(sz, images_ref, scene_ref, mask_ref, first_ref, second_ref, *scratch):
    edge, sides, flags, sem, side_sem, flag_sem = scratch
    epoch = lax.axis_index("epoch") * sz.local
    even = lax.axis_index("sky") % 2 == 0
    places = (0, sz.width - LANES)
    flag_copy = pltpu.make_async_copy(mask_ref, flags, flag_sem)
    flag_copy.start()
    copies = []
    for e in range(sz.local):
        for side in range(2):
            slot = 2 * e + side
            copies.append(
                pltpu.make_async_copy(
                    images_ref.at[e, :, pl.ds(places[side], LANES)],
                    edge.at[slot, pl.ds(HALO, sz.height), :],
                    sem.at[slot],
                )
            )
            copies[-1].start()
    side_copies = [
        pltpu.make_async_copy(
            scene_ref.at[:, pl.ds(places[side], LANES)], sides.at[side], side_sem.at[side]
        )
        for side in range(2)
    ]
    for copy in side_copies:
        copy.start()
    tail = sz.line - sz.height - HALO
    for slot in range(2 * sz.local):
        edge[slot, 0:HALO] = jnp.zeros((HALO, LANES), BF16)
        edge[slot, sz.line - tail :] = jnp.zeros((tail, LANES), BF16)
    tail_at = HALO * sz.local

    def put(left, right, rows, cols):
        first_ref[rows, cols] = jnp.where(even, right, left).astype(BF16)
        second_ref[rows, cols] = jnp.where(even, left, right).astype(BF16)

    flag_copy.wait()
    goods = []
    for side in range(2):
        good = flags[:, places[side] : places[side] + LANES].astype(F32)
        if side == 1:
            good = pltpu.roll(good, HALO, 1)
        if sz.mask_rows > sz.epochs:
            good = jnp.concatenate(
                [good, jnp.zeros((sz.mask_rows - sz.epochs, LANES), F32)], axis=0
            )
        goods.append(good)
    below = slice(tail_at, tail_at + HALO)
    for q in range(sz.mask_rows // HALO):
        at = 2 * sz.chunk + q * LANES
        rows = slice(q * HALO, (q + 1) * HALO)
        put(goods[0][rows], goods[1][rows], below, slice(at, at + LANES))
    rest = 2 * sz.chunk + (sz.mask_rows // HALO) * LANES
    none = jnp.zeros((HALO, sz.line - rest), F32)
    put(none, none, below, slice(rest, sz.line))
    cells = []
    for side in range(2):
        side_copies[side].wait()
        shift = 0 if side == 0 else LANES - RIM
        cells.append(dot(selection(RIM, LANES, shift), sides[side], ((1,), (1,))))
    for q in range(2):
        rows = slice(q * HALO, (q + 1) * HALO)
        put(cells[0][rows], cells[1][rows], below, slice(q * sz.chunk, q * sz.chunk + sz.rows))
        if sz.chunk > sz.rows:
            none = jnp.zeros((HALO, sz.chunk - sz.rows), F32)
            put(none, none, below, slice(q * sz.chunk + sz.rows, (q + 1) * sz.chunk))
    for e in range(sz.local):
        lines = []
        for side in range(2):
            slot = 2 * e + side
            copies[slot].wait()
            good = row_of(flags[:, places[side] : places[side] + LANES].astype(F32), epoch + e)
            shift = 0 if side == 0 else LANES - HALO
            pick = (iota((HALO, LANES), 1) == iota((HALO, LANES), 0) + shift) & (good > 0)
            lines.append(dot(pick.astype(F32).astype(BF16), edge[slot], ((1,), (1,))))
        put(lines[0], lines[1], slice(HALO * e, HALO * (e + 1)), slice(0, sz.line))


def edges(sz, images, scene, mask):
    shape = jax.ShapeDtypeStruct((sz.buffer_rows, sz.line), BF16)
    return pl.pallas_call(
        functools.partial(edges_kernel, sz),
        out_shape=(shape, shape),
        in_specs=[HBM, HBM, HBM],
        out_specs=(VMEM, VMEM),
        scratch_shapes=[
            pltpu.VMEM((2 * sz.local, sz.line, LANES), BF16),
            pltpu.VMEM((2, sz.rows, LANES), BF16),
            pltpu.VMEM((sz.epochs, sz.width), jnp.int32),
            pltpu.SemaphoreType.DMA((2 * sz.local,)),
            pltpu.SemaphoreType.DMA((2,)),
            pltpu.SemaphoreType.DMA,
        ],
        compiler_params=WHOLE,
        cost_estimate=SHORT,
        name="edges",
    )(images, scene, mask)


def sides_of(first, second):
    even = lax.axis_index("sky") % 2 == 0
    return jnp.where(even, second, first), jnp.where(even, first, second)


def widen_kernel(sz, scene_ref, mask_ref, first_ref, second_ref, *outs):
    wide_ref, good_ref = outs
    below = slice(HALO * sz.local, HALO * (sz.local + 1))

    def cells(value):
        return jnp.concatenate(
            [value[:, q * sz.chunk : q * sz.chunk + sz.rows] for q in range(2)], axis=0
        )

    def flags(value):
        parts = []
        for q in range(sz.mask_rows // HALO):
            at = 2 * sz.chunk + q * LANES
            parts.append(value[:, at : at + LANES])
        return jnp.concatenate(parts, axis=0) if len(parts) > 1 else parts[0]

    before, after = sides_of(first_ref[below], second_ref[below])
    wide = dot(scene_ref[...], selection(sz.width, sz.wide, RIM))
    wide += dot(cells(before), selection(RIM, sz.wide, 0), ((0,), (0,)))
    wide += dot(cells(after), selection(RIM, sz.wide, sz.width + RIM), ((0,), (0,)))
    wide_ref[...] = wide.astype(BF16)
    own = mask_ref[...].astype(F32)
    if sz.mask_rows > sz.epochs:
        own = jnp.concatenate(
            [own, jnp.zeros((sz.mask_rows - sz.epochs, sz.width), F32)], axis=0
        )
    good = dot(own.astype(BF16), selection(sz.width, sz.wide, HALO))
    inner = iota((LANES, sz.wide), 0) < HALO
    zero = jnp.zeros((LANES, sz.wide), BF16)
    good += dot(flags(before), jnp.where(inner, selection(LANES, sz.wide, 0), zero))
    good += dot(flags(after), jnp.where(inner, selection(LANES, sz.wide, sz.width + HALO), zero))
    good_ref[...] = good


def destination(slot, place):
    return (
        3 * (1 - place % 2),
        2 - place // 2,
        (2 * place + 1) % 5,
        place,
    )[slot]


def rim_tables(sz, row_line, col_line, row_shift, col_shift):
    row_table = toeplitz(row_line, row_shift - 4, min(sz.rows, LANES), SPAN)
    enter = toeplitz(col_line, 28 - col_shift, HALO, SPAN)[:, :LANES]
    leave = toeplitz(col_line, SPAN + LANES - 116 - col_shift, HALO, SPAN + LANES)[:, :LANES]
    none = jnp.zeros((HALO, LANES), BF16)
    col_table = jnp.concatenate(
        [jnp.concatenate([enter, none], axis=1), jnp.concatenate([none, leave], axis=1)], axis=0
    )
    return row_table, col_table


def rim_line(sz, start, epoch, e, column, coverage_ref, twice, first_ref, second_ref, row_table):
    size = min(sz.rows, LANES)
    covers = []
    for tile in (tile_of(start - HALO), tile_of(start), tile_of(start + sz.rows)):
        covers.append(
            [
                cover_at(coverage_ref, epoch, tile, tile_of(c))
                for c in (column - HALO, column + sz.width)
            ]
        )
    side = iota((RIM, SPAN), 0) < HALO
    factors = [jnp.where(side, left, right) for left, right in covers]
    pieces = []
    for s in range(0, sz.rows, size):
        at = start + s
        base = pl.multiple_of((at // LANES) * LANES, LANES)
        rows = slice(HALO * e, HALO * (e + 1))
        both = jnp.concatenate(
            sides_of(first_ref[rows, pl.ds(base, SPAN)], second_ref[rows, pl.ds(base, SPAN)]),
            axis=0,
        ).astype(F32)
        if size < LANES:
            both = pltpu.roll(both, lax.rem(SPAN - (at - base), SPAN), 1)
        lane = iota((RIM, SPAN), 1) + (s - HALO)
        both = both * jnp.where(
            lane < 0, factors[0], jnp.where(lane < sz.rows, factors[1], factors[2])
        )
        pieces.append(dot(both.astype(BF16), row_table, ((1,), (1,))))
    rim = jnp.concatenate(pieces, axis=1) if len(pieces) > 1 else pieces[0]
    return (rim * twice).astype(BF16)


def finish_kernel(
    sz, slots, coverage_ref, offsets_ref, weight_ref, scene_ref, mask_ref, first_ref, second_ref,
    psf_rows_ref, psf_cols_ref, *more,
):
    count = len(slots)
    blocks, outs = more[:count], more[count : 2 * count]
    wide_ref, good_ref, row_lines, col_lines = more[2 * count :]
    place = lax.axis_index("epoch")
    column = lax.axis_index("sky") * sz.width
    load_taps(psf_rows_ref, row_lines, sz.epochs, sz.taps)
    load_taps(psf_cols_ref, col_lines, sz.epochs, sz.taps)
    totals = [None] * count
    for e in range(sz.local):
        epoch = place * sz.local + e
        row_table, col_table = rim_tables(
            sz, row_of(row_lines[1], epoch), row_of(col_lines[0], epoch),
            offsets_ref[0, epoch], offsets_ref[1, epoch],
        )
        for i, slot in enumerate(slots):
            line = rim_line(
                sz, destination(slot, place) * sz.rows, epoch, e, column, coverage_ref,
                -2.0 * weight_ref[epoch], first_ref, second_ref, row_table,
            )
            part = dot(line, col_table, ((0,), (0,)))
            totals[i] = part if e == 0 else totals[i] + part
    low, mid = slice(0, LANES), slice(LANES, sz.width - LANES)
    high = slice(sz.width - LANES, sz.width)
    own = slice(0, sz.rows)
    for block, out, total in zip(blocks, outs, totals):
        out[own, low] = (block[:, low].astype(F32) + total[:, :LANES]).astype(BF16)
        out[own, mid] = block[:, mid]
        out[own, high] = (block[:, high].astype(F32) + total[:, LANES:]).astype(BF16)
    widen_kernel(sz, scene_ref, mask_ref, first_ref, second_ref, wide_ref, good_ref)
    if count == 0:
        return
    top, bottom = wide_ref[:RIM], wide_ref[sz.rows - RIM :]
    for out, last in zip(outs, (place % 2 == 0, place < 2)):
        rim = jnp.where(last, bottom, top)
        out[sz.rows : sz.rows + RIM] = rim[:, : sz.width]
        left = slice(sz.rows + RIM, sz.rows + RIM + HALO)
        out[left, :LANES] = rim[:HALO, sz.width :]
        out[left, LANES:SPAN] = rim[HALO:, sz.width :]
        out[left, SPAN:] = jnp.zeros((HALO, sz.width - SPAN), BF16)


def unpack_rim(sz, ref):
    left = slice(sz.rows + RIM, sz.rows + RIM + HALO)
    rest = jnp.concatenate([ref[left, :LANES], ref[left, LANES:SPAN]], axis=0)
    return jnp.concatenate([ref[sz.rows : sz.rows + RIM], rest], axis=1)


def finish(
    sz, slots, coverage, offsets, weight, scene, mask, first, second, psf_rows, psf_cols, *blocks
):
    pack = jax.ShapeDtypeStruct((sz.rows + RIM + HALO, sz.width), BF16)
    shapes = [pack] * len(slots) + [
        jax.ShapeDtypeStruct((sz.rows, sz.wide), BF16),
        jax.ShapeDtypeStruct((sz.mask_rows, sz.wide), F32),
    ]
    return pl.pallas_call(
        functools.partial(finish_kernel, sz, slots),
        out_shape=tuple(shapes),
        in_specs=[SMEM] * 3 + [VMEM] * (6 + len(slots)),
        out_specs=tuple([VMEM] * len(shapes)),
        scratch_shapes=[pltpu.VMEM((2, sz.tap_rows, LANES), F32)] * 2,
        compiler_params=PARAMS,
        cost_estimate=SHORT,
        name="finish",
    )(coverage, offsets, weight, scene, mask, first, second, psf_rows, psf_cols, *blocks)


def image_kernel(
    sz, slots, rims, coverage_ref, offsets_ref, weight_ref,
    images_ref, mask_ref, psf_rows_ref, psf_cols_ref, *more,
):
    count = 1 if slots is None else len(slots)
    ends, more = more[:rims], more[rims:]
    outs = more[:count]
    window, row_lines, col_lines, row_table, main_table, cross_table, sem = more[count:]
    place = lax.axis_index("epoch")
    first = place * sz.local
    column = lax.axis_index("sky") * sz.width
    if slots is None:
        targets = [pl.program_id(0)]
    else:
        targets = [destination(slot, place) for slot in slots]

    copies = []
    for i, target in enumerate(targets):
        start = target * sz.rows
        head = jnp.maximum(start - HALO, 0)
        foot = jnp.minimum(start + sz.rows, sz.height - HALO)
        for e in range(sz.local):
            for n, (source, at, length) in enumerate(
                ((start, HALO, sz.rows), (head, 0, HALO), (foot, HALO + sz.rows, HALO))
            ):
                copies.append(
                    pltpu.make_async_copy(
                        images_ref.at[e, pl.ds(pl.multiple_of(source, HALO), length), :],
                        window.at[i, e, pl.ds(at, length), :],
                        sem.at[i, e, n],
                    )
                )
    for copy in copies:
        copy.start()
    load_taps(psf_rows_ref, row_lines, sz.epochs, sz.taps)
    load_taps(psf_cols_ref, col_lines, sz.epochs, sz.taps)
    for e in range(sz.local):
        epoch = first + e
        row_shift, col_shift = offsets_ref[0, epoch], offsets_ref[1, epoch]
        row_table[e] = toeplitz(row_of(row_lines[1], epoch), row_shift - 4, STEP, SPAN)
        line = row_of(col_lines[0], epoch)
        main = toeplitz(line, 12 - col_shift, SPAN, SPAN + LANES)[:, :SPAN]
        main_table[e] = main
        apart = (iota((SPAN, SPAN), 0) < LANES) != (iota((SPAN, SPAN), 1) < LANES)
        cross_table[e] = jnp.where(apart, main, jnp.zeros_like(main))
    rim_parts = []
    for e in range(sz.local if rims else 0):
        epoch = first + e
        tables = rim_tables(
            sz, row_of(row_lines[1], epoch), row_of(col_lines[0], epoch),
            offsets_ref[0, epoch], offsets_ref[1, epoch],
        )
        for i, target in enumerate(targets):
            line = rim_line(
                sz, target * sz.rows, epoch, e, column, coverage_ref,
                -2.0 * weight_ref[epoch], *ends, tables[0],
            )
            part = dot(line, tables[1], ((0,), (0,)))
            if e == 0:
                rim_parts.append(part)
            else:
                rim_parts[i] += part
    for i, target in enumerate(targets):
        for copy in copies[3 * sz.local * i : 3 * sz.local * (i + 1)]:
            copy.wait()
        start = target * sz.rows
        zones = (
            (0, HALO, tile_of(start - HALO)),
            (HALO, HALO + sz.rows, tile_of(start)),
            (HALO + sz.rows, RIM + sz.rows, tile_of(start + sz.rows)),
        )
        total = [None] * (sz.width // LANES)

        def add(at, value):
            for n in range(value.shape[1] // LANES):
                piece = value[:, n * LANES : (n + 1) * LANES]
                k = at + n
                total[k] = piece if total[k] is None else total[k] + piece

        for e in range(sz.local):
            epoch = first + e
            twice = -2.0 * weight_ref[epoch]
            good = row_of(mask_ref[...].astype(F32), epoch)
            for begin, end, tile in zones:
                factor = good * cover_at(coverage_ref, epoch, tile, column // TILE)
                window[i, e, begin:end] = window[i, e, begin:end] * factor.astype(BF16)
            parts = []
            for s, n in spans(sz.rows):
                part = dot(row_table[e, :n, : n + RIM], window[i, e, s : s + n + RIM])
                parts.append((part * twice).astype(BF16))
            rows_done = jnp.concatenate(parts, axis=0) if len(parts) > 1 else parts[0]
            for b in range(0, sz.width, SPAN):
                add(b // LANES, dot(rows_done[:, b : b + SPAN], main_table[e]))
            for b in range(LANES, sz.width - LANES, SPAN):
                add(b // LANES, dot(rows_done[:, b : b + SPAN], cross_table[e]))
        if rims:
            add(0, rim_parts[i][:, :LANES])
            add(sz.width // LANES - 1, rim_parts[i][:, LANES:])
        for k, piece in enumerate(total):
            outs[i][:, k * LANES : (k + 1) * LANES] = piece.astype(BF16)


def image_blocks(sz, slots, coverage, offsets, weight, images, mask, psf_rows, psf_cols, *ends):
    if slots is None:
        count = 1
        grid = dict(
            grid=(sz.blocks,),
            out_shape=jax.ShapeDtypeStruct((sz.blocks * sz.rows, sz.width), BF16),
            out_specs=pl.BlockSpec((sz.rows, sz.width), lambda i: (i, 0)),
        )
    else:
        count = len(slots)
        grid = dict(
            out_shape=tuple([jax.ShapeDtypeStruct((sz.rows, sz.width), BF16)] * count),
            out_specs=tuple([VMEM] * count),
        )
    return pl.pallas_call(
        functools.partial(image_kernel, sz, slots, len(ends)),
        in_specs=[SMEM, SMEM, SMEM, HBM] + [VMEM] * (3 + len(ends)),
        scratch_shapes=[
            pltpu.VMEM((count, sz.local, sz.rows + RIM, sz.width), BF16),
            pltpu.VMEM((2, sz.tap_rows, LANES), F32),
            pltpu.VMEM((2, sz.tap_rows, LANES), F32),
            pltpu.VMEM((sz.local, STEP, SPAN), BF16),
            pltpu.VMEM((sz.local, SPAN, SPAN), BF16),
            pltpu.VMEM((sz.local, SPAN, SPAN), BF16),
            pltpu.SemaphoreType.DMA((count, sz.local, 3)),
        ],
        compiler_params=PARAMS,
        cost_estimate=SHORT,
        name="image_blocks",
        **grid,
    )(coverage, offsets, weight, images, mask, psf_rows, psf_cols, *ends)


def model_kernel(
    sz, coverage_ref, offsets_ref, weight_ref,
    wide_ref, good_ref, psf_rows_ref, psf_cols_ref, *more,
):
    *extra, out_ref, scene, lifted, residual, pulled, row_lines, col_lines = more
    epoch = pl.program_id(0)
    place = lax.axis_index("epoch")
    start = place * sz.rows
    column = lax.axis_index("sky") * sz.width

    @pl.when(epoch == 0)
    def _():
        load_taps(psf_rows_ref, row_lines, sz.epochs, sz.taps)
        load_taps(psf_cols_ref, col_lines, sz.epochs, sz.taps)
        scene[RIM : RIM + sz.rows] = wide_ref[...]
        if sz.blocks != 4:
            head_ref, foot_ref, base_ref = extra
            scene[0:RIM] = head_ref[...]
            scene[RIM + sz.rows :] = foot_ref[...]
            out_ref[...] = base_ref[...]
        else:
            own_ref, one_ref, two_ref = extra
            near, far = unpack_rim(sz, one_ref), unpack_rim(sz, two_ref)
            none = jnp.zeros_like(near)
            outer = (place == 0) | (place == 3)
            odd = place % 2 == 1
            scene[0:RIM] = jnp.where(odd, near, jnp.where(outer, none, far))
            scene[RIM + sz.rows :] = jnp.where(odd, jnp.where(outer, none, far), near)
            for b in range(0, sz.width, LANES):
                cols = slice(b, b + LANES)
                one = one_ref[: sz.rows, cols].astype(F32)
                two = two_ref[: sz.rows, cols].astype(F32)
                out_ref[:, cols] = own_ref[:, cols].astype(F32) + jnp.where(outer, one, two)

    row_shift, col_shift = offsets_ref[0, epoch], offsets_ref[1, epoch]
    row_in = toeplitz(row_of(row_lines[0], epoch), -4 - row_shift, STEP, SPAN)
    row_out = toeplitz(row_of(row_lines[1], epoch), row_shift - 4, STEP, SPAN)
    col_in = stacked(row_of(col_lines[1], epoch), 28 + col_shift)
    col_out = stacked(row_of(col_lines[0], epoch), 28 - col_shift)

    for s, n in spans(sz.rows + RIM):
        lifted[s : s + n] = dot(row_in[:n, : n + RIM], scene[s : s + n + RIM]).astype(BF16)

    twice = 2.0 * weight_ref[epoch]
    good = row_of(good_ref[...], epoch) * twice
    lane = iota((1, sz.wide), 1)
    factors = []
    for row_tile in (tile_of(start - HALO), tile_of(start), tile_of(start + sz.rows)):
        left, here, right = (
            cover_at(coverage_ref, epoch, row_tile, tile_of(c))
            for c in (column - HALO, column, column + sz.width)
        )
        factors.append(
            good * jnp.where(lane < HALO, left, jnp.where(lane < HALO + sz.width, here, right))
        )
    for b in range(0, sz.wide, LANES):
        if b < sz.width:
            modeled = dot(lifted[:, b : b + SPAN], col_in)
        else:
            modeled = dot(lifted[:, b : b + LANES], col_in[:LANES])
        low, mid, high = (f[:, b : b + LANES] for f in factors)
        edge = sz.rows + HALO
        residual[0:HALO, b : b + LANES] = (modeled[0:HALO] * low).astype(BF16)
        residual[HALO:edge, b : b + LANES] = (modeled[HALO:edge] * mid).astype(BF16)
        residual[edge:, b : b + LANES] = (modeled[edge:] * high).astype(BF16)
    for b in range(0, sz.width, LANES):
        pulled[:, b : b + LANES] = dot(residual[:, b : b + SPAN], col_out).astype(BF16)
    for s, n in spans(sz.rows):
        out_ref[s : s + n] += dot(row_out[:n, : n + RIM], pulled[s : s + n + RIM])


def model_term(sz, coverage, offsets, weight, wide, good, psf_rows, psf_cols, *extra):
    high = sz.rows + RIM
    return pl.pallas_call(
        functools.partial(model_kernel, sz),
        grid=(sz.epochs,),
        out_shape=jax.ShapeDtypeStruct((sz.rows, sz.width), F32),
        in_specs=[SMEM] * 3 + [VMEM] * (4 + len(extra)),
        out_specs=VMEM,
        scratch_shapes=[
            pltpu.VMEM((sz.rows + 2 * RIM, sz.wide), BF16),
            pltpu.VMEM((high, sz.wide), BF16),
            pltpu.VMEM((high, sz.wide), BF16),
            pltpu.VMEM((high, sz.width), BF16),
            pltpu.VMEM((2, sz.tap_rows, LANES), F32),
            pltpu.VMEM((2, sz.tap_rows, LANES), F32),
        ],
        compiler_params=PARAMS,
        cost_estimate=pl.CostEstimate(
            flops=sz.epochs * 1300000000, bytes_accessed=2000000, transcendentals=0
        ),
        name="model_term",
    )(coverage, offsets, weight, wide, good, psf_rows, psf_cols, *extra)


def on_device(sky_scene, images, psf_rows, psf_cols, offsets, epoch_weight, column_mask, coverage):
    sz = Sizes(images, sky_scene, psf_rows)
    peers = lax.axis_size("sky")
    depth = lax.axis_size("epoch")
    scalars = (jnp.transpose(coverage, (1, 2, 0)), offsets.T, epoch_weight)
    profiles = (psf_rows, psf_cols)

    def pairs(start, count):
        return [p for i in range(start, count - 1, 2) for p in ((i, i + 1), (i + 1, i))]

    def blocks(slots, shifts, *ends):
        return image_blocks(
            sz, slots, scalars[0], shifts, epoch_weight, images, column_mask, *profiles, *ends
        )

    first, second = edges(sz, images, sky_scene, column_mask)
    shifts, first = lax.optimization_barrier((scalars[1], first))
    first = lax.ppermute(first, "sky", pairs(0, peers))
    second = lax.ppermute(second, "sky", pairs(1, peers))
    if depth == 4:
        place = lax.axis_index("epoch")
        outer = (place == 0) | (place == 3)
        one, two = blocks((0, 1), shifts)
        one, two, wide, good = finish(
            sz, (0, 1), *scalars, sky_scene, column_mask, first, second, *profiles, one, two
        )
        got_one = lax.ppermute(one, "epoch", pairs(0, depth))
        got_two = lax.ppermute(two, "epoch", pairs(1, depth))
        shifts, two = lax.optimization_barrier((scalars[1], two))
        three, own = blocks((2, 3), shifts, first, second)
        got_three = lax.ppermute(three, "epoch", [(0, 1), (3, 2)])
        passed = jnp.where(outer, two[: sz.rows], three + got_one[: sz.rows])
        passed, good = lax.optimization_barrier((passed, good))
        got_four = lax.ppermute(passed, "epoch", [(0, 2), (3, 1), (1, 3), (2, 0)])
        model = model_term(sz, *scalars, wide, good, *profiles, own, got_one, got_two)
        return model + got_four.astype(F32) + got_three.astype(F32)

    downward = [(i, i + 1) for i in range(depth - 1)]
    upward = [(i + 1, i) for i in range(depth - 1)]
    wide, good = finish(
        sz, (), *scalars, sky_scene, column_mask, first, second, *profiles
    )
    head = lax.ppermute(wide[-RIM:], "epoch", downward)
    foot = lax.ppermute(wide[:RIM], "epoch", upward)
    terms = blocks(None, scalars[1], first, second).astype(F32)
    base = lax.psum_scatter(terms, "epoch", scatter_dimension=0, tiled=True)
    return model_term(sz, *scalars, wide, good, *profiles, head, foot, base)


def solution(mesh):
    return jax.shard_map(
        on_device,
        mesh=mesh,
        in_specs=(
            P(("field", "epoch"), "sky"),
            P(("field", "epoch"), None, "sky"),
            P("field", None),
            P("field", None),
            P("field", None),
            P("field"),
            P("field", "sky"),
            P("field", None, None),
        ),
        out_specs=P(("field", "epoch"), "sky"),
        check_vma=False,
    )
```

time: 72.1 us -> 57.7 us (0.80)
  the two profiles are of different devices: /device:TPU:9 before, /device:TPU:0 now
where the time goes in v2:
time: 57.7 us; the launch traced here: 57 us
  Pallas kernels  28 us (49%)
  starting transfers between devices  12.3 us (21%)
  waiting for transfers between devices  11.8 us (20%)
  local copies, waits for them, and re-layouts  3.52 us (6%)
  other arithmetic  1.28 us (2%)
    pallas_call x1, Pallas kernels, model_term(): pl.pallas_call(functools.partial(model_kernel, sz), grid=(sz.epochs,), ou...  12.7 us
    ppermute x1, waiting for transfers between devices, on_device(): got_four = lax.ppermute(passed, 'epoch', [(0, 2), (3, 1), (1, 3), (2, 0)])  11.7 us
    pallas_call x2, Pallas kernels, image_blocks(): pl.pallas_call(functools.partial(image_kernel, sz, slots, len(ends)), in_...  7.98 us
    ppermute x1, starting transfers between devices, on_device(): got_three = lax.ppermute(three, 'epoch', [(0, 1), (3, 2)])  6.3 us
    pallas_call x1, Pallas kernels, edges(): pl.pallas_call(functools.partial(edges_kernel, sz), out_shape=(shape, sha...  4.02 us
    unnamed x24, local copies, waits for them, and re-layouts  3.52 us
    pallas_call x1, Pallas kernels, finish(): pl.pallas_call(functools.partial(finish_kernel, sz, slots), out_shape=tup...  3.31 us
    ppermute x1, starting transfers between devices, on_device(): got_one = lax.ppermute(one, 'epoch', pairs(0, depth))  2.6 us
  transfers between devices with their start and end apart: 6, of which 1 were waited for; matrix products, arithmetic and copies ran while one was open for 0% of the time, Pallas kernels for 36%

profile of v2, /device:TPU:0, one launch (start us, length us, event | category | flops | bytes accessed | tf_op | source)
XLA Modules:
  0.0 57.0 jit_solution(17604518979192876313)
XLA Ops:
  0.0 0.0 copy-start.7
  0.0 0.0 copy-start.6
  0.0 4.0 %edges.1 = (bf16[48,2176]{1,0:T(8,128)(2,1)}, bf16[48,2176]{1,0:T(8,128)(2,1)}) custom-call(bf16[2,2048,512]{2,1,0:T(8,128)(2,1)} %images_ref.5, bf16[512,512]{1,0:T(8,128)(2,1)} %scene_ref.3, s32[8,512]{1,0:T(8,128)} %mask_ref.7), custom_call_target="tpu_custom_call" | custom-call | flops 1000 | bytes 1000 | tf_op jit(solution)/shard_map/edges/pallas_call | solution.py:179
  4.1 0.5 collective-permute-start
  4.6 0.7 %collective-permute-start.1 = (bf16[48,2176]{1,0:T(8,128)(2,1)}, bf16[48,2176]{1,0:T(8,128)(2,1)S(1)}, u32[]{:S(2)}, u32[]{:S(2)}) collective-permute-start(bf16[48,2176]{1,0:T(8,128)(2,1)} %get-tuple-element.23), channel_id=1, source_target_pairs={{1,2},{2,1},{5,6},{6,5},{9,10},{10,9},{13,14},{14,13},{17,18},{18,... | collective-permute-start | bytes 626696 | tf_op jit(solution)/shard_map/ppermute | solution.py:608
  5.3 0.0 copy-done.3
  5.3 0.0 copy-done
  5.3 0.0 copy-done.8
  5.3 0.0 copy-done.9
  5.3 0.0 copy-done.7
  5.3 0.0 copy-done.6
  5.3 0.0 copy-start.4
  5.3 0.7 %copy-done.4 = s32[8,4,4]{0,2,1:T(4,128)S(1)} copy-done((s32[8,4,4]{0,2,1:T(4,128)S(1)}, s32[8,4,4]{0,2,1:T(4,128)}, u32[]{:S(2)}) %copy-start.4) | copy-done | bytes 536
  6.0 3.5 %image_blocks.2 = (bf16[512,512]{1,0:T(8,128)(2,1)S(1)}, bf16[512,512]{1,0:T(8,128)(2,1)S(1)}) custom-call(s32[4,4,8]{2,1,0:T(4,128)S(1)} %bitcast.2, s32[2,8]{1,0:T(2,128)S(1)} %bitcast.6, f32[8]{0:T(128)S(1)} %copy-done.9, bf16[2,2048,512]{2,1,0:T(8,128)(2,1)S(1)} %copy-done, s32[8,512]{1,0:T(8,128)S(1)} %copy-done.3, bf16[8,25]{1,0:T(8,128)(2,1)S(1)} %copy-done.6, ...), custom_call_target="tpu_custom_call" | custom-call | flops 1000 | bytes 1000 | tf_op jit(solution)/shard_map/image_blocks/pallas_call | solution.py:476
  9.5 0.0 collective-permute-done.first_ref.more_0_
  9.5 0.0 collective-permute-done.1.second_ref.more_1_
  9.6 3.3 %finish.1 = (bf16[560,512]{1,0:T(8,128)(2,1)}, bf16[560,512]{1,0:T(8,128)(2,1)S(1)}, bf16[512,640]{1,0:T(8,128)(2,1)S(1)}, f32[16,640]{1,0:T(8,128)S(1)}) custom-call(s32[4,4,8]{2,1,0:T(4,128)S(1)} %bitcast.3, s32[2,8]{1,0:T(2,128)S(1)} %bitcast.7, f32[8]{0:T(128)S(1)} %copy-done.9, bf16[512,512]{1,0:T(8,128)(2,1)S(1)} %copy-done.2, s32[8,512]{1,0:T(8,128)S(1)} %copy-done.3, ...), custom_call_target="tpu_custom_call" | custom-call | flops 1000 | bytes 1000 | tf_op jit(solution)/shard_map/finish/pallas_call | solution.py:348
  12.9 0.6 %copy-done.10 = f32[16,640]{1,0:T(8,128)} copy-done((f32[16,640]{1,0:T(8,128)}, f32[16,640]{1,0:T(8,128)S(1)}, u32[]{:S(2)}) %copy-start.10) | copy-done | bytes 40984
  13.5 2.6 %collective-permute-start.2 = (bf16[560,512]{1,0:T(8,128)(2,1)}, bf16[560,512]{1,0:T(8,128)(2,1)S(1)}, u32[]{:S(2)}, u32[]{:S(2)}) collective-permute-start(bf16[560,512]{1,0:T(8,128)(2,1)} %get-tuple-element.32), channel_id=1, source_target_pairs={{0,4},{4,0},{8,12},{12,8},{1,5},{5,1},{9,13},{13,9},{2,6},{6,2},{1... | collective-permute-start | bytes 1720328 | tf_op jit(solution)/shard_map/ppermute | solution.py:616
  16.1 0.7 %collective-permute-start.3 = (bf16[560,512]{1,0:T(8,128)(2,1)S(1)}, bf16[560,512]{1,0:T(8,128)(2,1)S(1)}, u32[]{:S(2)}, u32[]{:S(2)}) collective-permute-start(bf16[560,512]{1,0:T(8,128)(2,1)S(1)} %get-tuple-element.29), channel_id=1, source_target_pairs={{4,8},{8,4},{5,9},{9,5},{6,10},{10,6},{7,11},{11,7},{20,24},{24,20... | collective-permute-start | bytes 1720328 | tf_op jit(solution)/shard_map/ppermute | solution.py:617
  16.8 0.0 copy-start.1
  16.8 2.2 %copy-done.1 = bf16[2,2048,512]{2,1,0:T(8,128)(2,1)S(1)} copy-done((bf16[2,2048,512]{2,1,0:T(8,128)(2,1)S(1)}, bf16[2,2048,512]{2,1,0:T(8,128)(2,1)}, u32[]{:S(2)}) %copy-start.1) | copy-done | bytes 4194328
  19.0 4.5 %image_blocks.3 = (bf16[512,512]{1,0:T(8,128)(2,1)S(1)}, bf16[512,512]{1,0:T(8,128)(2,1)S(1)}) custom-call(s32[4,4,8]{2,1,0:T(4,128)S(1)} %bitcast.4, s32[2,8]{1,0:T(2,128)S(1)} %bitcast.8, f32[8]{0:T(128)S(1)} %copy-done.9, bf16[2,2048,512]{2,1,0:T(8,128)(2,1)S(1)} %copy-done.1, s32[8,512]{1,0:T(8,128)S(1)} %copy-done.3, bf16[8,25]{1,0:T(8,128)(2,1)S(1)} %copy-done.6, ...), custom_call_target="tpu_custom_call" | custom-call | flops 1000 | bytes 1000 | tf_op jit(solution)/shard_map/image_blocks/pallas_call | solution.py:476
  23.5 6.3 %collective-permute-start.5 = (bf16[512,512]{1,0:T(8,128)(2,1)S(1)}, bf16[512,512]{1,0:T(8,128)(2,1)S(1)}, u32[]{:S(2)}, u32[]{:S(2)}) collective-permute-start(bf16[512,512]{1,0:T(8,128)(2,1)S(1)} %get-tuple-element.31), channel_id=1, source_target_pairs={{0,4},{12,8},{1,5},{13,9},{2,6},{14,10},{3,7},{15,11},{16,20},{28,... | collective-permute-start | bytes 1572872 | tf_op jit(solution)/shard_map/ppermute | solution.py:620
  29.8 0.0 collective-permute-done.2.more_1_
  29.8 0.1 fusion
  29.9 1.5 %collective-permute-start.4 = (bf16[512,512]{1,0:T(8,128)(2,1)S(1)}, bf16[512,512]{1,0:T(8,128)(2,1)S(1)}, u32[]{:S(2)}, u32[]{:S(2)}) collective-permute-start(bf16[512,512]{1,0:T(8,128)(2,1)S(1)} %fusion), channel_id=1, source_target_pairs={{0,8},{12,4},{4,12},{8,0},{1,9},{13,5},{5,13},{9,1},{2,10},{14,6},... | collective-permute-start | bytes 1572872 | tf_op jit(solution)/shard_map/ppermute | solution.py:623
  31.4 0.0 collective-permute-done.3.more_2_
  31.4 12.7 %model_term.1 = f32[512,512]{1,0:T(8,128)S(1)} custom-call(s32[4,4,8]{2,1,0:T(4,128)S(1)} %bitcast.5, s32[2,8]{1,0:T(2,128)S(1)} %bitcast.9, f32[8]{0:T(128)S(1)} %copy-done.9, bf16[512,640]{1,0:T(8,128)(2,1)S(1)} %get-tuple-element.27.wide_ref, f32[16,640]{1,0:T(8,128)S(1)} %copy-done.11, bf16[8,25]{1,0:T(8,128)(2,1)S(1)} %copy-done.6, ...), custom_call_target="tpu_custom_call" | custom-call | flops 10400000000 | bytes 2000000 | tf_op jit(solution)/shard_map/model_term/pallas_call | solution.py:568
  44.1 0.0 collective-permute-done.5
  44.1 11.7 %collective-permute-done.4 = bf16[512,512]{1,0:T(8,128)(2,1)S(1)} collective-permute-done((bf16[512,512]{1,0:T(8,128)(2,1)S(1)}, bf16[512,512]{1,0:T(8,128)(2,1)S(1)}, u32[]{:S(2)}, u32[]{:S(2)}) %collective-permute-start.4) | collective-permute-done | bytes 524320 | tf_op jit(solution)/shard_map/ppermute | solution.py:623
  55.9 1.2 %convert_add_fusion = f32[512,512]{1,0:T(8,128)} fusion(bf16[512,512]{1,0:T(8,128)(2,1)S(1)} %collective-permute-done.5, f32[512,512]{1,0:T(8,128)S(1)} %model_term.1, bf16[512,512]{1,0:T(8,128)(2,1)S(1)} %collective-permute-done.4), kind=kLoop, calls=%fused_computation | loop fusion | flops 1048576 | bytes 3145728 | tf_op jit(solution)/shard_map/add | solution.py:625
  (11 shorter events, 0.0 us)
Async XLA Ops:
  0.0 5.3 %copy-start.3 = (s32[8,512]{1,0:T(8,128)S(1)}, s32[8,512]{1,0:T(8,128)}, u32[]{:S(2)}) copy-start(s32[8,512]{1,0:T(8,128)} %mask_ref.7) | copy-start | bytes 49156
  0.0 5.3 %copy-start = (bf16[2,2048,512]{2,1,0:T(8,128)(2,1)S(1)}, bf16[2,2048,512]{2,1,0:T(8,128)(2,1)}, u32[]{:S(2)}) copy-start(bf16[2,2048,512]{2,1,0:T(8,128)(2,1)} %images_ref.5) | copy-start | bytes 12582916
  0.0 9.6 %copy-start.2 = (bf16[512,512]{1,0:T(8,128)(2,1)S(1)}, bf16[512,512]{1,0:T(8,128)(2,1)}, u32[]{:S(2)}) copy-start(bf16[512,512]{1,0:T(8,128)(2,1)} %scene_ref.3) | copy-start | bytes 1572868
  0.0 5.3 %copy-start.8 = (s32[8,2]{0,1:T(2,128)S(1)}, s32[8,2]{0,1:T(2,128)}, u32[]{:S(2)}) copy-start(s32[8,2]{0,1:T(2,128)} %param.12) | copy-start | bytes 196
  0.0 5.3 %copy-start.9 = (f32[8]{0:T(128)S(1)}, f32[8]{0:T(128)}, u32[]{:S(2)}) copy-start(f32[8]{0:T(128)} %weight_ref.7) | copy-start | bytes 100
  0.0 5.3 %copy-start.7 = (bf16[8,25]{1,0:T(8,128)(2,1)S(1)}, bf16[8,25]{1,0:T(8,128)(2,1)}, u32[]{:S(2)}) copy-start(bf16[8,25]{1,0:T(8,128)(2,1)} %psf_cols_ref.7) | copy-start | bytes 1204
  0.0 5.3 %copy-start.6 = (bf16[8,25]{1,0:T(8,128)(2,1)S(1)}, bf16[8,25]{1,0:T(8,128)(2,1)}, u32[]{:S(2)}) copy-start(bf16[8,25]{1,0:T(8,128)(2,1)} %psf_rows_ref.7) | copy-start | bytes 1204
  4.1 5.5 %collective-permute-start = (bf16[48,2176]{1,0:T(8,128)(2,1)}, bf16[48,2176]{1,0:T(8,128)(2,1)S(1)}, u32[]{:S(2)}, u32[]{:S(2)}) collective-permute-start(bf16[48,2176]{1,0:T(8,128)(2,1)} %get-tuple-element.22), channel_id=1, source_target_pairs={{0,1},{1,0},{2,3},{3,2},{4,5},{5,4},{6,7},{7,6},{8,9},{9,8},{10,11... | collective-permute-start | bytes 626696 | tf_op jit(solution)/shard_map/ppermute | solution.py:607
  4.6 5.0 %collective-permute-start.1 = (bf16[48,2176]{1,0:T(8,128)(2,1)}, bf16[48,2176]{1,0:T(8,128)(2,1)S(1)}, u32[]{:S(2)}, u32[]{:S(2)}) collective-permute-start(bf16[48,2176]{1,0:T(8,128)(2,1)} %get-tuple-element.23), channel_id=1, source_target_pairs={{1,2},{2,1},{5,6},{6,5},{9,10},{10,9},{13,14},{14,13},{17,18},{18,... | collective-permute-start | bytes 626696 | tf_op jit(solution)/shard_map/ppermute | solution.py:608
  5.3 0.7 %copy-start.4 = (s32[8,4,4]{0,2,1:T(4,128)S(1)}, s32[8,4,4]{0,2,1:T(4,128)}, u32[]{:S(2)}) copy-start(s32[8,4,4]{0,2,1:T(4,128)} %param.15) | copy-start | bytes 1540
  6.0 10.8 %copy-start.5 = (s32[8,4,4]{0,2,1:T(4,128)S(1)}, s32[8,4,4]{0,2,1:T(4,128)}, u32[]{:S(2)}) copy-start(s32[8,4,4]{0,2,1:T(4,128)} %param.15) | copy-start | bytes 1540
  12.9 0.6 %copy-start.10 = (f32[16,640]{1,0:T(8,128)}, f32[16,640]{1,0:T(8,128)S(1)}, u32[]{:S(2)}) copy-start(f32[16,640]{1,0:T(8,128)S(1)} %get-tuple-element.34.good_ref) | copy-start | bytes 122884
  13.5 16.3 %collective-permute-start.2 = (bf16[560,512]{1,0:T(8,128)(2,1)}, bf16[560,512]{1,0:T(8,128)(2,1)S(1)}, u32[]{:S(2)}, u32[]{:S(2)}) collective-permute-start(bf16[560,512]{1,0:T(8,128)(2,1)} %get-tuple-element.32), channel_id=1, source_target_pairs={{0,4},{4,0},{8,12},{12,8},{1,5},{5,1},{9,13},{13,9},{2,6},{6,2},{1... | collective-permute-start | bytes 1720328 | tf_op jit(solution)/shard_map/ppermute | solution.py:616
  16.1 15.3 %collective-permute-start.3 = (bf16[560,512]{1,0:T(8,128)(2,1)S(1)}, bf16[560,512]{1,0:T(8,128)(2,1)S(1)}, u32[]{:S(2)}, u32[]{:S(2)}) collective-permute-start(bf16[560,512]{1,0:T(8,128)(2,1)S(1)} %get-tuple-element.29), channel_id=1, source_target_pairs={{4,8},{8,4},{5,9},{9,5},{6,10},{10,6},{7,11},{11,7},{20,24},{24,20... | collective-permute-start | bytes 1720328 | tf_op jit(solution)/shard_map/ppermute | solution.py:617
  16.8 2.2 %copy-start.1 = (bf16[2,2048,512]{2,1,0:T(8,128)(2,1)S(1)}, bf16[2,2048,512]{2,1,0:T(8,128)(2,1)}, u32[]{:S(2)}) copy-start(bf16[2,2048,512]{2,1,0:T(8,128)(2,1)} %images_ref.5) | copy-start | bytes 12582916
  19.0 12.4 %copy-start.11 = (f32[16,640]{1,0:T(8,128)S(1)}, f32[16,640]{1,0:T(8,128)}, u32[]{:S(2)}) copy-start(f32[16,640]{1,0:T(8,128)} %copy-done.10) | copy-start | bytes 122884
  23.5 20.6 %collective-permute-start.5 = (bf16[512,512]{1,0:T(8,128)(2,1)S(1)}, bf16[512,512]{1,0:T(8,128)(2,1)S(1)}, u32[]{:S(2)}, u32[]{:S(2)}) collective-permute-start(bf16[512,512]{1,0:T(8,128)(2,1)S(1)} %get-tuple-element.31), channel_id=1, source_target_pairs={{0,4},{12,8},{1,5},{13,9},{2,6},{14,10},{3,7},{15,11},{16,20},{28,... | collective-permute-start | bytes 1572872 | tf_op jit(solution)/shard_map/ppermute | solution.py:620
  29.9 26.0 %collective-permute-start.4 = (bf16[512,512]{1,0:T(8,128)(2,1)S(1)}, bf16[512,512]{1,0:T(8,128)(2,1)S(1)}, u32[]{:S(2)}, u32[]{:S(2)}) collective-permute-start(bf16[512,512]{1,0:T(8,128)(2,1)S(1)} %fusion), channel_id=1, source_target_pairs={{0,8},{12,4},{4,12},{8,0},{1,9},{13,5},{5,13},{9,1},{2,10},{14,6},... | collective-permute-start | bytes 1572872 | tf_op jit(solution)/shard_map/ppermute | solution.py:623

commit v3 on v2

v3 whole, which is shorter than its diff:
```python
import functools

import jax
import jax.numpy as jnp
from jax import lax
from jax.experimental import pallas as pl
from jax.experimental.pallas import tpu as pltpu
from jax.sharding import PartitionSpec as P

TILE = 512
HALO = 16
RIM = 2 * HALO
LANES = 128
SPAN = 256
STEP = SPAN - RIM
F32 = jnp.float32
BF16 = jnp.bfloat16
VMEM = pl.BlockSpec(memory_space=pltpu.VMEM)
SMEM = pl.BlockSpec(memory_space=pltpu.SMEM)
HBM = pl.BlockSpec(memory_space=pltpu.HBM)
PARAMS = pltpu.CompilerParams(vmem_limit_bytes=40 * 1024 * 1024)
SHORT = pl.CostEstimate(flops=1000, bytes_accessed=1000, transcendentals=0)
WHOLE = pltpu.CompilerParams(vmem_limit_bytes=59 * 1024 * 1024)


def up_to(value, unit):
    return -(-value // unit) * unit


def dot(a, b, dims=((1,), (0,))):
    return lax.dot_general(a, b, (dims, ((), ())), preferred_element_type=F32)


def iota(shape, dim):
    return lax.broadcasted_iota(jnp.int32, shape, dim)


def selection(rows, cols, shift):
    return (iota((rows, cols), 1) == iota((rows, cols), 0) + shift).astype(BF16)


def toeplitz(taps, start, rows, width):
    line = jnp.concatenate([taps, jnp.zeros((1, width - LANES), F32)], axis=1)
    line = jnp.broadcast_to(line, (8, width))
    line = pltpu.roll(line, lax.rem(2 * width - start, width), 1)[0:1]
    line = jnp.broadcast_to(line, (rows, width))
    return pltpu.roll(line, 0, 1, stride=1, stride_axis=0).astype(BF16)


def row_of(values, index):
    return jnp.sum(jnp.where(iota(values.shape, 0) == index, values, 0), axis=0, keepdims=True)


def load_taps(psf_ref, lines, epochs, taps):
    lines[0] = jnp.zeros(lines.shape[1:], F32)
    lines[0, :epochs, :taps] = psf_ref[...].astype(F32)
    mirror = iota((LANES, LANES), 0) + iota((LANES, LANES), 1) == taps - 1
    lines[1] = dot(lines[0].astype(BF16), mirror.astype(F32).astype(BF16))


def spans(length):
    return [(s, min(STEP, length - s)) for s in range(0, length, STEP)]


class Sizes:
    def __init__(self, images, sky_scene, psf_rows):
        self.local, self.height, self.width = images.shape
        self.rows = sky_scene.shape[0]
        self.epochs = psf_rows.shape[0]
        self.taps = psf_rows.shape[1]
        self.tile_rows = self.height // TILE
        self.wide = self.width + LANES
        self.groups = self.height // SPAN
        self.part = min(self.rows, SPAN)
        self.mask_rows = up_to(self.epochs, HALO)
        self.scene_at = SPAN * self.local
        self.mask_at = self.scene_at + self.part
        self.buffer_rows = self.mask_at + self.mask_rows
        self.blocks = self.height // self.rows
        self.tap_rows = self.mask_rows


def cover_at(coverage_ref, epoch, row_tile, col_tile):
    last_row = coverage_ref.shape[0] - 1
    last_col = coverage_ref.shape[1] - 1
    inside = (row_tile >= 0) & (row_tile <= last_row) & (col_tile >= 0) & (col_tile <= last_col)
    value = coverage_ref[jnp.clip(row_tile, 0, last_row), jnp.clip(col_tile, 0, last_col), epoch]
    return jnp.where(inside, value, 0).astype(F32)


def tile_of(position):
    return (position + TILE) // TILE - 1


def low(index, size):
    return index & (size - 1)


def high(index, size):
    return lax.shift_right_logical(index, size.bit_length() - 1)


def packing(count, width, shift):
    row, lane = iota((LANES * count, LANES), 0), iota((LANES * count, LANES), 1)
    here = high(lane, width) == high(row, LANES)
    here &= low(row, LANES) == low(lane, width) + shift
    return here.astype(F32).astype(BF16)


def side_by_side(ref, count, rows):
    return jnp.concatenate([ref[g * rows : (g + 1) * rows] for g in range(count)], axis=1)


def edge_copies(sz, images_ref, scene_ref, edge, sides, sem, side_sem):
    places = (0, sz.width - LANES)
    copies = []
    for e in range(sz.local):
        for side in range(2):
            slot = 2 * e + side
            copies.append(
                pltpu.make_async_copy(
                    images_ref.at[e, :, pl.ds(places[side], LANES)], edge.at[slot], sem.at[slot]
                )
            )
    side_copies = [
        pltpu.make_async_copy(
            scene_ref.at[:, pl.ds(places[side], LANES)], sides.at[side], side_sem.at[side]
        )
        for side in range(2)
    ]
    return copies, side_copies


def pack_edges(sz, flags, edge, sides, copies, side_copies, first_ref, second_ref):
    epoch = lax.axis_index("epoch") * sz.local
    even = lax.axis_index("sky") % 2 == 0
    places = (0, sz.width - LANES)

    def put(left, right, rows):
        first_ref[rows] = jnp.where(even, right, left).astype(BF16)
        second_ref[rows] = jnp.where(even, left, right).astype(BF16)

    packs = [packing(sz.groups, HALO, shift) for shift in (0, LANES - HALO)]
    row, lane = iota((LANES, LANES), 0), iota((LANES, LANES), 1)
    repeats = [
        (row == low(lane, HALO) + shift).astype(F32).astype(BF16) for shift in (0, LANES - HALO)
    ]
    for copy in copies + side_copies:
        copy.wait()
    goods, rows_good = [], []
    for side in range(2):
        good = flags[:, places[side] : places[side] + LANES].astype(F32)
        rows_good.append(good)
        if side == 1:
            good = pltpu.roll(good, HALO, 1)
        if sz.mask_rows > sz.epochs:
            good = jnp.concatenate(
                [good, jnp.zeros((sz.mask_rows - sz.epochs, LANES), F32)], axis=0
            )
        goods.append(good)
    put(goods[0], goods[1], slice(sz.mask_at, sz.buffer_rows))
    for e in range(sz.local):
        lines = []
        for side in range(2):
            slot = 2 * e + side
            good = jnp.broadcast_to(row_of(rows_good[side], epoch + e), (HALO, LANES))
            good = dot(good.astype(BF16), repeats[side])[0:1]
            lines.append(dot(side_by_side(edge.at[slot], sz.groups, SPAN), packs[side]) * good)
        put(lines[0], lines[1], slice(SPAN * e, SPAN * (e + 1)))
    cells = []
    count = sz.rows // sz.part
    for side, shift in enumerate((0, LANES - RIM)):
        cells.append(
            dot(side_by_side(sides.at[side], count, sz.part), packing(count, RIM, shift))
        )
    put(cells[0], cells[1], slice(sz.scene_at, sz.mask_at))


def edges_kernel(sz, images_ref, scene_ref, mask_ref, first_ref, second_ref, *scratch):
    edge, sides, flags, sem, side_sem, flag_sem = scratch
    copies, side_copies = edge_copies(sz, images_ref, scene_ref, edge, sides, sem, side_sem)
    flag_copy = pltpu.make_async_copy(mask_ref, flags, flag_sem)
    for copy in [flag_copy] + copies + side_copies:
        copy.start()
    flag_copy.wait()
    pack_edges(sz, flags, edge, sides, copies, side_copies, first_ref, second_ref)


def edges(sz, images, scene, mask):
    shape = jax.ShapeDtypeStruct((sz.buffer_rows, LANES), BF16)
    return pl.pallas_call(
        functools.partial(edges_kernel, sz),
        out_shape=(shape, shape),
        in_specs=[HBM, HBM, HBM],
        out_specs=(VMEM, VMEM),
        scratch_shapes=[
            pltpu.VMEM((2 * sz.local, sz.height, LANES), BF16),
            pltpu.VMEM((2, sz.rows, LANES), BF16),
            pltpu.VMEM((sz.epochs, sz.width), jnp.int32),
            pltpu.SemaphoreType.DMA((2 * sz.local,)),
            pltpu.SemaphoreType.DMA((2,)),
            pltpu.SemaphoreType.DMA,
        ],
        compiler_params=WHOLE,
        cost_estimate=SHORT,
        name="edges",
    )(images, scene, mask)


def sides_of(first, second):
    even = lax.axis_index("sky") % 2 == 0
    return jnp.where(even, second, first), jnp.where(even, first, second)


def widen_rows(sz, scene_ref, first_ref, second_ref, start, count):
    group, inside = start // sz.part, start % sz.part
    cells = slice(sz.scene_at + inside, sz.scene_at + inside + count)
    row, lane = iota((LANES, sz.wide), 0), iota((LANES, sz.wide), 1)
    wide = dot(scene_ref[start : start + count], selection(sz.width, sz.wide, RIM))
    ends = sides_of(first_ref[cells], second_ref[cells])
    for end, at in zip(ends, (0, sz.width + RIM)):
        place = (high(row, RIM) == group) & (lane == low(row, RIM) + at)
        wide += dot(end, place.astype(F32).astype(BF16))
    return wide.astype(BF16)


def widen_kernel(sz, scene_ref, mask_ref, first_ref, second_ref, wide_ref, good_ref):
    for start in range(0, sz.rows, sz.part):
        wide_ref[start : start + sz.part] = widen_rows(
            sz, scene_ref, first_ref, second_ref, start, sz.part
        )
    flags = slice(sz.mask_at, sz.buffer_rows)
    before, after = sides_of(first_ref[flags], second_ref[flags])
    own = mask_ref[...].astype(F32)
    if sz.mask_rows > sz.epochs:
        own = jnp.concatenate(
            [own, jnp.zeros((sz.mask_rows - sz.epochs, sz.width), F32)], axis=0
        )
    good = dot(own.astype(BF16), selection(sz.width, sz.wide, HALO))
    inner = iota((LANES, sz.wide), 0) < HALO
    zero = jnp.zeros((LANES, sz.wide), BF16)
    good += dot(before, jnp.where(inner, selection(LANES, sz.wide, 0), zero))
    good += dot(after, jnp.where(inner, selection(LANES, sz.wide, sz.width + HALO), zero))
    good_ref[...] = good


def destination(slot, place):
    return (
        3 * (1 - place % 2),
        2 - place // 2,
        (2 * place + 1) % 5,
        place,
    )[slot]


def rim_rows(sz, epoch, e, coverage_ref, row_line, row_shift, twice, first_ref, second_ref):
    rows = slice(SPAN * e, SPAN * (e + 1))
    column = lax.axis_index("sky") * sz.width
    both = jnp.concatenate(sides_of(first_ref[rows], second_ref[rows]), axis=1)
    lane = iota((1, 2 * LANES), 1)
    factor = jnp.zeros((1, 2 * LANES), F32)
    for side, at in enumerate((column - HALO, column + sz.width)):
        for tile in range(sz.tile_rows):
            cover = cover_at(coverage_ref, epoch, tile, tile_of(at))
            here = high(lane, LANES) == side
            here &= high(low(lane, LANES), HALO * TILE // SPAN) == tile
            factor = jnp.where(here, cover, factor)
    both = both.astype(F32) * factor
    above = pltpu.roll(both[SPAN - HALO :], HALO, 1)
    below = pltpu.roll(both[:HALO], 2 * LANES - HALO, 1)
    above = jnp.where(low(lane, LANES) < HALO, 0.0, above)
    below = jnp.where(low(lane, LANES) >= HALO * (sz.groups - 1), 0.0, below)
    window = jnp.concatenate([above, both, below], axis=0).astype(BF16)
    table = toeplitz(row_line, row_shift - 4, SPAN, SPAN + LANES)[:, : SPAN + RIM]
    return (dot(table, window) * twice).astype(BF16)


def rim_columns(col_line, col_shift):
    enter = toeplitz(col_line, 28 - col_shift, HALO, SPAN)[:, :LANES]
    leave = toeplitz(col_line, SPAN + LANES - 116 - col_shift, HALO, SPAN + LANES)[:, :LANES]
    none = jnp.zeros((HALO, LANES), BF16)
    upper = [jnp.concatenate([enter, none], axis=1)] * (LANES // HALO)
    lower = [jnp.concatenate([none, leave], axis=1)] * (LANES // HALO)
    return jnp.concatenate(upper + lower, axis=0)


def rim_part(sz, start, rim_ref, table):
    group = start // SPAN
    row = iota((2 * LANES, SPAN), 0)
    parts = []
    for k in range(max(sz.rows // SPAN, 1)):
        picked = jnp.where(high(low(row, LANES), HALO) == group + k, table, jnp.zeros_like(table))
        if sz.rows >= SPAN:
            rows = rim_ref[...]
        else:
            rows = rim_ref[pl.ds(pl.multiple_of(start - group * SPAN, sz.rows), sz.rows)]
        parts.append(dot(rows, picked))
    return jnp.concatenate(parts, axis=0) if len(parts) > 1 else parts[0]


def rim_places(sz, h):
    row, lane = iota((SPAN, LANES), 0), iota((SPAN, LANES), 1)
    here = (lane == row + RIM * h) & (row < HALO)
    here |= (lane == row - SPAN + RIM * (h + 1)) & (row >= SPAN - HALO)
    return here.astype(F32).astype(BF16)


def rim_spread(sz, h):
    row, lane = iota((LANES, SPAN), 0), iota((LANES, SPAN), 1)
    here = (row == lane + RIM * h) & (lane < HALO)
    here |= (row == lane - SPAN + RIM * (h + 1)) & (lane >= SPAN - HALO)
    return here.astype(F32).astype(BF16)


def pack_rows(sz, ref, at, rim):
    ref[at : at + RIM] = rim[:, : sz.width]
    left = slice(at + RIM, at + RIM + HALO)
    ref[left, :LANES] = rim[:HALO, sz.width :]
    ref[left, LANES:SPAN] = rim[HALO:, sz.width :]
    ref[left, SPAN:] = jnp.zeros((HALO, sz.width - SPAN), BF16)


def pack_part(sz, ref, at, part):
    total = None
    for h in range(sz.rows // LANES):
        rows = part[h * LANES : (h + 1) * LANES].astype(BF16)
        moved = dot(rows, rim_places(sz, h))
        total = moved if total is None else total + moved
    total = total.astype(BF16)
    for k in range(LANES // RIM):
        ref[at : at + RIM, k * LANES : (k + 1) * LANES] = total[k * RIM : (k + 1) * RIM]


def unpack_rim(sz, ref, at):
    left = slice(at + RIM, at + RIM + HALO)
    rest = jnp.concatenate([ref[left, :LANES], ref[left, LANES:SPAN]], axis=0)
    return jnp.concatenate([ref[at : at + RIM], rest], axis=1)


def unpack_part(sz, ref, at):
    pieces = [ref[at : at + RIM, k * LANES : (k + 1) * LANES] for k in range(LANES // RIM)]
    packed = jnp.concatenate(pieces, axis=0)
    parts = [dot(packed, rim_spread(sz, h)) for h in range(sz.rows // LANES)]
    return jnp.concatenate(parts, axis=0)


def complete(sz, block, part):
    left, right = slice(0, LANES), slice(sz.width - LANES, sz.width)
    mid = slice(LANES, sz.width - LANES)
    return (
        (left, (block[:, left].astype(F32) + part[:, :LANES]).astype(BF16)),
        (mid, block[:, mid]),
        (right, (block[:, right].astype(F32) + part[:, LANES:]).astype(BF16)),
    )


def rim_parts_of(sz, slots, place, offsets_ref, col_lines, rim_ref):
    tables = []
    for e in range(sz.local):
        epoch = place * sz.local + e
        tables.append(rim_columns(row_of(col_lines[0], epoch), offsets_ref[1, epoch]))
    parts = []
    for slot in slots:
        part = None
        for e in range(sz.local):
            term = rim_part(sz, destination(slot, place) * sz.rows, rim_ref.at[e], tables[e])
            part = term if part is None else part + term
        parts.append(part)
    return parts


def early_kernel(
    sz, coverage_ref, offsets_ref, weight_ref, scene_ref, first_ref, second_ref,
    psf_rows_ref, psf_cols_ref, one_ref, three_ref, near_out, far_out, pass_out, rim_ref,
    row_lines, col_lines,
):
    place = lax.axis_index("epoch")
    outer = (place == 0) | (place == 3)
    load_taps(psf_rows_ref, row_lines, sz.epochs, sz.taps)
    load_taps(psf_cols_ref, col_lines, sz.epochs, sz.taps)
    for e in range(sz.local):
        epoch = place * sz.local + e
        rim_ref[e] = rim_rows(
            sz, epoch, e, coverage_ref, row_of(row_lines[1], epoch), offsets_ref[0, epoch],
            -2.0 * weight_ref[epoch], first_ref, second_ref,
        )
    parts = rim_parts_of(sz, (0, 2, 1), place, offsets_ref, col_lines, rim_ref)
    top = widen_rows(sz, scene_ref, first_ref, second_ref, 0, RIM)
    bottom = widen_rows(sz, scene_ref, first_ref, second_ref, sz.rows - RIM, RIM)
    pack_rows(sz, near_out, sz.rows, jnp.where(place % 2 == 0, bottom, top))
    pack_rows(sz, far_out, 0, jnp.where(place < 2, bottom, top))
    pack_part(sz, far_out, RIM + HALO, parts[2])
    first_block, third_block = complete(sz, one_ref, parts[0]), complete(sz, three_ref, parts[1])
    for (cols, other), (_, mine) in zip(first_block, third_block):
        near_out[: sz.rows, cols] = jnp.where(outer, mine, other)
        pass_out[: sz.rows, cols] = mine
    pass_out[sz.rows :] = jnp.zeros((HALO, sz.width), BF16)


def early(sz, coverage, offsets, weight, scene, first, second, psf_rows, psf_cols, one, three):
    return pl.pallas_call(
        functools.partial(early_kernel, sz),
        out_shape=(
            jax.ShapeDtypeStruct((sz.rows + RIM + HALO, sz.width), BF16),
            jax.ShapeDtypeStruct((2 * RIM + HALO, sz.width), BF16),
            jax.ShapeDtypeStruct((sz.rows + HALO, sz.width), BF16),
            jax.ShapeDtypeStruct((sz.local, SPAN, 2 * LANES), BF16),
        ),
        in_specs=[SMEM] * 3 + [VMEM] * 7,
        out_specs=(VMEM, VMEM, VMEM, VMEM),
        scratch_shapes=[pltpu.VMEM((2, sz.tap_rows, LANES), F32)] * 2,
        compiler_params=PARAMS,
        cost_estimate=SHORT,
        name="early",
    )(coverage, offsets, weight, scene, first, second, psf_rows, psf_cols, one, three)


def finish_kernel(sz, offsets_ref, scene_ref, mask_ref, first_ref, second_ref, *more):
    if sz.blocks != 4:
        widen_kernel(sz, scene_ref, mask_ref, first_ref, second_ref, *more)
        return
    psf_cols_ref, rim_ref, two_ref, own_ref, wide_ref, good_ref, fix_out = more[:7]
    two_out, own_out, col_lines = more[7:]
    place = lax.axis_index("epoch")
    load_taps(psf_cols_ref, col_lines, sz.epochs, sz.taps)
    parts = rim_parts_of(sz, (0, 1, 3), place, offsets_ref, col_lines, rim_ref)
    widen_kernel(sz, scene_ref, mask_ref, first_ref, second_ref, wide_ref, good_ref)
    pack_part(sz, fix_out, 0, parts[0])
    for block, out, part in ((two_ref, two_out, parts[1]), (own_ref, own_out, parts[2])):
        for cols, value in complete(sz, block, part):
            out[:, cols] = value


def finish(sz, offsets, scene, mask, first, second, *more):
    full = jax.ShapeDtypeStruct((sz.rows, sz.width), BF16)
    shapes = [
        jax.ShapeDtypeStruct((sz.rows, sz.wide), BF16),
        jax.ShapeDtypeStruct((sz.mask_rows, sz.wide), F32),
    ]
    scratch = []
    if more:
        shapes += [jax.ShapeDtypeStruct((RIM, sz.width), BF16), full, full]
        scratch = [pltpu.VMEM((2, sz.tap_rows, LANES), F32)]
    return pl.pallas_call(
        functools.partial(finish_kernel, sz),
        out_shape=tuple(shapes),
        in_specs=[SMEM] + [VMEM] * (4 + len(more)),
        out_specs=tuple([VMEM] * len(shapes)),
        scratch_shapes=scratch,
        compiler_params=PARAMS,
        cost_estimate=SHORT,
        name="finish",
    )(offsets, scene, mask, first, second, *more)


def image_kernel(sz, slots, rims, packs, images_ref, *more):
    count = 1 if slots is None else len(slots)
    small, ends, more = more[:6], more[6 : 6 + rims], more[6 + rims :]
    if packs:
        scene_ref, *more = more
    outs, more = more[:count], more[count:]
    if packs:
        first_out, second_out, edge, sides, edge_sem, side_sem, *more = more
    held, small_sem, more = more[:6], more[6], more[7:]
    coverage_ref, offsets_ref, weight_ref, mask_ref, psf_rows_ref, psf_cols_ref = held
    window, row_done, row_lines, col_lines, row_table, main_table, cross_table, rim_ref, sem = more
    place = lax.axis_index("epoch")
    first = place * sz.local
    column = lax.axis_index("sky") * sz.width
    if slots is None:
        targets = [pl.program_id(0)]
    else:
        targets = [destination(slot, place) for slot in slots]

    copies = []
    for i, target in enumerate(targets):
        start = target * sz.rows
        head = jnp.maximum(start - HALO, 0)
        foot = jnp.minimum(start + sz.rows, sz.height - HALO)
        for e in range(sz.local):
            for n, (source, at, length) in enumerate(
                ((start, HALO, sz.rows), (head, 0, HALO), (foot, HALO + sz.rows, HALO))
            ):
                copies.append(
                    pltpu.make_async_copy(
                        images_ref.at[e, pl.ds(pl.multiple_of(source, HALO), length), :],
                        window.at[i, e, pl.ds(at, length), :],
                        sem.at[i, e, n],
                    )
                )
    held_copies = [
        pltpu.make_async_copy(source, target, small_sem.at[n])
        for n, (source, target) in enumerate(zip(small, held))
    ]
    for copy in held_copies + copies:
        copy.start()
    if packs:
        edge_waits = edge_copies(sz, images_ref, scene_ref, edge, sides, edge_sem, side_sem)
        for copy in edge_waits[0] + edge_waits[1]:
            copy.start()
    for copy in held_copies:
        copy.wait()
    load_taps(psf_rows_ref, row_lines, sz.epochs, sz.taps)
    load_taps(psf_cols_ref, col_lines, sz.epochs, sz.taps)
    for e in range(sz.local):
        epoch = first + e
        row_shift, col_shift = offsets_ref[0, epoch], offsets_ref[1, epoch]
        row_table[e] = toeplitz(row_of(row_lines[1], epoch), row_shift - 4, STEP, SPAN)
        line = row_of(col_lines[0], epoch)
        main = toeplitz(line, 12 - col_shift, SPAN, SPAN + LANES)[:, :SPAN]
        main_table[e] = main
        apart = (iota((SPAN, SPAN), 0) < LANES) != (iota((SPAN, SPAN), 1) < LANES)
        cross_table[e] = jnp.where(apart, main, jnp.zeros_like(main))
    rim_parts = []
    for e in range(sz.local if rims else 0):
        epoch = first + e
        rim_ref[e] = rim_rows(
            sz, epoch, e, coverage_ref, row_of(row_lines[1], epoch), offsets_ref[0, epoch],
            -2.0 * weight_ref[epoch], *ends,
        )
        table = rim_columns(row_of(col_lines[0], epoch), offsets_ref[1, epoch])
        for i, target in enumerate(targets):
            part = rim_part(sz, target * sz.rows, rim_ref.at[e], table)
            if e == 0:
                rim_parts.append(part)
            else:
                rim_parts[i] += part
    column_tile = column // TILE
    for i, target in enumerate(targets):
        for copy in copies[3 * sz.local * i : 3 * sz.local * (i + 1)]:
            copy.wait()
        start = target * sz.rows
        zones = (
            (0, HALO, tile_of(start - HALO)),
            (HALO, HALO + sz.rows, tile_of(start)),
            (HALO + sz.rows, RIM + sz.rows, tile_of(start + sz.rows)),
        )
        for e in range(sz.local):
            epoch = first + e
            good = row_of(mask_ref[...].astype(F32), epoch)
            for begin, end, tile in zones:
                factor = good * cover_at(coverage_ref, epoch, tile, column_tile)
                window[i, e, begin:end] = window[i, e, begin:end] * factor.astype(BF16)
            twice = -2.0 * weight_ref[epoch]
            for s, n in spans(sz.rows):
                part = dot(row_table[e, :n, : n + RIM], window[i, e, s : s + n + RIM])
                row_done[i, e, s : s + n] = (part * twice).astype(BF16)
    for i in range(count):
        total = []
        for b in range(0, sz.width, SPAN):
            out = None
            for e in range(sz.local):
                part = dot(row_done[i, e, :, b : b + SPAN], main_table[e])
                out = part if out is None else out + part
            total += [out[:, :LANES], out[:, LANES:]]
        for b in range(LANES, sz.width - LANES, SPAN):
            out = None
            for e in range(sz.local):
                part = dot(row_done[i, e, :, b : b + SPAN], cross_table[e])
                out = part if out is None else out + part
            total[b // LANES] += out[:, :LANES]
            total[b // LANES + 1] += out[:, LANES:]
        if rims:
            total[0] += rim_parts[i][:, :LANES]
            total[-1] += rim_parts[i][:, LANES:]
        for k, piece in enumerate(total):
            outs[i][:, k * LANES : (k + 1) * LANES] = piece.astype(BF16)
    if packs:
        pack_edges(sz, mask_ref, edge, sides, *edge_waits, first_out, second_out)


def image_blocks(
    sz, slots, coverage, offsets, weight, images, mask, psf_rows, psf_cols, *ends, scene=None
):
    packs = scene is not None
    if slots is None:
        count = 1
        grid = dict(
            grid=(sz.blocks,),
            out_shape=jax.ShapeDtypeStruct((sz.blocks * sz.rows, sz.width), BF16),
            out_specs=pl.BlockSpec((sz.rows, sz.width), lambda i: (i, 0)),
        )
    else:
        count = len(slots)
        shapes = [jax.ShapeDtypeStruct((sz.rows, sz.width), BF16)] * count
        if packs:
            shapes += [jax.ShapeDtypeStruct((sz.buffer_rows, LANES), BF16)] * 2
        grid = dict(out_shape=tuple(shapes), out_specs=tuple([VMEM] * len(shapes)))
    pack_scratch = [
        pltpu.VMEM((2 * sz.local, sz.height, LANES), BF16),
        pltpu.VMEM((2, sz.rows, LANES), BF16),
        pltpu.SemaphoreType.DMA((2 * sz.local,)),
        pltpu.SemaphoreType.DMA((2,)),
    ]
    return pl.pallas_call(
        functools.partial(image_kernel, sz, slots, len(ends), packs),
        in_specs=[HBM] * 7 + [VMEM] * len(ends) + [HBM] * packs,
        scratch_shapes=pack_scratch * packs
        + [
            pltpu.SMEM(coverage.shape, jnp.int32),
            pltpu.SMEM(offsets.shape, jnp.int32),
            pltpu.SMEM(weight.shape, F32),
            pltpu.VMEM(mask.shape, jnp.int32),
            pltpu.VMEM(psf_rows.shape, BF16),
            pltpu.VMEM(psf_cols.shape, BF16),
            pltpu.SemaphoreType.DMA((6,)),
            pltpu.VMEM((count, sz.local, sz.rows + RIM, sz.width), BF16),
            pltpu.VMEM((count, sz.local, sz.rows, sz.width), BF16),
            pltpu.VMEM((2, sz.tap_rows, LANES), F32),
            pltpu.VMEM((2, sz.tap_rows, LANES), F32),
            pltpu.VMEM((sz.local, STEP, SPAN), BF16),
            pltpu.VMEM((sz.local, SPAN, SPAN), BF16),
            pltpu.VMEM((sz.local, SPAN, SPAN), BF16),
            pltpu.VMEM((sz.local, SPAN, 2 * LANES), BF16),
            pltpu.SemaphoreType.DMA((count, sz.local, 3)),
        ],
        compiler_params=WHOLE if slots is not None and 0 in slots else PARAMS,
        cost_estimate=SHORT,
        name="image_blocks",
        **grid,
    )(images, coverage, offsets, weight, mask, psf_rows, psf_cols, *ends, *([scene] * packs))


def column_tables(taps, start):
    pair = toeplitz(taps, start, LANES, SPAN)
    here, past = pair[:, :LANES], pair[:, LANES:]
    none = jnp.zeros_like(here)
    main = jnp.concatenate(
        [jnp.concatenate([here, none], axis=1), jnp.concatenate([past, here], axis=1)], axis=0
    )
    rest = jnp.concatenate(
        [jnp.concatenate([past, none], axis=1), jnp.concatenate([none, past], axis=1)], axis=0
    )
    return main, rest, here, past


def column_pass(sz, source, tables, tail):
    main, rest, here, past = tables
    tiles = []
    for b in range(0, sz.width, SPAN):
        out = dot(source[:, b : b + SPAN], main)
        tiles += [out[:, :LANES], out[:, LANES:]]
    ends = list(range(SPAN, sz.wide, SPAN))
    if len(ends) == 2:
        joined = jnp.concatenate([source[:, at : at + LANES] for at in ends], axis=1)
        out = dot(joined, rest)
        parts = [out[:, :LANES], out[:, LANES:]]
    else:
        parts = [dot(source[:, at : at + LANES], past) for at in ends]
    for at, part in zip(ends, parts):
        tiles[at // LANES - 1] += part
    if tail:
        tiles.append(dot(source[:, sz.width : sz.wide], here))
    return tiles


def model_kernel(
    sz, batch, coverage_ref, offsets_ref, weight_ref,
    wide_ref, good_ref, psf_rows_ref, psf_cols_ref, *more,
):
    *extra, out_ref, scene, lifted, residual, pulled, row_lines, col_lines = more
    step = pl.program_id(0)
    place = lax.axis_index("epoch")
    start = place * sz.rows
    column = lax.axis_index("sky") * sz.width

    @pl.when(step == 0)
    def _():
        load_taps(psf_rows_ref, row_lines, sz.epochs, sz.taps)
        load_taps(psf_cols_ref, col_lines, sz.epochs, sz.taps)
        scene[RIM : RIM + sz.rows] = wide_ref[...]
        if sz.blocks != 4:
            head_ref, foot_ref, base_ref = extra
            scene[0:RIM] = head_ref[...]
            scene[RIM + sz.rows :] = foot_ref[...]
            out_ref[...] = base_ref[...]
        else:
            own_ref, two_ref, near_ref, far_ref = extra
            near, far = unpack_rim(sz, near_ref, sz.rows), unpack_rim(sz, far_ref, 0)
            none = jnp.zeros_like(near)
            outer = (place == 0) | (place == 3)
            odd = place % 2 == 1
            scene[0:RIM] = jnp.where(odd, near, jnp.where(outer, none, far))
            scene[RIM + sz.rows :] = jnp.where(odd, jnp.where(outer, none, far), near)
            fix = unpack_part(sz, far_ref, RIM + HALO)
            for b in range(0, sz.width, LANES):
                cols = slice(b, b + LANES)
                base = own_ref[:, cols].astype(F32) + two_ref[:, cols].astype(F32)
                base += near_ref[: sz.rows, cols].astype(F32)
                for at, side in ((0, 0), (LANES, sz.width - LANES)):
                    if b == side:
                        base += fix[:, at : at + LANES]
                out_ref[:, cols] = base

    epochs = [step * batch + n for n in range(batch)]
    edge = sz.rows + HALO
    for n, epoch in enumerate(epochs):
        row_in = toeplitz(row_of(row_lines[0], epoch), -4 - offsets_ref[0, epoch], STEP, SPAN)
        for s, count in spans(sz.rows + RIM):
            lifted[n, s : s + count] = dot(
                row_in[:count, : count + RIM], scene[s : s + count + RIM]
            ).astype(BF16)
    for n, epoch in enumerate(epochs):
        good = row_of(good_ref[...], epoch) * (2.0 * weight_ref[epoch])
        lane = iota((1, sz.wide), 1)
        factors = []
        for row_tile in (tile_of(start - HALO), tile_of(start), tile_of(start + sz.rows)):
            left, here, right = (
                cover_at(coverage_ref, epoch, row_tile, tile_of(c))
                for c in (column - HALO, column, column + sz.width)
            )
            factors.append(
                good * jnp.where(lane < HALO, left, jnp.where(lane < HALO + sz.width, here, right))
            )
        tables = column_tables(row_of(col_lines[1], epoch), 28 + offsets_ref[1, epoch])
        for k, modeled in enumerate(column_pass(sz, lifted[n], tables, True)):
            b = k * LANES
            head, mid, foot = (f[:, b : b + LANES] for f in factors)
            residual[n, 0:HALO, b : b + LANES] = (modeled[0:HALO] * head).astype(BF16)
            residual[n, HALO:edge, b : b + LANES] = (modeled[HALO:edge] * mid).astype(BF16)
            residual[n, edge:, b : b + LANES] = (modeled[edge:] * foot).astype(BF16)
    for n, epoch in enumerate(epochs):
        tables = column_tables(row_of(col_lines[0], epoch), 28 - offsets_ref[1, epoch])
        for k, tile in enumerate(column_pass(sz, residual[n], tables, False)):
            pulled[n, :, k * LANES : (k + 1) * LANES] = tile.astype(BF16)
    row_outs = [
        toeplitz(row_of(row_lines[1], epoch), offsets_ref[0, epoch] - 4, STEP, SPAN)
        for epoch in epochs
    ]
    for s, count in spans(sz.rows):
        total = out_ref[s : s + count]
        for n in range(batch):
            total += dot(row_outs[n][:count, : count + RIM], pulled[n, s : s + count + RIM])
        out_ref[s : s + count] = total


def model_term(sz, coverage, offsets, weight, wide, good, psf_rows, psf_cols, *extra):
    high = sz.rows + RIM
    batch = 4 if sz.epochs % 4 == 0 else 1
    return pl.pallas_call(
        functools.partial(model_kernel, sz, batch),
        grid=(sz.epochs // batch,),
        out_shape=jax.ShapeDtypeStruct((sz.rows, sz.width), F32),
        in_specs=[SMEM] * 3 + [VMEM] * (4 + len(extra)),
        out_specs=VMEM,
        scratch_shapes=[
            pltpu.VMEM((sz.rows + 2 * RIM, sz.wide), BF16),
            pltpu.VMEM((batch, high, sz.wide), BF16),
            pltpu.VMEM((batch, high, sz.wide), BF16),
            pltpu.VMEM((batch, high, sz.width), BF16),
            pltpu.VMEM((2, sz.tap_rows, LANES), F32),
            pltpu.VMEM((2, sz.tap_rows, LANES), F32),
        ],
        compiler_params=PARAMS,
        cost_estimate=SHORT,
        name="model_term",
    )(coverage, offsets, weight, wide, good, psf_rows, psf_cols, *extra)


def spread_kernel(sz, part_ref, model_ref, out_ref):
    part = unpack_part(sz, part_ref, 0)
    for at, cols in ((0, slice(0, LANES)), (LANES, slice(sz.width - LANES, sz.width))):
        out_ref[:, cols] = model_ref[:, cols] + part[:, at : at + LANES]


def spread(sz, part, model):
    return pl.pallas_call(
        functools.partial(spread_kernel, sz),
        out_shape=jax.ShapeDtypeStruct(model.shape, F32),
        in_specs=[VMEM, VMEM],
        out_specs=VMEM,
        input_output_aliases={1: 0},
        compiler_params=PARAMS,
        cost_estimate=SHORT,
        name="spread",
    )(part, model)


def on_device(sky_scene, images, psf_rows, psf_cols, offsets, epoch_weight, column_mask, coverage):
    sz = Sizes(images, sky_scene, psf_rows)
    peers = lax.axis_size("sky")
    depth = lax.axis_size("epoch")
    scalars = (jnp.transpose(coverage, (1, 2, 0)), offsets.T, epoch_weight)
    profiles = (psf_rows, psf_cols)

    def pairs(start, count):
        return [p for i in range(start, count - 1, 2) for p in ((i, i + 1), (i + 1, i))]

    def blocks(slots, shifts, *ends, scene=None):
        return image_blocks(
            sz, slots, scalars[0], shifts, epoch_weight, images, column_mask, *profiles, *ends,
            scene=scene,
        )

    if depth == 4:
        one, two, first, second = blocks((0, 1), scalars[1], scene=sky_scene)
        got_one = lax.ppermute(one, "epoch", [(0, 1), (3, 2)])
        got_two = lax.ppermute(two, "epoch", pairs(1, depth))
        shifts, one = lax.optimization_barrier((scalars[1], one))
        three, own = blocks((2, 3), shifts)
        first = lax.ppermute(first, "sky", pairs(0, peers))
        second = lax.ppermute(second, "sky", pairs(1, peers))
        near, far, passed, rim = early(
            sz, *scalars, sky_scene, first, second, *profiles, one, three
        )
        got_near = lax.ppermute(near, "epoch", pairs(0, depth))
        got_far = lax.ppermute(far, "epoch", pairs(1, depth))
        passed += jnp.pad(got_one, ((0, HALO), (0, 0)))
        passed, got_far, got_two, rim = lax.optimization_barrier((passed, got_far, got_two, rim))
        got_passed = lax.ppermute(passed, "epoch", [(1, 3), (2, 0)])
        wide, good, fix, two, own = finish(
            sz, scalars[1], sky_scene, column_mask, first, second, psf_cols, rim, two, own
        )
        got_fix = lax.ppermute(fix, "epoch", [(0, 3), (3, 0)])
        got_last = lax.ppermute(two, "epoch", [(0, 2), (3, 1)])
        model = model_term(sz, *scalars, wide, good, *profiles, own, got_two, got_near, got_far)
        model = spread(sz, got_fix, model)
        return model + (got_passed[: sz.rows].astype(F32) + got_last.astype(F32))

    first, second = edges(sz, images, sky_scene, column_mask)
    first = lax.ppermute(first, "sky", pairs(0, peers))
    second = lax.ppermute(second, "sky", pairs(1, peers))
    downward = [(i, i + 1) for i in range(depth - 1)]
    upward = [(i + 1, i) for i in range(depth - 1)]
    wide, good = finish(sz, scalars[1], sky_scene, column_mask, first, second)
    head = lax.ppermute(wide[-RIM:], "epoch", downward)
    foot = lax.ppermute(wide[:RIM], "epoch", upward)
    terms = blocks(None, scalars[1], first, second).astype(F32)
    base = lax.psum_scatter(terms, "epoch", scatter_dimension=0, tiled=True)
    return model_term(sz, *scalars, wide, good, *profiles, head, foot, base)


def solution(mesh):
    return jax.shard_map(
        on_device,
        mesh=mesh,
        in_specs=(
            P(("field", "epoch"), "sky"),
            P(("field", "epoch"), None, "sky"),
            P("field", None),
            P("field", None),
            P("field", None),
            P("field"),
            P("field", "sky"),
            P("field", None, None),
        ),
        out_specs=P(("field", "epoch"), "sky"),
        check_vma=False,
    )
```

time: 57.7 us -> 55.3 us (0.958)
  starting transfers between devices: 12.3 us -> 23.2 us
  Pallas kernels: 28 us -> 22.2 us
  waiting for transfers between devices: 11.8 us -> 7.79 us
  local copies, waits for them, and re-layouts: 3.52 us -> 0.04 us
    ppermute x3 -> x6, starting transfers between devices: 10.4 us -> 21.7 us  [the longest x1 7.26 us: on_device(): got_last = lax.ppermute(two, 'epoch', [(0, 2), (3, 1)])]
    pallas_call x5 -> x6, Pallas kernels: 28 us -> 22.2 us  [the longest x2 9.21 us: image_blocks(): pl.pallas_call(functools.partial(image_kernel, sz, slots, len(ends), pack...]
    ppermute x3 -> x6, waiting for transfers between devices: 11.8 us -> 7.78 us  [the longest x1 4.11 us: on_device(): got_near = lax.ppermute(near, 'epoch', pairs(0, depth))]
    unnamed x24 -> x20, local copies, waits for them, and re-layouts: 3.52 us -> 0.04 us
    add x1 -> x2, other arithmetic: 1.18 us -> 1.31 us  [the longest x1 1.18 us: on_device(): return model + (got_passed[:sz.rows].astype(F32) + got_last.astype(F32))]
  transfers between devices with their start and end apart: 6 -> 9, of which waited for: 1 -> 2; matrix products, arithmetic and copies ran while one was open for 0% -> 0% of each run, Pallas kernels for 36% -> 29%
where the time goes in v3:
time: 55.3 us; the launch traced here: 54.8 us
  starting transfers between devices  23.2 us (42%)
  Pallas kernels  22.2 us (40%)
  waiting for transfers between devices  7.79 us (14%)
  other arithmetic  1.31 us (2%)
    pallas_call x2, Pallas kernels, image_blocks(): pl.pallas_call(functools.partial(image_kernel, sz, slots, len(ends), pack...  9.21 us
    pallas_call x1, Pallas kernels, model_term(): pl.pallas_call(functools.partial(model_kernel, sz, batch), grid=(sz.epoch...  8.57 us
    ppermute x1, starting transfers between devices, on_device(): got_last = lax.ppermute(two, 'epoch', [(0, 2), (3, 1)])  7.26 us
    ppermute x1, starting transfers between devices, on_device(): got_one = lax.ppermute(one, 'epoch', [(0, 1), (3, 2)])  4.98 us
    ppermute x1, waiting for transfers between devices, on_device(): got_near = lax.ppermute(near, 'epoch', pairs(0, depth))  4.11 us
    ppermute x1, starting transfers between devices, on_device(): got_near = lax.ppermute(near, 'epoch', pairs(0, depth))  3.91 us
    ppermute x1, waiting for transfers between devices, on_device(): got_passed = lax.ppermute(passed, 'epoch', [(1, 3), (2, 0)])  3.66 us
    ppermute x1, starting transfers between devices, on_device(): got_fix = lax.ppermute(fix, 'epoch', [(0, 3), (3, 0)])  3.43 us
  transfers between devices with their start and end apart: 9, of which 2 were waited for; matrix products, arithmetic and copies ran while one was open for 0% of the time, Pallas kernels for 29%

profile of v3, /device:TPU:0, one launch (start us, length us, event | category | flops | bytes accessed | tf_op | source)
XLA Modules:
  0.0 54.8 jit_solution(10425800832719312870)
XLA Ops:
  0.0 6.1 %image_blocks.2 = (bf16[512,512]{1,0:T(8,128)(2,1)}, bf16[512,512]{1,0:T(8,128)(2,1)}, bf16[784,128]{1,0:T(8,128)(2,1)}, bf16[784,128]{1,0:T(8,128)(2,1)}) custom-call(bf16[2,2048,512]{2,1,0:T(8,128)(2,1)} %images_ref.3, s32[4,4,8]{2,1,0:T(4,128)} %bitcast.2, s32[2,8]{1,0:T(2,128)} %bitcast.6, f32[8]{0:T(128)} %weight_ref.3, s32[8,512]{1,0:T(8,128)} %mask_ref.1, ...), custom_call_target="tpu_custom_call" | custom-call | flops 1000 | bytes 1000 | tf_op jit(solution)/shard_map/image_blocks/pallas_call | solution.py:595
  6.2 5.0 %collective-permute-start.2 = (bf16[512,512]{1,0:T(8,128)(2,1)}, bf16[512,512]{1,0:T(8,128)(2,1)S(1)}, u32[]{:S(2)}, u32[]{:S(2)}) collective-permute-start(bf16[512,512]{1,0:T(8,128)(2,1)} %get-tuple-element.29.one_ref), channel_id=1, source_target_pairs={{0,4},{12,8},{1,5},{13,9},{2,6},{14,10},{3,7},{15,11},{16,20},{28,... | collective-permute-start | bytes 1572872 | tf_op jit(solution)/shard_map/ppermute | solution.py:797
  11.2 0.7 %collective-permute-start.4 = (bf16[512,512]{1,0:T(8,128)(2,1)}, bf16[512,512]{1,0:T(8,128)(2,1)S(1)}, u32[]{:S(2)}, u32[]{:S(2)}) collective-permute-start(bf16[512,512]{1,0:T(8,128)(2,1)} %get-tuple-element.34.more_2_), channel_id=1, source_target_pairs={{4,8},{8,4},{5,9},{9,5},{6,10},{10,6},{7,11},{11,7},{20,24},{24,20... | collective-permute-start | bytes 1572872 | tf_op jit(solution)/shard_map/ppermute | solution.py:798
  11.9 0.1 collective-permute-start
  11.9 0.0 copy-start.1
  11.9 0.0 copy-start.3
  12.0 0.8 %collective-permute-start.1 = (bf16[784,128]{1,0:T(8,128)(2,1)}, bf16[784,128]{1,0:T(8,128)(2,1)S(1)}, u32[]{:S(2)}, u32[]{:S(2)}) collective-permute-start(bf16[784,128]{1,0:T(8,128)(2,1)} %get-tuple-element.27), channel_id=1, source_target_pairs={{1,2},{2,1},{5,6},{6,5},{9,10},{10,9},{13,14},{14,13},{17,18},{18,... | collective-permute-start | bytes 602120 | tf_op jit(solution)/shard_map/ppermute | solution.py:802
  12.8 0.0 copy-done
  12.8 0.0 copy-done.4
  12.8 0.0 copy-done.5
  12.8 0.0 copy-done.6
  12.8 3.1 %image_blocks.3 = (bf16[512,512]{1,0:T(8,128)(2,1)S(1)}, bf16[512,512]{1,0:T(8,128)(2,1)S(1)}) custom-call(bf16[2,2048,512]{2,1,0:T(8,128)(2,1)S(1)} %copy-done, s32[4,4,8]{2,1,0:T(4,128)S(1)} %bitcast.3, s32[2,8]{1,0:T(2,128)S(1)} %bitcast.7, f32[8]{0:T(128)S(1)} %copy-done.9, s32[8,512]{1,0:T(8,128)S(1)} %copy-done.4, bf16[8,25]{1,0:T(8,128)(2,1)S(1)} %copy-done.7, ...), custom_call_target="tpu_custom_call" | custom-call | flops 1000 | bytes 1000 | tf_op jit(solution)/shard_map/image_blocks/pallas_call | solution.py:595
  15.9 0.0 collective-permute-done.first_ref
  16.0 0.0 collective-permute-done.1.second_ref
  16.0 2.0 %early.1 = (bf16[560,512]{1,0:T(8,128)(2,1)S(1)}, bf16[80,512]{1,0:T(8,128)(2,1)S(1)}, bf16[528,512]{1,0:T(8,128)(2,1)S(1)}, bf16[2,256,256]{2,1,0:T(8,128)(2,1)S(1)}) custom-call(s32[4,4,8]{2,1,0:T(4,128)S(1)} %bitcast.4, s32[2,8]{1,0:T(2,128)S(1)} %bitcast.8, f32[8]{0:T(128)S(1)} %copy-done.9, bf16[512,512]{1,0:T(8,128)(2,1)S(1)} %copy-done.1, ...), custom_call_target="tpu_custom_call" | custom-call | flops 1000 | bytes 1000 | tf_op jit(solution)/shard_map/early/pallas_call | solution.py:401
  18.0 0.8 %collective-permute-start.3 = (bf16[80,512]{1,0:T(8,128)(2,1)S(1)}, bf16[80,512]{1,0:T(8,128)(2,1)S(1)}, u32[]{:S(2)}, u32[]{:S(2)}) collective-permute-start(bf16[80,512]{1,0:T(8,128)(2,1)S(1)} %get-tuple-element.33), channel_id=1, source_target_pairs={{4,8},{8,4},{5,9},{9,5},{6,10},{10,6},{7,11},{11,7},{20,24},{24,20... | collective-permute-start | bytes 245768 | tf_op jit(solution)/shard_map/ppermute | solution.py:807
  18.8 3.9 %collective-permute-start.6 = (bf16[560,512]{1,0:T(8,128)(2,1)S(1)}, bf16[560,512]{1,0:T(8,128)(2,1)S(1)}, u32[]{:S(2)}, u32[]{:S(2)}) collective-permute-start(bf16[560,512]{1,0:T(8,128)(2,1)S(1)} %get-tuple-element.43), channel_id=1, source_target_pairs={{0,4},{4,0},{8,12},{12,8},{1,5},{5,1},{9,13},{13,9},{2,6},{6,2},{1... | collective-permute-start | bytes 1720328 | tf_op jit(solution)/shard_map/ppermute | solution.py:806
  22.7 0.0 collective-permute-done.2
  22.7 0.1 pad_add_fusion
  22.9 0.0 collective-permute-done.3.more_3_
  22.9 0.0 collective-permute-done.4.more_1_
  22.9 1.3 %collective-permute-start.7 = (bf16[528,512]{1,0:T(8,128)(2,1)S(1)}, bf16[528,512]{1,0:T(8,128)(2,1)S(1)}, u32[]{:S(2)}, u32[]{:S(2)}) collective-permute-start(bf16[528,512]{1,0:T(8,128)(2,1)S(1)} %pad_add_fusion), channel_id=1, source_target_pairs={{4,12},{8,0},{5,13},{9,1},{6,14},{10,2},{7,15},{11,3},{20,28},{24,... | collective-permute-start | bytes 1622024 | tf_op jit(solution)/shard_map/ppermute | solution.py:810
  24.2 2.1 %finish.1 = (bf16[512,640]{1,0:T(8,128)(2,1)S(1)}, f32[16,640]{1,0:T(8,128)S(1)}, bf16[32,512]{1,0:T(8,128)(2,1)S(1)}, bf16[512,512]{1,0:T(8,128)(2,1)S(1)}, bf16[512,512]{1,0:T(8,128)(2,1)S(1)}) custom-call(s32[2,8]{1,0:T(2,128)S(1)} %bitcast.9, bf16[512,512]{1,0:T(8,128)(2,1)S(1)} %copy-done.1, s32[8,512]{1,0:T(8,128)S(1)} %copy-done.4, ...), custom_call_target="tpu_custom_call" | custom-call | flops 1000 | bytes 1000 | tf_op jit(solution)/shard_map/finish/pallas_call | solution.py:444
  26.3 7.3 %collective-permute-start.8 = (bf16[512,512]{1,0:T(8,128)(2,1)S(1)}, bf16[512,512]{1,0:T(8,128)(2,1)S(1)}, u32[]{:S(2)}, u32[]{:S(2)}) collective-permute-start(bf16[512,512]{1,0:T(8,128)(2,1)S(1)} %get-tuple-element.46), channel_id=1, source_target_pairs={{0,8},{12,4},{1,9},{13,5},{2,10},{14,6},{3,11},{15,7},{16,24},{28,... | collective-permute-start | bytes 1572872 | tf_op jit(solution)/shard_map/ppermute | solution.py:815
  33.6 3.4 %collective-permute-start.5 = (bf16[32,512]{1,0:T(8,128)(2,1)S(1)}, bf16[32,512]{1,0:T(8,128)(2,1)S(1)}, u32[]{:S(2)}, u32[]{:S(2)}) collective-permute-start(bf16[32,512]{1,0:T(8,128)(2,1)S(1)} %get-tuple-element.38), channel_id=1, source_target_pairs={{0,12},{12,0},{1,13},{13,1},{2,14},{14,2},{3,15},{15,3},{16,28},{2... | collective-permute-start | bytes 98312 | tf_op jit(solution)/shard_map/ppermute | solution.py:814
  37.0 4.1 %collective-permute-done.6.more_2_ = bf16[560,512]{1,0:T(8,128)(2,1)S(1)} collective-permute-done((bf16[560,512]{1,0:T(8,128)(2,1)S(1)}, bf16[560,512]{1,0:T(8,128)(2,1)S(1)}, u32[]{:S(2)}, u32[]{:S(2)}) %collective-permute-start.6) | collective-permute-done | bytes 573472 | tf_op jit(solution)/shard_map/ppermute | solution.py:806
  41.1 8.6 %model_term.1.model_ref = f32[512,512]{1,0:T(8,128)S(1)} custom-call(s32[4,4,8]{2,1,0:T(4,128)S(1)} %bitcast.5, s32[2,8]{1,0:T(2,128)S(1)} %bitcast.10, f32[8]{0:T(128)S(1)} %copy-done.9, bf16[512,640]{1,0:T(8,128)(2,1)S(1)} %get-tuple-element.39.wide_ref, f32[16,640]{1,0:T(8,128)S(1)} %get-tuple-element.40.good_ref, bf16[8,25]{1,0:T(8,128)(2,1)S(1)} %copy-done.7, ...), custom_call_target="tpu_custom_call" | custom-call | flops 1000 | bytes 1000 | tf_op jit(solution)/shard_map/model_term/pallas_call | solution.py:740
  49.7 0.0 collective-permute-done.5.part_ref
  49.7 0.2 spread.1
  50.0 0.0 collective-permute-done.8
  50.0 3.7 %collective-permute-done.7 = bf16[528,512]{1,0:T(8,128)(2,1)S(1)} collective-permute-done((bf16[528,512]{1,0:T(8,128)(2,1)S(1)}, bf16[528,512]{1,0:T(8,128)(2,1)S(1)}, u32[]{:S(2)}, u32[]{:S(2)}) %collective-permute-start.7) | collective-permute-done | bytes 540704 | tf_op jit(solution)/shard_map/ppermute | solution.py:810
  53.6 1.2 %add_add_fusion = f32[512,512]{1,0:T(8,128)} fusion(f32[512,512]{1,0:T(8,128)S(1)} %spread.1, bf16[512,512]{1,0:T(8,128)(2,1)S(1)} %collective-permute-done.8, bf16[528,512]{1,0:T(8,128)(2,1)S(1)} %collective-permute-done.7), kind=kLoop, calls=%fused_computation | loop fusion | flops 1048576 | bytes 3145728 | tf_op jit(solution)/shard_map/add | solution.py:818
  (14 shorter events, 0.0 us)
Async XLA Ops:
  0.0 12.8 %copy-start = (bf16[2,2048,512]{2,1,0:T(8,128)(2,1)S(1)}, bf16[2,2048,512]{2,1,0:T(8,128)(2,1)}, u32[]{:S(2)}) copy-start(bf16[2,2048,512]{2,1,0:T(8,128)(2,1)} %images_ref.3) | copy-start | bytes 12582916
  0.0 12.8 %copy-start.4 = (s32[8,512]{1,0:T(8,128)S(1)}, s32[8,512]{1,0:T(8,128)}, u32[]{:S(2)}) copy-start(s32[8,512]{1,0:T(8,128)} %mask_ref.1) | copy-start | bytes 49156
  0.0 12.8 %copy-start.5 = (s32[8,4,4]{0,2,1:T(4,128)S(1)}, s32[8,4,4]{0,2,1:T(4,128)}, u32[]{:S(2)}) copy-start(s32[8,4,4]{0,2,1:T(4,128)} %param.15) | copy-start | bytes 1540
  0.0 12.8 %copy-start.6 = (bf16[8,25]{1,0:T(8,128)(2,1)S(1)}, bf16[8,25]{1,0:T(8,128)(2,1)}, u32[]{:S(2)}) copy-start(bf16[8,25]{1,0:T(8,128)(2,1)} %psf_cols_ref.3) | copy-start | bytes 1204
  0.0 12.8 %copy-start.7 = (bf16[8,25]{1,0:T(8,128)(2,1)S(1)}, bf16[8,25]{1,0:T(8,128)(2,1)}, u32[]{:S(2)}) copy-start(bf16[8,25]{1,0:T(8,128)(2,1)} %psf_rows_ref.3) | copy-start | bytes 1204
  0.0 12.8 %copy-start.8 = (s32[8,2]{0,1:T(2,128)S(1)}, s32[8,2]{0,1:T(2,128)}, u32[]{:S(2)}) copy-start(s32[8,2]{0,1:T(2,128)} %param.12) | copy-start | bytes 196
  0.0 12.8 %copy-start.9 = (f32[8]{0:T(128)S(1)}, f32[8]{0:T(128)}, u32[]{:S(2)}) copy-start(f32[8]{0:T(128)} %weight_ref.3) | copy-start | bytes 100
  6.2 16.6 %collective-permute-start.2 = (bf16[512,512]{1,0:T(8,128)(2,1)}, bf16[512,512]{1,0:T(8,128)(2,1)S(1)}, u32[]{:S(2)}, u32[]{:S(2)}) collective-permute-start(bf16[512,512]{1,0:T(8,128)(2,1)} %get-tuple-element.29.one_ref), channel_id=1, source_target_pairs={{0,4},{12,8},{1,5},{13,9},{2,6},{14,10},{3,7},{15,11},{16,20},{28,... | collective-permute-start | bytes 1572872 | tf_op jit(solution)/shard_map/ppermute | solution.py:797
  11.2 11.7 %collective-permute-start.4 = (bf16[512,512]{1,0:T(8,128)(2,1)}, bf16[512,512]{1,0:T(8,128)(2,1)S(1)}, u32[]{:S(2)}, u32[]{:S(2)}) collective-permute-start(bf16[512,512]{1,0:T(8,128)(2,1)} %get-tuple-element.34.more_2_), channel_id=1, source_target_pairs={{4,8},{8,4},{5,9},{9,5},{6,10},{10,6},{7,11},{11,7},{20,24},{24,20... | collective-permute-start | bytes 1572872 | tf_op jit(solution)/shard_map/ppermute | solution.py:798
  11.9 4.1 %collective-permute-start = (bf16[784,128]{1,0:T(8,128)(2,1)}, bf16[784,128]{1,0:T(8,128)(2,1)S(1)}, u32[]{:S(2)}, u32[]{:S(2)}) collective-permute-start(bf16[784,128]{1,0:T(8,128)(2,1)} %get-tuple-element.26), channel_id=1, source_target_pairs={{0,1},{1,0},{2,3},{3,2},{4,5},{5,4},{6,7},{7,6},{8,9},{9,8},{10,11... | collective-permute-start | bytes 602120 | tf_op jit(solution)/shard_map/ppermute | solution.py:801
  11.9 4.0 %copy-start.1 = (bf16[512,512]{1,0:T(8,128)(2,1)S(1)}, bf16[512,512]{1,0:T(8,128)(2,1)}, u32[]{:S(2)}) copy-start(bf16[512,512]{1,0:T(8,128)(2,1)} %scene_ref.3) | copy-start | bytes 1572868
  11.9 4.0 %copy-start.3 = (bf16[512,512]{1,0:T(8,128)(2,1)S(1)}, bf16[512,512]{1,0:T(8,128)(2,1)}, u32[]{:S(2)}) copy-start(bf16[512,512]{1,0:T(8,128)(2,1)} %get-tuple-element.29.one_ref) | copy-start | bytes 1572868
  12.0 4.0 %collective-permute-start.1 = (bf16[784,128]{1,0:T(8,128)(2,1)}, bf16[784,128]{1,0:T(8,128)(2,1)S(1)}, u32[]{:S(2)}, u32[]{:S(2)}) collective-permute-start(bf16[784,128]{1,0:T(8,128)(2,1)} %get-tuple-element.27), channel_id=1, source_target_pairs={{1,2},{2,1},{5,6},{6,5},{9,10},{10,9},{13,14},{14,13},{17,18},{18,... | collective-permute-start | bytes 602120 | tf_op jit(solution)/shard_map/ppermute | solution.py:802
  18.0 6.2 %copy-start.2 = (bf16[512,512]{1,0:T(8,128)(2,1)S(1)}, bf16[512,512]{1,0:T(8,128)(2,1)}, u32[]{:S(2)}) copy-start(bf16[512,512]{1,0:T(8,128)(2,1)} %get-tuple-element.34.more_2_) | copy-start | bytes 1572868
  18.0 4.9 %collective-permute-start.3 = (bf16[80,512]{1,0:T(8,128)(2,1)S(1)}, bf16[80,512]{1,0:T(8,128)(2,1)S(1)}, u32[]{:S(2)}, u32[]{:S(2)}) collective-permute-start(bf16[80,512]{1,0:T(8,128)(2,1)S(1)} %get-tuple-element.33), channel_id=1, source_target_pairs={{4,8},{8,4},{5,9},{9,5},{6,10},{10,6},{7,11},{11,7},{20,24},{24,20... | collective-permute-start | bytes 245768 | tf_op jit(solution)/shard_map/ppermute | solution.py:807
  18.8 22.3 %collective-permute-start.6 = (bf16[560,512]{1,0:T(8,128)(2,1)S(1)}, bf16[560,512]{1,0:T(8,128)(2,1)S(1)}, u32[]{:S(2)}, u32[]{:S(2)}) collective-permute-start(bf16[560,512]{1,0:T(8,128)(2,1)S(1)} %get-tuple-element.43), channel_id=1, source_target_pairs={{0,4},{4,0},{8,12},{12,8},{1,5},{5,1},{9,13},{13,9},{2,6},{6,2},{1... | collective-permute-start | bytes 1720328 | tf_op jit(solution)/shard_map/ppermute | solution.py:806
  22.9 30.8 %collective-permute-start.7 = (bf16[528,512]{1,0:T(8,128)(2,1)S(1)}, bf16[528,512]{1,0:T(8,128)(2,1)S(1)}, u32[]{:S(2)}, u32[]{:S(2)}) collective-permute-start(bf16[528,512]{1,0:T(8,128)(2,1)S(1)} %pad_add_fusion), channel_id=1, source_target_pairs={{4,12},{8,0},{5,13},{9,1},{6,14},{10,2},{7,15},{11,3},{20,28},{24,... | collective-permute-start | bytes 1622024 | tf_op jit(solution)/shard_map/ppermute | solution.py:810
  26.3 23.6 %collective-permute-start.8 = (bf16[512,512]{1,0:T(8,128)(2,1)S(1)}, bf16[512,512]{1,0:T(8,128)(2,1)S(1)}, u32[]{:S(2)}, u32[]{:S(2)}) collective-permute-start(bf16[512,512]{1,0:T(8,128)(2,1)S(1)} %get-tuple-element.46), channel_id=1, source_target_pairs={{0,8},{12,4},{1,9},{13,5},{2,10},{14,6},{3,11},{15,7},{16,24},{28,... | collective-permute-start | bytes 1572872 | tf_op jit(solution)/shard_map/ppermute | solution.py:815
  33.6 16.1 %collective-permute-start.5 = (bf16[32,512]{1,0:T(8,128)(2,1)S(1)}, bf16[32,512]{1,0:T(8,128)(2,1)S(1)}, u32[]{:S(2)}, u32[]{:S(2)}) collective-permute-start(bf16[32,512]{1,0:T(8,128)(2,1)S(1)} %get-tuple-element.38), channel_id=1, source_target_pairs={{0,12},{12,0},{1,13},{13,1},{2,14},{14,2},{3,15},{15,3},{16,28},{2... | collective-permute-start | bytes 98312 | tf_op jit(solution)/shard_map/ppermute | solution.py:814

commit v4 on v3

--- a/solution.py
+++ b/solution.py
@@ -344,14 +344,11 @@
     return jnp.concatenate(parts, axis=0)
 
 
-def complete(sz, block, part):
-    left, right = slice(0, LANES), slice(sz.width - LANES, sz.width)
-    mid = slice(LANES, sz.width - LANES)
-    return (
-        (left, (block[:, left].astype(F32) + part[:, :LANES]).astype(BF16)),
-        (mid, block[:, mid]),
-        (right, (block[:, right].astype(F32) + part[:, LANES:]).astype(BF16)),
-    )
+def complete(sz, out, part):
+    rows = slice(0, sz.rows)
+    for at, cols in ((0, slice(0, LANES)), (LANES, slice(sz.width - LANES, sz.width))):
+        value = out[rows, cols].astype(F32) + part[:, at : at + LANES]
+        out[rows, cols] = value.astype(BF16)
 
 
 def rim_parts_of(sz, slots, place, offsets_ref, col_lines, rim_ref):
@@ -369,10 +366,9 @@
     return parts
 
 
-def early_kernel(
+def notes_kernel(
     sz, coverage_ref, offsets_ref, weight_ref, scene_ref, first_ref, second_ref,
-    psf_rows_ref, psf_cols_ref, one_ref, three_ref, near_out, far_out, pass_out, rim_ref,
-    row_lines, col_lines,
+    psf_rows_ref, psf_cols_ref, far_out, rim_ref, part_out, row_lines, col_lines,
 ):
     place = lax.axis_index("epoch")
     outer = (place == 0) | (place == 3)
@@ -384,51 +380,101 @@
             sz, epoch, e, coverage_ref, row_of(row_lines[1], epoch), offsets_ref[0, epoch],
             -2.0 * weight_ref[epoch], first_ref, second_ref,
         )
-    parts = rim_parts_of(sz, (0, 2, 1), place, offsets_ref, col_lines, rim_ref)
+    parts = rim_parts_of(sz, (0, 1), place, offsets_ref, col_lines, rim_ref)
+    top = widen_rows(sz, scene_ref, first_ref, second_ref, 0, RIM)
+    bottom = widen_rows(sz, scene_ref, first_ref, second_ref, sz.rows - RIM, RIM)
+    pack_rows(sz, far_out, 0, jnp.where(place < 2, bottom, top))
+    pack_part(sz, far_out, RIM + HALO, jnp.where(outer, parts[0], parts[1]))
+    part_out[...] = parts[1].astype(BF16)
+
+
+def notes(sz, coverage, offsets, weight, scene, first, second, psf_rows, psf_cols):
+    return pl.pallas_call(
+        functools.partial(notes_kernel, sz),
+        out_shape=(
+            jax.ShapeDtypeStruct((2 * RIM + HALO, sz.width), BF16),
+            jax.ShapeDtypeStruct((sz.local, SPAN, 2 * LANES), BF16),
+            jax.ShapeDtypeStruct((sz.rows, SPAN), BF16),
+        ),
+        in_specs=[SMEM] * 3 + [VMEM] * 5,
+        out_specs=(VMEM, VMEM, VMEM),
+        scratch_shapes=[pltpu.VMEM((2, sz.tap_rows, LANES), F32)] * 2,
+        compiler_params=PARAMS,
+        cost_estimate=SHORT,
+        name="notes",
+    )(coverage, offsets, weight, scene, first, second, psf_rows, psf_cols)
+
+
+def early_kernel(
+    sz, offsets_ref, scene_ref, first_ref, second_ref, psf_cols_ref, rim_ref, three_ref,
+    near_out, col_lines,
+):
+    place = lax.axis_index("epoch")
+    load_taps(psf_cols_ref, col_lines, sz.epochs, sz.taps)
+    (part,) = rim_parts_of(sz, (2,), place, offsets_ref, col_lines, rim_ref)
     top = widen_rows(sz, scene_ref, first_ref, second_ref, 0, RIM)
     bottom = widen_rows(sz, scene_ref, first_ref, second_ref, sz.rows - RIM, RIM)
     pack_rows(sz, near_out, sz.rows, jnp.where(place % 2 == 0, bottom, top))
-    pack_rows(sz, far_out, 0, jnp.where(place < 2, bottom, top))
-    pack_part(sz, far_out, RIM + HALO, parts[2])
-    first_block, third_block = complete(sz, one_ref, parts[0]), complete(sz, three_ref, parts[1])
-    for (cols, other), (_, mine) in zip(first_block, third_block):
-        near_out[: sz.rows, cols] = jnp.where(outer, mine, other)
-        pass_out[: sz.rows, cols] = mine
-    pass_out[sz.rows :] = jnp.zeros((HALO, sz.width), BF16)
-
-
-def early(sz, coverage, offsets, weight, scene, first, second, psf_rows, psf_cols, one, three):
+    near_out[: sz.rows] = three_ref[...]
+    complete(sz, near_out, part)
+
+
+def early(sz, offsets, scene, first, second, psf_cols, rim, three):
     return pl.pallas_call(
         functools.partial(early_kernel, sz),
-        out_shape=(
-            jax.ShapeDtypeStruct((sz.rows + RIM + HALO, sz.width), BF16),
-            jax.ShapeDtypeStruct((2 * RIM + HALO, sz.width), BF16),
-            jax.ShapeDtypeStruct((sz.rows + HALO, sz.width), BF16),
-            jax.ShapeDtypeStruct((sz.local, SPAN, 2 * LANES), BF16),
-        ),
-        in_specs=[SMEM] * 3 + [VMEM] * 7,
-        out_specs=(VMEM, VMEM, VMEM, VMEM),
-        scratch_shapes=[pltpu.VMEM((2, sz.tap_rows, LANES), F32)] * 2,
+        out_shape=jax.ShapeDtypeStruct((sz.rows + RIM + HALO, sz.width), BF16),
+        in_specs=[SMEM] + [VMEM] * 6,
+        out_specs=VMEM,
+        scratch_shapes=[pltpu.VMEM((2, sz.tap_rows, LANES), F32)],
         compiler_params=PARAMS,
         cost_estimate=SHORT,
         name="early",
-    )(coverage, offsets, weight, scene, first, second, psf_rows, psf_cols, one, three)
+    )(offsets, scene, first, second, psf_cols, rim, three)
+
+
+def merge_kernel(sz, two_ref, near_ref, one_ref, part_ref, out_ref):
+    place = lax.axis_index("epoch")
+    outer = (place == 0) | (place == 3)
+
+    @pl.when(outer)
+    def _():
+        out_ref[...] = two_ref[...]
+        complete(sz, out_ref, part_ref[...].astype(F32))
+
+    @pl.when(jnp.logical_not(outer))
+    def _():
+        total = near_ref[: sz.rows].astype(F32) + one_ref[...].astype(F32)
+        out_ref[...] = total.astype(BF16)
+
+
+def merge(sz, two, near, one, part):
+    return pl.pallas_call(
+        functools.partial(merge_kernel, sz),
+        out_shape=jax.ShapeDtypeStruct((sz.rows, sz.width), BF16),
+        in_specs=[VMEM] * 4,
+        out_specs=VMEM,
+        compiler_params=PARAMS,
+        cost_estimate=SHORT,
+        name="merge",
+    )(two, near, one, part)
 
 
 def finish_kernel(sz, offsets_ref, scene_ref, mask_ref, first_ref, second_ref, *more):
     if sz.blocks != 4:
         widen_kernel(sz, scene_ref, mask_ref, first_ref, second_ref, *more)
         return
-    psf_cols_ref, rim_ref, two_ref, own_ref, wide_ref, good_ref, fix_out = more[:7]
-    two_out, own_out, col_lines = more[7:]
+    psf_cols_ref, rim_ref, own_ref, wide_ref, good_ref, back_out, own_out, col_lines, sem = more
     place = lax.axis_index("epoch")
+    copy = pltpu.make_async_copy(own_ref, own_out, sem)
+    copy.start()
     load_taps(psf_cols_ref, col_lines, sz.epochs, sz.taps)
-    parts = rim_parts_of(sz, (0, 1, 3), place, offsets_ref, col_lines, rim_ref)
+    parts = rim_parts_of(sz, (0, 3), place, offsets_ref, col_lines, rim_ref)
     widen_kernel(sz, scene_ref, mask_ref, first_ref, second_ref, wide_ref, good_ref)
-    pack_part(sz, fix_out, 0, parts[0])
-    for block, out, part in ((two_ref, two_out, parts[1]), (own_ref, own_out, parts[2])):
-        for cols, value in complete(sz, block, part):
-            out[:, cols] = value
+    top, bottom = wide_ref[:RIM], wide_ref[sz.rows - RIM :]
+    pack_rows(sz, back_out, 0, jnp.where(place % 2 == 0, bottom, top))
+    pack_part(sz, back_out, RIM + HALO, parts[0])
+    copy.wait()
+    complete(sz, own_out, parts[1])
 
 
 def finish(sz, offsets, scene, mask, first, second, *more):
@@ -439,12 +485,12 @@
     ]
     scratch = []
     if more:
-        shapes += [jax.ShapeDtypeStruct((RIM, sz.width), BF16), full, full]
-        scratch = [pltpu.VMEM((2, sz.tap_rows, LANES), F32)]
+        shapes += [jax.ShapeDtypeStruct((2 * RIM + HALO, sz.width), BF16), full]
+        scratch = [pltpu.VMEM((2, sz.tap_rows, LANES), F32), pltpu.SemaphoreType.DMA]
     return pl.pallas_call(
         functools.partial(finish_kernel, sz),
         out_shape=tuple(shapes),
-        in_specs=[SMEM] + [VMEM] * (4 + len(more)),
+        in_specs=[SMEM] + [VMEM] * 4 + [VMEM, VMEM, HBM][: len(more)],
         out_specs=tuple([VMEM] * len(shapes)),
         scratch_shapes=scratch,
         compiler_params=PARAMS,
@@ -675,18 +721,23 @@
             scene[RIM + sz.rows :] = foot_ref[...]
             out_ref[...] = base_ref[...]
         else:
-            own_ref, two_ref, near_ref, far_ref = extra
-            near, far = unpack_rim(sz, near_ref, sz.rows), unpack_rim(sz, far_ref, 0)
+            own_ref, one_ref, two_ref, three_ref, back_ref, far_ref = extra
+            outer = (place == 0) | (place == 3)
+            near = jnp.where(
+                outer, unpack_rim(sz, back_ref, 0), unpack_rim(sz, three_ref, sz.rows)
+            )
+            far = unpack_rim(sz, far_ref, 0)
             none = jnp.zeros_like(near)
-            outer = (place == 0) | (place == 3)
             odd = place % 2 == 1
             scene[0:RIM] = jnp.where(odd, near, jnp.where(outer, none, far))
             scene[RIM + sz.rows :] = jnp.where(odd, jnp.where(outer, none, far), near)
-            fix = unpack_part(sz, far_ref, RIM + HALO)
+            rows = slice(RIM + HALO, 2 * RIM + HALO)
+            fix = unpack_part(sz, back_ref[rows], 0) + unpack_part(sz, far_ref[rows], 0)
             for b in range(0, sz.width, LANES):
                 cols = slice(b, b + LANES)
-                base = own_ref[:, cols].astype(F32) + two_ref[:, cols].astype(F32)
-                base += near_ref[: sz.rows, cols].astype(F32)
+                inner = two_ref[:, cols].astype(F32) + three_ref[: sz.rows, cols].astype(F32)
+                base = jnp.where(outer, one_ref[:, cols].astype(F32), inner)
+                base += own_ref[:, cols].astype(F32)
                 for at, side in ((0, 0), (LANES, sz.width - LANES)):
                     if b == side:
                         base += fix[:, at : at + LANES]
@@ -757,25 +808,6 @@
     )(coverage, offsets, weight, wide, good, psf_rows, psf_cols, *extra)
 
 
-def spread_kernel(sz, part_ref, model_ref, out_ref):
-    part = unpack_part(sz, part_ref, 0)
-    for at, cols in ((0, slice(0, LANES)), (LANES, slice(sz.width - LANES, sz.width))):
-        out_ref[:, cols] = model_ref[:, cols] + part[:, at : at + LANES]
-
-
-def spread(sz, part, model):
-    return pl.pallas_call(
-        functools.partial(spread_kernel, sz),
-        out_shape=jax.ShapeDtypeStruct(model.shape, F32),
-        in_specs=[VMEM, VMEM],
-        out_specs=VMEM,
-        input_output_aliases={1: 0},
-        compiler_params=PARAMS,
-        cost_estimate=SHORT,
-        name="spread",
-    )(part, model)
-
-
 def on_device(sky_scene, images, psf_rows, psf_cols, offsets, epoch_weight, column_mask, coverage):
     sz = Sizes(images, sky_scene, psf_rows)
     peers = lax.axis_size("sky")
@@ -794,28 +826,29 @@
 
     if depth == 4:
         one, two, first, second = blocks((0, 1), scalars[1], scene=sky_scene)
-        got_one = lax.ppermute(one, "epoch", [(0, 1), (3, 2)])
+        got_one = lax.ppermute(one, "epoch", pairs(0, depth))
         got_two = lax.ppermute(two, "epoch", pairs(1, depth))
         shifts, one = lax.optimization_barrier((scalars[1], one))
         three, own = blocks((2, 3), shifts)
         first = lax.ppermute(first, "sky", pairs(0, peers))
         second = lax.ppermute(second, "sky", pairs(1, peers))
-        near, far, passed, rim = early(
-            sz, *scalars, sky_scene, first, second, *profiles, one, three
-        )
-        got_near = lax.ppermute(near, "epoch", pairs(0, depth))
-        got_far = lax.ppermute(far, "epoch", pairs(1, depth))
-        passed += jnp.pad(got_one, ((0, HALO), (0, 0)))
+        second, three = lax.optimization_barrier((second, three))
+        far, rim, part = notes(sz, *scalars, sky_scene, first, second, *profiles)
+        near = early(sz, scalars[1], sky_scene, first, second, psf_cols, rim, three)
+        got_three = lax.ppermute(near, "epoch", [(0, 1), (3, 2)])
+        got_far = lax.ppermute(far, "epoch", [(0, 3), (3, 0), (1, 2), (2, 1)])
+        passed = merge(sz, two, near, got_one, part)
         passed, got_far, got_two, rim = lax.optimization_barrier((passed, got_far, got_two, rim))
-        got_passed = lax.ppermute(passed, "epoch", [(1, 3), (2, 0)])
-        wide, good, fix, two, own = finish(
-            sz, scalars[1], sky_scene, column_mask, first, second, psf_cols, rim, two, own
-        )
-        got_fix = lax.ppermute(fix, "epoch", [(0, 3), (3, 0)])
-        got_last = lax.ppermute(two, "epoch", [(0, 2), (3, 1)])
-        model = model_term(sz, *scalars, wide, good, *profiles, own, got_two, got_near, got_far)
-        model = spread(sz, got_fix, model)
-        return model + (got_passed[: sz.rows].astype(F32) + got_last.astype(F32))
+        got_passed = lax.ppermute(passed, "epoch", [(0, 2), (3, 1), (1, 3), (2, 0)])
+        wide, good, back, own = finish(
+            sz, scalars[1], sky_scene, column_mask, first, second, psf_cols, rim, own
+        )
+        got_back = lax.ppermute(back, "epoch", [(1, 0), (2, 3)])
+        model = model_term(
+            sz, *scalars, wide, good, *profiles,
+            own, got_one, got_two, got_three, got_back, got_far,
+        )
+        return model + got_passed.astype(F32)
 
     first, second = edges(sz, images, sky_scene, column_mask)
     first = lax.ppermute(first, "sky", pairs(0, peers))

time: 55.3 us -> 53.5 us (0.967)
  starting transfers between devices: 23.2 us -> 19.7 us
  waiting for transfers between devices: 7.79 us -> 8.95 us
  Pallas kernels: 22.2 us -> 23.3 us
    ppermute x6 -> x5, starting transfers between devices: 21.7 us -> 15.4 us  [the longest x1 4.42 us: on_device(): got_passed = lax.ppermute(passed, 'epoch', [(0, 2), (3, 1), (1, 3), (2, 0)])]
    ppermute x1, starting transfers between devices: 0.07 us -> 2.9 us  [on_device(): first = lax.ppermute(first, 'sky', pairs(0, peers))]
    ppermute x6 -> x5, waiting for transfers between devices: 7.78 us -> 8.94 us  [the longest x1 8.93 us: on_device(): got_back = lax.ppermute(back, 'epoch', [(1, 0), (2, 3)])]
    pallas_call x2 -> x3, Pallas kernels: 2.24 us -> 3.24 us  [the longest x1 1.84 us: notes(): pl.pallas_call(functools.partial(notes_kernel, sz), out_shape=(jax.ShapeD...]
    add x2 -> x1, other arithmetic: 1.31 us -> 1.13 us  [on_device(): return model + got_passed.astype(F32)]
  transfers between devices with their start and end apart: 9 -> 8, of which waited for: 2 -> 1; matrix products, arithmetic and copies ran while one was open for 0% -> 0% of each run, Pallas kernels for 29% -> 32%
where the time goes in v4:
time: 53.5 us; the launch traced here: 53.3 us
  Pallas kernels  23.3 us (44%)
  starting transfers between devices  19.7 us (37%)
  waiting for transfers between devices  8.95 us (17%)
  other arithmetic  1.13 us (2%)
    pallas_call x2, Pallas kernels, image_blocks(): pl.pallas_call(functools.partial(image_kernel, sz, slots, len(ends), pack...  9.27 us
    ppermute x1, waiting for transfers between devices, on_device(): got_back = lax.ppermute(back, 'epoch', [(1, 0), (2, 3)])  8.93 us
    pallas_call x1, Pallas kernels, model_term(): pl.pallas_call(functools.partial(model_kernel, sz, batch), grid=(sz.epoch...  8.73 us
    ppermute x1, starting transfers between devices, on_device(): got_passed = lax.ppermute(passed, 'epoch', [(0, 2), (3, 1), (1, 3), (2, 0)])  4.42 us
    ppermute x1, starting transfers between devices, on_device(): got_three = lax.ppermute(near, 'epoch', [(0, 1), (3, 2)])  3.82 us
    ppermute x1, starting transfers between devices, on_device(): got_one = lax.ppermute(one, 'epoch', pairs(0, depth))  3.13 us
    ppermute x1, starting transfers between devices, on_device(): first = lax.ppermute(first, 'sky', pairs(0, peers))  2.9 us
    ppermute x1, starting transfers between devices, on_device(): got_far = lax.ppermute(far, 'epoch', [(0, 3), (3, 0), (1, 2), (2, 1)])  2.6 us
  transfers between devices with their start and end apart: 8, of which 1 were waited for; matrix products, arithmetic and copies ran while one was open for 0% of the time, Pallas kernels for 32%

profile of v4, /device:TPU:0, one launch (start us, length us, event | category | flops | bytes accessed | tf_op | source)
XLA Modules:
  0.0 53.3 jit_solution(1611428707367826054)
XLA Ops:
  0.0 0.0 copy-start.4
  0.0 0.0 copy-start.6
  0.0 0.0 copy-start.1
  0.0 6.2 %image_blocks.2 = (bf16[512,512]{1,0:T(8,128)(2,1)}, bf16[512,512]{1,0:T(8,128)(2,1)}, bf16[784,128]{1,0:T(8,128)(2,1)}, bf16[784,128]{1,0:T(8,128)(2,1)}) custom-call(bf16[2,2048,512]{2,1,0:T(8,128)(2,1)} %images_ref.3, s32[4,4,8]{2,1,0:T(4,128)} %bitcast.2, s32[2,8]{1,0:T(2,128)} %bitcast.6, f32[8]{0:T(128)} %weight_ref.3, s32[8,512]{1,0:T(8,128)} %mask_ref.1, ...), custom_call_target="tpu_custom_call" | custom-call | flops 1000 | bytes 1000 | tf_op jit(solution)/shard_map/image_blocks/pallas_call | solution.py:641
  6.2 3.1 %collective-permute-start.2 = (bf16[512,512]{1,0:T(8,128)(2,1)}, bf16[512,512]{1,0:T(8,128)(2,1)S(1)}, u32[]{:S(2)}, u32[]{:S(2)}) collective-permute-start(bf16[512,512]{1,0:T(8,128)(2,1)} %get-tuple-element.27), channel_id=1, source_target_pairs={{0,4},{4,0},{8,12},{12,8},{1,5},{5,1},{9,13},{13,9},{2,6},{6,2},{1... | collective-permute-start | bytes 1572872 | tf_op jit(solution)/shard_map/ppermute | solution.py:829
  9.4 0.7 %collective-permute-start.4 = (bf16[512,512]{1,0:T(8,128)(2,1)}, bf16[512,512]{1,0:T(8,128)(2,1)S(1)}, u32[]{:S(2)}, u32[]{:S(2)}) collective-permute-start(bf16[512,512]{1,0:T(8,128)(2,1)} %get-tuple-element.31.two_ref), channel_id=1, source_target_pairs={{4,8},{8,4},{5,9},{9,5},{6,10},{10,6},{7,11},{11,7},{20,24},{24,20... | collective-permute-start | bytes 1572872 | tf_op jit(solution)/shard_map/ppermute | solution.py:830
  10.1 0.7 %collective-permute-start.1 = (bf16[784,128]{1,0:T(8,128)(2,1)}, bf16[784,128]{1,0:T(8,128)(2,1)S(1)}, u32[]{:S(2)}, u32[]{:S(2)}) collective-permute-start(bf16[784,128]{1,0:T(8,128)(2,1)} %get-tuple-element.26), channel_id=1, source_target_pairs={{1,2},{2,1},{5,6},{6,5},{9,10},{10,9},{13,14},{14,13},{17,18},{18,... | collective-permute-start | bytes 602120 | tf_op jit(solution)/shard_map/ppermute | solution.py:834
  10.7 2.9 %collective-permute-start = (bf16[784,128]{1,0:T(8,128)(2,1)}, bf16[784,128]{1,0:T(8,128)(2,1)S(1)}, u32[]{:S(2)}, u32[]{:S(2)}) collective-permute-start(bf16[784,128]{1,0:T(8,128)(2,1)} %get-tuple-element.25), channel_id=1, source_target_pairs={{0,1},{1,0},{2,3},{3,2},{4,5},{5,4},{6,7},{7,6},{8,9},{9,8},{10,11... | collective-permute-start | bytes 602120 | tf_op jit(solution)/shard_map/ppermute | solution.py:833
  13.7 0.0 copy-done.3
  13.7 0.0 copy-done
  13.7 0.0 copy-done.4
  13.7 0.0 copy-done.6
  13.7 3.1 %image_blocks.3 = (bf16[512,512]{1,0:T(8,128)(2,1)S(1)}, bf16[512,512]{1,0:T(8,128)(2,1)S(1)}) custom-call(bf16[2,2048,512]{2,1,0:T(8,128)(2,1)S(1)} %copy-done, s32[4,4,8]{2,1,0:T(4,128)S(1)} %bitcast.3, s32[2,8]{1,0:T(2,128)S(1)} %bitcast.7, f32[8]{0:T(128)S(1)} %copy-done.8, s32[8,512]{1,0:T(8,128)S(1)} %copy-done.3, bf16[8,25]{1,0:T(8,128)(2,1)S(1)} %copy-done.7, ...), custom_call_target="tpu_custom_call" | custom-call | flops 1000 | bytes 1000 | tf_op jit(solution)/shard_map/image_blocks/pallas_call | solution.py:641
  16.8 0.0 collective-permute-done.1.second_ref
  16.8 0.0 collective-permute-done.first_ref
  16.8 1.8 %notes.1 = (bf16[80,512]{1,0:T(8,128)(2,1)S(1)}, bf16[2,256,256]{2,1,0:T(8,128)(2,1)S(1)}, bf16[512,256]{1,0:T(8,128)(2,1)S(1)}) custom-call(s32[4,4,8]{2,1,0:T(4,128)S(1)} %bitcast.4, s32[2,8]{1,0:T(2,128)S(1)} %bitcast.8, f32[8]{0:T(128)S(1)} %copy-done.8, bf16[512,512]{1,0:T(8,128)(2,1)S(1)} %copy-done.1, ...), custom_call_target="tpu_custom_call" | custom-call | flops 1000 | bytes 1000 | tf_op jit(solution)/shard_map/notes/pallas_call | solution.py:392
  18.7 2.6 %collective-permute-start.3 = (bf16[80,512]{1,0:T(8,128)(2,1)S(1)}, bf16[80,512]{1,0:T(8,128)(2,1)S(1)}, u32[]{:S(2)}, u32[]{:S(2)}) collective-permute-start(bf16[80,512]{1,0:T(8,128)(2,1)S(1)} %get-tuple-element.35), channel_id=1, source_target_pairs={{0,12},{12,0},{4,8},{8,4},{1,13},{13,1},{5,9},{9,5},{2,14},{14,2},... | collective-permute-start | bytes 245768 | tf_op jit(solution)/shard_map/ppermute | solution.py:839
  21.3 1.2 %early.1.near_ref = bf16[560,512]{1,0:T(8,128)(2,1)S(1)} custom-call(s32[2,8]{1,0:T(2,128)S(1)} %bitcast.9, bf16[512,512]{1,0:T(8,128)(2,1)S(1)} %copy-done.1, bf16[784,128]{1,0:T(8,128)(2,1)S(1)} %collective-permute-done.first_ref, bf16[784,128]{1,0:T(8,128)(2,1)S(1)} %collective-permute-done.1.second_ref, bf16[8,25]{1,0:T(8,128)(2,1)S(1)} %copy-done.5, ...), custom_call_target="tpu_custom_call" | custom-call | flops 1000 | bytes 1000 | tf_op jit(solution)/shard_map/early/pallas_call | solution.py:423
  22.5 3.8 %collective-permute-start.5 = (bf16[560,512]{1,0:T(8,128)(2,1)S(1)}, bf16[560,512]{1,0:T(8,128)(2,1)S(1)}, u32[]{:S(2)}, u32[]{:S(2)}) collective-permute-start(bf16[560,512]{1,0:T(8,128)(2,1)S(1)} %early.1.near_ref), channel_id=1, source_target_pairs={{0,4},{12,8},{1,5},{13,9},{2,6},{14,10},{3,7},{15,11},{16,20},{28,... | collective-permute-start | bytes 1720328 | tf_op jit(solution)/shard_map/ppermute | solution.py:838
  26.3 0.0 collective-permute-done.2.one_ref.more_1_
  26.3 0.0 copy-done.2
  26.3 0.2 merge.1
  26.5 0.0 collective-permute-done.3.more_5_
  26.5 0.0 collective-permute-done.4.more_2_
  26.5 4.4 %collective-permute-start.7 = (bf16[512,512]{1,0:T(8,128)(2,1)S(1)}, bf16[512,512]{1,0:T(8,128)(2,1)S(1)}, u32[]{:S(2)}, u32[]{:S(2)}) collective-permute-start(bf16[512,512]{1,0:T(8,128)(2,1)S(1)} %merge.1), channel_id=1, source_target_pairs={{0,8},{12,4},{4,12},{8,0},{1,9},{13,5},{5,13},{9,1},{2,10},{14,6},... | collective-permute-start | bytes 1572872 | tf_op jit(solution)/shard_map/ppermute | solution.py:842
  31.0 2.1 %finish.1 = (bf16[512,640]{1,0:T(8,128)(2,1)S(1)}, f32[16,640]{1,0:T(8,128)S(1)}, bf16[80,512]{1,0:T(8,128)(2,1)S(1)}, bf16[512,512]{1,0:T(8,128)(2,1)S(1)}) custom-call(s32[2,8]{1,0:T(2,128)S(1)} %bitcast.10, bf16[512,512]{1,0:T(8,128)(2,1)S(1)} %copy-done.1, s32[8,512]{1,0:T(8,128)S(1)} %copy-done.3, bf16[784,128]{1,0:T(8,128)(2,1)S(1)} %collective-permute-done.first_ref, ...), custom_call_target="tpu_custom_call" | custom-call | flops 1000 | bytes 1000 | tf_op jit(solution)/shard_map/finish/pallas_call | solution.py:490
  33.1 1.5 %collective-permute-start.6 = (bf16[80,512]{1,0:T(8,128)(2,1)S(1)}, bf16[80,512]{1,0:T(8,128)(2,1)S(1)}, u32[]{:S(2)}, u32[]{:S(2)}) collective-permute-start(bf16[80,512]{1,0:T(8,128)(2,1)S(1)} %get-tuple-element.42), channel_id=1, source_target_pairs={{4,0},{8,12},{5,1},{9,13},{6,2},{10,14},{7,3},{11,15},{20,16},{24,... | collective-permute-start | bytes 245768 | tf_op jit(solution)/shard_map/ppermute | solution.py:846
  34.5 8.9 %collective-permute-done.6.more_4_ = bf16[80,512]{1,0:T(8,128)(2,1)S(1)} collective-permute-done((bf16[80,512]{1,0:T(8,128)(2,1)S(1)}, bf16[80,512]{1,0:T(8,128)(2,1)S(1)}, u32[]{:S(2)}, u32[]{:S(2)}) %collective-permute-start.6) | collective-permute-done | bytes 81952 | tf_op jit(solution)/shard_map/ppermute | solution.py:846
  43.5 0.0 collective-permute-done.5.more_3_
  43.5 8.7 %model_term.1 = f32[512,512]{1,0:T(8,128)S(1)} custom-call(s32[4,4,8]{2,1,0:T(4,128)S(1)} %bitcast.5, s32[2,8]{1,0:T(2,128)S(1)} %bitcast.11, f32[8]{0:T(128)S(1)} %copy-done.8, bf16[512,640]{1,0:T(8,128)(2,1)S(1)} %get-tuple-element.38.wide_ref, f32[16,640]{1,0:T(8,128)S(1)} %get-tuple-element.39.good_ref, bf16[8,25]{1,0:T(8,128)(2,1)S(1)} %copy-done.7, ...), custom_call_target="tpu_custom_call" | custom-call | flops 1000 | bytes 1000 | tf_op jit(solution)/shard_map/model_term/pallas_call | solution.py:791
  52.2 0.0 collective-permute-done.7
  52.2 1.1 %convert_add_fusion = f32[512,512]{1,0:T(8,128)} fusion(f32[512,512]{1,0:T(8,128)S(1)} %model_term.1, bf16[512,512]{1,0:T(8,128)(2,1)S(1)} %collective-permute-done.7), kind=kLoop, calls=%fused_computation | loop fusion | flops 524288 | bytes 2621440 | tf_op jit(solution)/shard_map/add | solution.py:851
  (10 shorter events, 0.0 us)
Async XLA Ops:
  0.0 13.6 %copy-start.5 = (bf16[8,25]{1,0:T(8,128)(2,1)S(1)}, bf16[8,25]{1,0:T(8,128)(2,1)}, u32[]{:S(2)}) copy-start(bf16[8,25]{1,0:T(8,128)(2,1)} %psf_cols_ref.5) | copy-start | bytes 1204
  0.0 13.6 %copy-start.8 = (f32[8]{0:T(128)S(1)}, f32[8]{0:T(128)}, u32[]{:S(2)}) copy-start(f32[8]{0:T(128)} %weight_ref.3) | copy-start | bytes 100
  0.0 13.6 %copy-start.7 = (bf16[8,25]{1,0:T(8,128)(2,1)S(1)}, bf16[8,25]{1,0:T(8,128)(2,1)}, u32[]{:S(2)}) copy-start(bf16[8,25]{1,0:T(8,128)(2,1)} %psf_rows_ref.3) | copy-start | bytes 1204
  0.0 13.6 %copy-start.3 = (s32[8,512]{1,0:T(8,128)S(1)}, s32[8,512]{1,0:T(8,128)}, u32[]{:S(2)}) copy-start(s32[8,512]{1,0:T(8,128)} %mask_ref.1) | copy-start | bytes 49156
  0.0 13.7 %copy-start = (bf16[2,2048,512]{2,1,0:T(8,128)(2,1)S(1)}, bf16[2,2048,512]{2,1,0:T(8,128)(2,1)}, u32[]{:S(2)}) copy-start(bf16[2,2048,512]{2,1,0:T(8,128)(2,1)} %images_ref.3) | copy-start | bytes 12582916
  0.0 13.7 %copy-start.4 = (s32[8,4,4]{0,2,1:T(4,128)S(1)}, s32[8,4,4]{0,2,1:T(4,128)}, u32[]{:S(2)}) copy-start(s32[8,4,4]{0,2,1:T(4,128)} %param.15) | copy-start | bytes 1540
  0.0 13.7 %copy-start.6 = (s32[8,2]{0,1:T(2,128)S(1)}, s32[8,2]{0,1:T(2,128)}, u32[]{:S(2)}) copy-start(s32[8,2]{0,1:T(2,128)} %param.12) | copy-start | bytes 196
  0.0 16.8 %copy-start.1 = (bf16[512,512]{1,0:T(8,128)(2,1)S(1)}, bf16[512,512]{1,0:T(8,128)(2,1)}, u32[]{:S(2)}) copy-start(bf16[512,512]{1,0:T(8,128)(2,1)} %scene_ref.5) | copy-start | bytes 1572868
  6.2 20.1 %copy-start.2 = (bf16[512,512]{1,0:T(8,128)(2,1)S(1)}, bf16[512,512]{1,0:T(8,128)(2,1)}, u32[]{:S(2)}) copy-start(bf16[512,512]{1,0:T(8,128)(2,1)} %get-tuple-element.31.two_ref) | copy-start | bytes 1572868
  6.2 20.1 %collective-permute-start.2 = (bf16[512,512]{1,0:T(8,128)(2,1)}, bf16[512,512]{1,0:T(8,128)(2,1)S(1)}, u32[]{:S(2)}, u32[]{:S(2)}) collective-permute-start(bf16[512,512]{1,0:T(8,128)(2,1)} %get-tuple-element.27), channel_id=1, source_target_pairs={{0,4},{4,0},{8,12},{12,8},{1,5},{5,1},{9,13},{13,9},{2,6},{6,2},{1... | collective-permute-start | bytes 1572872 | tf_op jit(solution)/shard_map/ppermute | solution.py:829
  9.4 17.2 %collective-permute-start.4 = (bf16[512,512]{1,0:T(8,128)(2,1)}, bf16[512,512]{1,0:T(8,128)(2,1)S(1)}, u32[]{:S(2)}, u32[]{:S(2)}) collective-permute-start(bf16[512,512]{1,0:T(8,128)(2,1)} %get-tuple-element.31.two_ref), channel_id=1, source_target_pairs={{4,8},{8,4},{5,9},{9,5},{6,10},{10,6},{7,11},{11,7},{20,24},{24,20... | collective-permute-start | bytes 1572872 | tf_op jit(solution)/shard_map/ppermute | solution.py:830
  10.1 6.7 %collective-permute-start.1 = (bf16[784,128]{1,0:T(8,128)(2,1)}, bf16[784,128]{1,0:T(8,128)(2,1)S(1)}, u32[]{:S(2)}, u32[]{:S(2)}) collective-permute-start(bf16[784,128]{1,0:T(8,128)(2,1)} %get-tuple-element.26), channel_id=1, source_target_pairs={{1,2},{2,1},{5,6},{6,5},{9,10},{10,9},{13,14},{14,13},{17,18},{18,... | collective-permute-start | bytes 602120 | tf_op jit(solution)/shard_map/ppermute | solution.py:834
  10.7 6.1 %collective-permute-start = (bf16[784,128]{1,0:T(8,128)(2,1)}, bf16[784,128]{1,0:T(8,128)(2,1)S(1)}, u32[]{:S(2)}, u32[]{:S(2)}) collective-permute-start(bf16[784,128]{1,0:T(8,128)(2,1)} %get-tuple-element.25), channel_id=1, source_target_pairs={{0,1},{1,0},{2,3},{3,2},{4,5},{5,4},{6,7},{7,6},{8,9},{9,8},{10,11... | collective-permute-start | bytes 602120 | tf_op jit(solution)/shard_map/ppermute | solution.py:833
  18.7 7.9 %collective-permute-start.3 = (bf16[80,512]{1,0:T(8,128)(2,1)S(1)}, bf16[80,512]{1,0:T(8,128)(2,1)S(1)}, u32[]{:S(2)}, u32[]{:S(2)}) collective-permute-start(bf16[80,512]{1,0:T(8,128)(2,1)S(1)} %get-tuple-element.35), channel_id=1, source_target_pairs={{0,12},{12,0},{4,8},{8,4},{1,13},{13,1},{5,9},{9,5},{2,14},{14,2},... | collective-permute-start | bytes 245768 | tf_op jit(solution)/shard_map/ppermute | solution.py:839
  22.5 21.0 %collective-permute-start.5 = (bf16[560,512]{1,0:T(8,128)(2,1)S(1)}, bf16[560,512]{1,0:T(8,128)(2,1)S(1)}, u32[]{:S(2)}, u32[]{:S(2)}) collective-permute-start(bf16[560,512]{1,0:T(8,128)(2,1)S(1)} %early.1.near_ref), channel_id=1, source_target_pairs={{0,4},{12,8},{1,5},{13,9},{2,6},{14,10},{3,7},{15,11},{16,20},{28,... | collective-permute-start | bytes 1720328 | tf_op jit(solution)/shard_map/ppermute | solution.py:838
  26.5 25.7 %collective-permute-start.7 = (bf16[512,512]{1,0:T(8,128)(2,1)S(1)}, bf16[512,512]{1,0:T(8,128)(2,1)S(1)}, u32[]{:S(2)}, u32[]{:S(2)}) collective-permute-start(bf16[512,512]{1,0:T(8,128)(2,1)S(1)} %merge.1), channel_id=1, source_target_pairs={{0,8},{12,4},{4,12},{8,0},{1,9},{13,5},{5,13},{9,1},{2,10},{14,6},... | collective-permute-start | bytes 1572872 | tf_op jit(solution)/shard_map/ppermute | solution.py:842
  33.1 10.4 %collective-permute-start.6 = (bf16[80,512]{1,0:T(8,128)(2,1)S(1)}, bf16[80,512]{1,0:T(8,128)(2,1)S(1)}, u32[]{:S(2)}, u32[]{:S(2)}) collective-permute-start(bf16[80,512]{1,0:T(8,128)(2,1)S(1)} %get-tuple-element.42), channel_id=1, source_target_pairs={{4,0},{8,12},{5,1},{9,13},{6,2},{10,14},{7,3},{11,15},{20,16},{24,... | collective-permute-start | bytes 245768 | tf_op jit(solution)/shard_map/ppermute | solution.py:846

commit v5 on v4

--- a/solution.py
+++ b/solution.py
@@ -787,7 +787,7 @@
 
 def model_term(sz, coverage, offsets, weight, wide, good, psf_rows, psf_cols, *extra):
     high = sz.rows + RIM
-    batch = 4 if sz.epochs % 4 == 0 else 1
+    batch = 8 if sz.epochs % 8 == 0 else 1
     return pl.pallas_call(
         functools.partial(model_kernel, sz, batch),
         grid=(sz.epochs // batch,),

time: 53.5 us -> 52.8 us (0.987)
  Pallas kernels: 23.3 us -> 22.4 us
    pallas_call x1, Pallas kernels: 8.73 us -> 7.82 us  [model_term(): pl.pallas_call(functools.partial(model_kernel, sz, batch), grid=(sz.epoch...]
  transfers between devices with their start and end apart: 8 -> 8, of which waited for: 1 -> 1; matrix products, arithmetic and copies ran while one was open for 0% -> 0% of each run, Pallas kernels for 32% -> 31%
where the time goes in v5:
time: 52.8 us; the launch traced here: 52.4 us
  Pallas kernels  22.4 us (42%)
  starting transfers between devices  19.7 us (37%)
  waiting for transfers between devices  8.95 us (17%)
  other arithmetic  1.13 us (2%)
    pallas_call x2, Pallas kernels, image_blocks(): pl.pallas_call(functools.partial(image_kernel, sz, slots, len(ends), pack...  9.27 us
    ppermute x1, waiting for transfers between devices, on_device(): got_back = lax.ppermute(back, 'epoch', [(1, 0), (2, 3)])  8.93 us
    pallas_call x1, Pallas kernels, model_term(): pl.pallas_call(functools.partial(model_kernel, sz, batch), grid=(sz.epoch...  7.82 us
    ppermute x1, starting transfers between devices, on_device(): got_passed = lax.ppermute(passed, 'epoch', [(0, 2), (3, 1), (1, 3), (2, 0)])  4.42 us
    ppermute x1, starting transfers between devices, on_device(): got_three = lax.ppermute(near, 'epoch', [(0, 1), (3, 2)])  3.82 us
    ppermute x1, starting transfers between devices, on_device(): got_one = lax.ppermute(one, 'epoch', pairs(0, depth))  3.13 us
    ppermute x1, starting transfers between devices, on_device(): first = lax.ppermute(first, 'sky', pairs(0, peers))  2.9 us
    ppermute x1, starting transfers between devices, on_device(): got_far = lax.ppermute(far, 'epoch', [(0, 3), (3, 0), (1, 2), (2, 1)])  2.6 us
  transfers between devices with their start and end apart: 8, of which 1 were waited for; matrix products, arithmetic and copies ran while one was open for 0% of the time, Pallas kernels for 31%

profile of v5, /device:TPU:0, one launch (start us, length us, event | category | flops | bytes accessed | tf_op | source)
XLA Modules:
  0.0 52.4 jit_solution(8574042536249129100)
XLA Ops:
  0.0 0.0 copy-start.4
  0.0 0.0 copy-start.6
  0.0 0.0 copy-start.1
  0.0 6.2 %image_blocks.2 = (bf16[512,512]{1,0:T(8,128)(2,1)}, bf16[512,512]{1,0:T(8,128)(2,1)}, bf16[784,128]{1,0:T(8,128)(2,1)}, bf16[784,128]{1,0:T(8,128)(2,1)}) custom-call(bf16[2,2048,512]{2,1,0:T(8,128)(2,1)} %images_ref.3, s32[4,4,8]{2,1,0:T(4,128)} %bitcast.2, s32[2,8]{1,0:T(2,128)} %bitcast.6, f32[8]{0:T(128)} %weight_ref.3, s32[8,512]{1,0:T(8,128)} %mask_ref.1, ...), custom_call_target="tpu_custom_call" | custom-call | flops 1000 | bytes 1000 | tf_op jit(solution)/shard_map/image_blocks/pallas_call | solution.py:641
  6.2 0.0 copy-start.2
  6.2 3.1 %collective-permute-start.2 = (bf16[512,512]{1,0:T(8,128)(2,1)}, bf16[512,512]{1,0:T(8,128)(2,1)S(1)}, u32[]{:S(2)}, u32[]{:S(2)}) collective-permute-start(bf16[512,512]{1,0:T(8,128)(2,1)} %get-tuple-element.27), channel_id=1, source_target_pairs={{0,4},{4,0},{8,12},{12,8},{1,5},{5,1},{9,13},{13,9},{2,6},{6,2},{1... | collective-permute-start | bytes 1572872 | tf_op jit(solution)/shard_map/ppermute | solution.py:829
  9.4 0.7 %collective-permute-start.4 = (bf16[512,512]{1,0:T(8,128)(2,1)}, bf16[512,512]{1,0:T(8,128)(2,1)S(1)}, u32[]{:S(2)}, u32[]{:S(2)}) collective-permute-start(bf16[512,512]{1,0:T(8,128)(2,1)} %get-tuple-element.31.two_ref), channel_id=1, source_target_pairs={{4,8},{8,4},{5,9},{9,5},{6,10},{10,6},{7,11},{11,7},{20,24},{24,20... | collective-permute-start | bytes 1572872 | tf_op jit(solution)/shard_map/ppermute | solution.py:830
  10.1 0.7 %collective-permute-start.1 = (bf16[784,128]{1,0:T(8,128)(2,1)}, bf16[784,128]{1,0:T(8,128)(2,1)S(1)}, u32[]{:S(2)}, u32[]{:S(2)}) collective-permute-start(bf16[784,128]{1,0:T(8,128)(2,1)} %get-tuple-element.26), channel_id=1, source_target_pairs={{1,2},{2,1},{5,6},{6,5},{9,10},{10,9},{13,14},{14,13},{17,18},{18,... | collective-permute-start | bytes 602120 | tf_op jit(solution)/shard_map/ppermute | solution.py:834
  10.7 2.9 %collective-permute-start = (bf16[784,128]{1,0:T(8,128)(2,1)}, bf16[784,128]{1,0:T(8,128)(2,1)S(1)}, u32[]{:S(2)}, u32[]{:S(2)}) collective-permute-start(bf16[784,128]{1,0:T(8,128)(2,1)} %get-tuple-element.25), channel_id=1, source_target_pairs={{0,1},{1,0},{2,3},{3,2},{4,5},{5,4},{6,7},{7,6},{8,9},{9,8},{10,11... | collective-permute-start | bytes 602120 | tf_op jit(solution)/shard_map/ppermute | solution.py:833
  13.6 0.0 copy-done.5
  13.6 0.0 copy-done.8
  13.6 0.0 copy-done.7
  13.7 3.1 %image_blocks.3 = (bf16[512,512]{1,0:T(8,128)(2,1)S(1)}, bf16[512,512]{1,0:T(8,128)(2,1)S(1)}) custom-call(bf16[2,2048,512]{2,1,0:T(8,128)(2,1)S(1)} %copy-done, s32[4,4,8]{2,1,0:T(4,128)S(1)} %bitcast.3, s32[2,8]{1,0:T(2,128)S(1)} %bitcast.7, f32[8]{0:T(128)S(1)} %copy-done.8, s32[8,512]{1,0:T(8,128)S(1)} %copy-done.3, bf16[8,25]{1,0:T(8,128)(2,1)S(1)} %copy-done.7, ...), custom_call_target="tpu_custom_call" | custom-call | flops 1000 | bytes 1000 | tf_op jit(solution)/shard_map/image_blocks/pallas_call | solution.py:641
  16.8 0.0 collective-permute-done.1.second_ref
  16.8 0.0 collective-permute-done.first_ref
  16.8 0.0 copy-done.1
  16.8 1.8 %notes.1 = (bf16[80,512]{1,0:T(8,128)(2,1)S(1)}, bf16[2,256,256]{2,1,0:T(8,128)(2,1)S(1)}, bf16[512,256]{1,0:T(8,128)(2,1)S(1)}) custom-call(s32[4,4,8]{2,1,0:T(4,128)S(1)} %bitcast.4, s32[2,8]{1,0:T(2,128)S(1)} %bitcast.8, f32[8]{0:T(128)S(1)} %copy-done.8, bf16[512,512]{1,0:T(8,128)(2,1)S(1)} %copy-done.1, ...), custom_call_target="tpu_custom_call" | custom-call | flops 1000 | bytes 1000 | tf_op jit(solution)/shard_map/notes/pallas_call | solution.py:392
  18.7 2.6 %collective-permute-start.3 = (bf16[80,512]{1,0:T(8,128)(2,1)S(1)}, bf16[80,512]{1,0:T(8,128)(2,1)S(1)}, u32[]{:S(2)}, u32[]{:S(2)}) collective-permute-start(bf16[80,512]{1,0:T(8,128)(2,1)S(1)} %get-tuple-element.35), channel_id=1, source_target_pairs={{0,12},{12,0},{4,8},{8,4},{1,13},{13,1},{5,9},{9,5},{2,14},{14,2},... | collective-permute-start | bytes 245768 | tf_op jit(solution)/shard_map/ppermute | solution.py:839
  21.3 1.2 %early.1.near_ref = bf16[560,512]{1,0:T(8,128)(2,1)S(1)} custom-call(s32[2,8]{1,0:T(2,128)S(1)} %bitcast.9, bf16[512,512]{1,0:T(8,128)(2,1)S(1)} %copy-done.1, bf16[784,128]{1,0:T(8,128)(2,1)S(1)} %collective-permute-done.first_ref, bf16[784,128]{1,0:T(8,128)(2,1)S(1)} %collective-permute-done.1.second_ref, bf16[8,25]{1,0:T(8,128)(2,1)S(1)} %copy-done.5, ...), custom_call_target="tpu_custom_call" | custom-call | flops 1000 | bytes 1000 | tf_op jit(solution)/shard_map/early/pallas_call | solution.py:423
  22.5 3.8 %collective-permute-start.5 = (bf16[560,512]{1,0:T(8,128)(2,1)S(1)}, bf16[560,512]{1,0:T(8,128)(2,1)S(1)}, u32[]{:S(2)}, u32[]{:S(2)}) collective-permute-start(bf16[560,512]{1,0:T(8,128)(2,1)S(1)} %early.1.near_ref), channel_id=1, source_target_pairs={{0,4},{12,8},{1,5},{13,9},{2,6},{14,10},{3,7},{15,11},{16,20},{28,... | collective-permute-start | bytes 1720328 | tf_op jit(solution)/shard_map/ppermute | solution.py:838
  26.3 0.0 collective-permute-done.2.one_ref.more_1_
  26.3 0.2 merge.1
  26.5 0.0 collective-permute-done.3.more_5_
  26.5 0.0 collective-permute-done.4.more_2_
  26.5 4.4 %collective-permute-start.7 = (bf16[512,512]{1,0:T(8,128)(2,1)S(1)}, bf16[512,512]{1,0:T(8,128)(2,1)S(1)}, u32[]{:S(2)}, u32[]{:S(2)}) collective-permute-start(bf16[512,512]{1,0:T(8,128)(2,1)S(1)} %merge.1), channel_id=1, source_target_pairs={{0,8},{12,4},{4,12},{8,0},{1,9},{13,5},{5,13},{9,1},{2,10},{14,6},... | collective-permute-start | bytes 1572872 | tf_op jit(solution)/shard_map/ppermute | solution.py:842
  31.0 2.1 %finish.1 = (bf16[512,640]{1,0:T(8,128)(2,1)S(1)}, f32[16,640]{1,0:T(8,128)S(1)}, bf16[80,512]{1,0:T(8,128)(2,1)S(1)}, bf16[512,512]{1,0:T(8,128)(2,1)S(1)}) custom-call(s32[2,8]{1,0:T(2,128)S(1)} %bitcast.10, bf16[512,512]{1,0:T(8,128)(2,1)S(1)} %copy-done.1, s32[8,512]{1,0:T(8,128)S(1)} %copy-done.3, bf16[784,128]{1,0:T(8,128)(2,1)S(1)} %collective-permute-done.first_ref, ...), custom_call_target="tpu_custom_call" | custom-call | flops 1000 | bytes 1000 | tf_op jit(solution)/shard_map/finish/pallas_call | solution.py:490
  33.1 1.5 %collective-permute-start.6 = (bf16[80,512]{1,0:T(8,128)(2,1)S(1)}, bf16[80,512]{1,0:T(8,128)(2,1)S(1)}, u32[]{:S(2)}, u32[]{:S(2)}) collective-permute-start(bf16[80,512]{1,0:T(8,128)(2,1)S(1)} %get-tuple-element.42), channel_id=1, source_target_pairs={{4,0},{8,12},{5,1},{9,13},{6,2},{10,14},{7,3},{11,15},{20,16},{24,... | collective-permute-start | bytes 245768 | tf_op jit(solution)/shard_map/ppermute | solution.py:846
  34.5 8.9 %collective-permute-done.6.more_4_ = bf16[80,512]{1,0:T(8,128)(2,1)S(1)} collective-permute-done((bf16[80,512]{1,0:T(8,128)(2,1)S(1)}, bf16[80,512]{1,0:T(8,128)(2,1)S(1)}, u32[]{:S(2)}, u32[]{:S(2)}) %collective-permute-start.6) | collective-permute-done | bytes 81952 | tf_op jit(solution)/shard_map/ppermute | solution.py:846
  43.5 0.0 collective-permute-done.5.more_3_
  43.5 7.8 %model_term.1 = f32[512,512]{1,0:T(8,128)S(1)} custom-call(s32[4,4,8]{2,1,0:T(4,128)S(1)} %bitcast.5, s32[2,8]{1,0:T(2,128)S(1)} %bitcast.11, f32[8]{0:T(128)S(1)} %copy-done.8, bf16[512,640]{1,0:T(8,128)(2,1)S(1)} %get-tuple-element.38.wide_ref, f32[16,640]{1,0:T(8,128)S(1)} %get-tuple-element.39.good_ref, bf16[8,25]{1,0:T(8,128)(2,1)S(1)} %copy-done.7, ...), custom_call_target="tpu_custom_call" | custom-call | flops 1000 | bytes 1000 | tf_op jit(solution)/shard_map/model_term/pallas_call | solution.py:791
  51.3 0.0 collective-permute-done.7
  51.3 1.1 %convert_add_fusion = f32[512,512]{1,0:T(8,128)} fusion(f32[512,512]{1,0:T(8,128)S(1)} %model_term.1, bf16[512,512]{1,0:T(8,128)(2,1)S(1)} %collective-permute-done.7), kind=kLoop, calls=%fused_computation | loop fusion | flops 524288 | bytes 2621440 | tf_op jit(solution)/shard_map/add | solution.py:851
  (10 shorter events, 0.0 us)
Async XLA Ops:
  0.0 13.6 %copy-start.5 = (bf16[8,25]{1,0:T(8,128)(2,1)S(1)}, bf16[8,25]{1,0:T(8,128)(2,1)}, u32[]{:S(2)}) copy-start(bf16[8,25]{1,0:T(8,128)(2,1)} %psf_cols_ref.5) | copy-start | bytes 1204
  0.0 13.6 %copy-start.8 = (f32[8]{0:T(128)S(1)}, f32[8]{0:T(128)}, u32[]{:S(2)}) copy-start(f32[8]{0:T(128)} %weight_ref.3) | copy-start | bytes 100
  0.0 13.6 %copy-start.7 = (bf16[8,25]{1,0:T(8,128)(2,1)S(1)}, bf16[8,25]{1,0:T(8,128)(2,1)}, u32[]{:S(2)}) copy-start(bf16[8,25]{1,0:T(8,128)(2,1)} %psf_rows_ref.3) | copy-start | bytes 1204
  0.0 13.6 %copy-start.3 = (s32[8,512]{1,0:T(8,128)S(1)}, s32[8,512]{1,0:T(8,128)}, u32[]{:S(2)}) copy-start(s32[8,512]{1,0:T(8,128)} %mask_ref.1) | copy-start | bytes 49156
  0.0 13.7 %copy-start = (bf16[2,2048,512]{2,1,0:T(8,128)(2,1)S(1)}, bf16[2,2048,512]{2,1,0:T(8,128)(2,1)}, u32[]{:S(2)}) copy-start(bf16[2,2048,512]{2,1,0:T(8,128)(2,1)} %images_ref.3) | copy-start | bytes 12582916
  0.0 13.7 %copy-start.4 = (s32[8,4,4]{0,2,1:T(4,128)S(1)}, s32[8,4,4]{0,2,1:T(4,128)}, u32[]{:S(2)}) copy-start(s32[8,4,4]{0,2,1:T(4,128)} %param.15) | copy-start | bytes 1540
  0.0 13.7 %copy-start.6 = (s32[8,2]{0,1:T(2,128)S(1)}, s32[8,2]{0,1:T(2,128)}, u32[]{:S(2)}) copy-start(s32[8,2]{0,1:T(2,128)} %param.12) | copy-start | bytes 196
  0.0 16.8 %copy-start.1 = (bf16[512,512]{1,0:T(8,128)(2,1)S(1)}, bf16[512,512]{1,0:T(8,128)(2,1)}, u32[]{:S(2)}) copy-start(bf16[512,512]{1,0:T(8,128)(2,1)} %scene_ref.5) | copy-start | bytes 1572868
  6.2 20.1 %copy-start.2 = (bf16[512,512]{1,0:T(8,128)(2,1)S(1)}, bf16[512,512]{1,0:T(8,128)(2,1)}, u32[]{:S(2)}) copy-start(bf16[512,512]{1,0:T(8,128)(2,1)} %get-tuple-element.31.two_ref) | copy-start | bytes 1572868
  6.2 20.1 %collective-permute-start.2 = (bf16[512,512]{1,0:T(8,128)(2,1)}, bf16[512,512]{1,0:T(8,128)(2,1)S(1)}, u32[]{:S(2)}, u32[]{:S(2)}) collective-permute-start(bf16[512,512]{1,0:T(8,128)(2,1)} %get-tuple-element.27), channel_id=1, source_target_pairs={{0,4},{4,0},{8,12},{12,8},{1,5},{5,1},{9,13},{13,9},{2,6},{6,2},{1... | collective-permute-start | bytes 1572872 | tf_op jit(solution)/shard_map/ppermute | solution.py:829
  9.4 17.2 %collective-permute-start.4 = (bf16[512,512]{1,0:T(8,128)(2,1)}, bf16[512,512]{1,0:T(8,128)(2,1)S(1)}, u32[]{:S(2)}, u32[]{:S(2)}) collective-permute-start(bf16[512,512]{1,0:T(8,128)(2,1)} %get-tuple-element.31.two_ref), channel_id=1, source_target_pairs={{4,8},{8,4},{5,9},{9,5},{6,10},{10,6},{7,11},{11,7},{20,24},{24,20... | collective-permute-start | bytes 1572872 | tf_op jit(solution)/shard_map/ppermute | solution.py:830
  10.1 6.7 %collective-permute-start.1 = (bf16[784,128]{1,0:T(8,128)(2,1)}, bf16[784,128]{1,0:T(8,128)(2,1)S(1)}, u32[]{:S(2)}, u32[]{:S(2)}) collective-permute-start(bf16[784,128]{1,0:T(8,128)(2,1)} %get-tuple-element.26), channel_id=1, source_target_pairs={{1,2},{2,1},{5,6},{6,5},{9,10},{10,9},{13,14},{14,13},{17,18},{18,... | collective-permute-start | bytes 602120 | tf_op jit(solution)/shard_map/ppermute | solution.py:834
  10.7 6.1 %collective-permute-start = (bf16[784,128]{1,0:T(8,128)(2,1)}, bf16[784,128]{1,0:T(8,128)(2,1)S(1)}, u32[]{:S(2)}, u32[]{:S(2)}) collective-permute-start(bf16[784,128]{1,0:T(8,128)(2,1)} %get-tuple-element.25), channel_id=1, source_target_pairs={{0,1},{1,0},{2,3},{3,2},{4,5},{5,4},{6,7},{7,6},{8,9},{9,8},{10,11... | collective-permute-start | bytes 602120 | tf_op jit(solution)/shard_map/ppermute | solution.py:833
  18.7 7.9 %collective-permute-start.3 = (bf16[80,512]{1,0:T(8,128)(2,1)S(1)}, bf16[80,512]{1,0:T(8,128)(2,1)S(1)}, u32[]{:S(2)}, u32[]{:S(2)}) collective-permute-start(bf16[80,512]{1,0:T(8,128)(2,1)S(1)} %get-tuple-element.35), channel_id=1, source_target_pairs={{0,12},{12,0},{4,8},{8,4},{1,13},{13,1},{5,9},{9,5},{2,14},{14,2},... | collective-permute-start | bytes 245768 | tf_op jit(solution)/shard_map/ppermute | solution.py:839
  22.5 21.0 %collective-permute-start.5 = (bf16[560,512]{1,0:T(8,128)(2,1)S(1)}, bf16[560,512]{1,0:T(8,128)(2,1)S(1)}, u32[]{:S(2)}, u32[]{:S(2)}) collective-permute-start(bf16[560,512]{1,0:T(8,128)(2,1)S(1)} %early.1.near_ref), channel_id=1, source_target_pairs={{0,4},{12,8},{1,5},{13,9},{2,6},{14,10},{3,7},{15,11},{16,20},{28,... | collective-permute-start | bytes 1720328 | tf_op jit(solution)/shard_map/ppermute | solution.py:838
  26.5 24.8 %collective-permute-start.7 = (bf16[512,512]{1,0:T(8,128)(2,1)S(1)}, bf16[512,512]{1,0:T(8,128)(2,1)S(1)}, u32[]{:S(2)}, u32[]{:S(2)}) collective-permute-start(bf16[512,512]{1,0:T(8,128)(2,1)S(1)} %merge.1), channel_id=1, source_target_pairs={{0,8},{12,4},{4,12},{8,0},{1,9},{13,5},{5,13},{9,1},{2,10},{14,6},... | collective-permute-start | bytes 1572872 | tf_op jit(solution)/shard_map/ppermute | solution.py:842
  33.1 10.4 %collective-permute-start.6 = (bf16[80,512]{1,0:T(8,128)(2,1)S(1)}, bf16[80,512]{1,0:T(8,128)(2,1)S(1)}, u32[]{:S(2)}, u32[]{:S(2)}) collective-permute-start(bf16[80,512]{1,0:T(8,128)(2,1)S(1)} %get-tuple-element.42), channel_id=1, source_target_pairs={{4,0},{8,12},{5,1},{9,13},{6,2},{10,14},{7,3},{11,15},{20,16},{24,... | collective-permute-start | bytes 245768 | tf_op jit(solution)/shard_map/ppermute | solution.py:846

commit v6 on v5

--- a/solution.py
+++ b/solution.py
@@ -542,8 +542,6 @@
         copy.start()
     if packs:
         edge_waits = edge_copies(sz, images_ref, scene_ref, edge, sides, edge_sem, side_sem)
-        for copy in edge_waits[0] + edge_waits[1]:
-            copy.start()
     for copy in held_copies:
         copy.wait()
     load_taps(psf_rows_ref, row_lines, sz.epochs, sz.taps)
@@ -575,6 +573,8 @@
     for i, target in enumerate(targets):
         for copy in copies[3 * sz.local * i : 3 * sz.local * (i + 1)]:
             copy.wait()
+        for copy in edge_waits[0] + edge_waits[1] if packs and i == 0 else ():
+            copy.start()
         start = target * sz.rows
         zones = (
             (0, HALO, tile_of(start - HALO)),

time: 52.8 us -> 52.2 us (0.989)
  Pallas kernels: 22.4 us -> 21.8 us
    pallas_call x2, Pallas kernels: 9.27 us -> 8.7 us  [image_blocks(): pl.pallas_call(functools.partial(image_kernel, sz, slots, len(ends), pack...]
where the time goes in v6:
time: 52.2 us; the launch traced here: 51.8 us
  Pallas kernels  21.8 us (42%)
  starting transfers between devices  19.7 us (38%)
  waiting for transfers between devices  8.95 us (17%)
  other arithmetic  1.13 us (2%)
    ppermute x1, waiting for transfers between devices, on_device(): got_back = lax.ppermute(back, 'epoch', [(1, 0), (2, 3)])  8.93 us
    pallas_call x2, Pallas kernels, image_blocks(): pl.pallas_call(functools.partial(image_kernel, sz, slots, len(ends), pack...  8.7 us
    pallas_call x1, Pallas kernels, model_term(): pl.pallas_call(functools.partial(model_kernel, sz, batch), grid=(sz.epoch...  7.82 us
    ppermute x1, starting transfers between devices, on_device(): got_passed = lax.ppermute(passed, 'epoch', [(0, 2), (3, 1), (1, 3), (2, 0)])  4.43 us
    ppermute x1, starting transfers between devices, on_device(): got_three = lax.ppermute(near, 'epoch', [(0, 1), (3, 2)])  3.85 us
    ppermute x1, starting transfers between devices, on_device(): got_one = lax.ppermute(one, 'epoch', pairs(0, depth))  3.09 us
    ppermute x1, starting transfers between devices, on_device(): first = lax.ppermute(first, 'sky', pairs(0, peers))  2.9 us
    ppermute x1, starting transfers between devices, on_device(): got_far = lax.ppermute(far, 'epoch', [(0, 3), (3, 0), (1, 2), (2, 1)])  2.55 us
  transfers between devices with their start and end apart: 8, of which 1 were waited for; matrix products, arithmetic and copies ran while one was open for 0% of the time, Pallas kernels for 31%

profile of v6, /device:TPU:0, one launch (start us, length us, event | category | flops | bytes accessed | tf_op | source)
XLA Modules:
  0.0 51.8 jit_solution(237449083481235417)
XLA Ops:
  0.0 0.0 copy-start.4
  0.0 0.0 copy-start.6
  0.0 0.0 copy-start.1
  0.0 5.6 %image_blocks.2 = (bf16[512,512]{1,0:T(8,128)(2,1)}, bf16[512,512]{1,0:T(8,128)(2,1)}, bf16[784,128]{1,0:T(8,128)(2,1)}, bf16[784,128]{1,0:T(8,128)(2,1)}) custom-call(bf16[2,2048,512]{2,1,0:T(8,128)(2,1)} %images_ref.3, s32[4,4,8]{2,1,0:T(4,128)} %bitcast.2, s32[2,8]{1,0:T(2,128)} %bitcast.6, f32[8]{0:T(128)} %weight_ref.3, s32[8,512]{1,0:T(8,128)} %mask_ref.1, ...), custom_call_target="tpu_custom_call" | custom-call | flops 1000 | bytes 1000 | tf_op jit(solution)/shard_map/image_blocks/pallas_call | solution.py:641
  5.7 0.0 copy-start.2
  5.7 3.1 %collective-permute-start.2 = (bf16[512,512]{1,0:T(8,128)(2,1)}, bf16[512,512]{1,0:T(8,128)(2,1)S(1)}, u32[]{:S(2)}, u32[]{:S(2)}) collective-permute-start(bf16[512,512]{1,0:T(8,128)(2,1)} %get-tuple-element.27), channel_id=1, source_target_pairs={{0,4},{4,0},{8,12},{12,8},{1,5},{5,1},{9,13},{13,9},{2,6},{6,2},{1... | collective-permute-start | bytes 1572872 | tf_op jit(solution)/shard_map/ppermute | solution.py:829
  8.8 0.7 %collective-permute-start.4 = (bf16[512,512]{1,0:T(8,128)(2,1)}, bf16[512,512]{1,0:T(8,128)(2,1)S(1)}, u32[]{:S(2)}, u32[]{:S(2)}) collective-permute-start(bf16[512,512]{1,0:T(8,128)(2,1)} %get-tuple-element.31.two_ref), channel_id=1, source_target_pairs={{4,8},{8,4},{5,9},{9,5},{6,10},{10,6},{7,11},{11,7},{20,24},{24,20... | collective-permute-start | bytes 1572872 | tf_op jit(solution)/shard_map/ppermute | solution.py:830
  9.5 0.7 %collective-permute-start.1 = (bf16[784,128]{1,0:T(8,128)(2,1)}, bf16[784,128]{1,0:T(8,128)(2,1)S(1)}, u32[]{:S(2)}, u32[]{:S(2)}) collective-permute-start(bf16[784,128]{1,0:T(8,128)(2,1)} %get-tuple-element.26), channel_id=1, source_target_pairs={{1,2},{2,1},{5,6},{6,5},{9,10},{10,9},{13,14},{14,13},{17,18},{18,... | collective-permute-start | bytes 602120 | tf_op jit(solution)/shard_map/ppermute | solution.py:834
  10.1 2.9 %collective-permute-start = (bf16[784,128]{1,0:T(8,128)(2,1)}, bf16[784,128]{1,0:T(8,128)(2,1)S(1)}, u32[]{:S(2)}, u32[]{:S(2)}) collective-permute-start(bf16[784,128]{1,0:T(8,128)(2,1)} %get-tuple-element.25), channel_id=1, source_target_pairs={{0,1},{1,0},{2,3},{3,2},{4,5},{5,4},{6,7},{7,6},{8,9},{9,8},{10,11... | collective-permute-start | bytes 602120 | tf_op jit(solution)/shard_map/ppermute | solution.py:833
  13.0 0.0 copy-done.5
  13.0 0.0 copy-done.8
  13.0 0.0 copy-done.3
  13.1 3.1 %image_blocks.3 = (bf16[512,512]{1,0:T(8,128)(2,1)S(1)}, bf16[512,512]{1,0:T(8,128)(2,1)S(1)}) custom-call(bf16[2,2048,512]{2,1,0:T(8,128)(2,1)S(1)} %copy-done, s32[4,4,8]{2,1,0:T(4,128)S(1)} %bitcast.3, s32[2,8]{1,0:T(2,128)S(1)} %bitcast.7, f32[8]{0:T(128)S(1)} %copy-done.8, s32[8,512]{1,0:T(8,128)S(1)} %copy-done.3, bf16[8,25]{1,0:T(8,128)(2,1)S(1)} %copy-done.7, ...), custom_call_target="tpu_custom_call" | custom-call | flops 1000 | bytes 1000 | tf_op jit(solution)/shard_map/image_blocks/pallas_call | solution.py:641
  16.2 0.0 collective-permute-done.1.second_ref
  16.2 0.0 collective-permute-done.first_ref
  16.2 1.8 %notes.1 = (bf16[80,512]{1,0:T(8,128)(2,1)S(1)}, bf16[2,256,256]{2,1,0:T(8,128)(2,1)S(1)}, bf16[512,256]{1,0:T(8,128)(2,1)S(1)}) custom-call(s32[4,4,8]{2,1,0:T(4,128)S(1)} %bitcast.4, s32[2,8]{1,0:T(2,128)S(1)} %bitcast.8, f32[8]{0:T(128)S(1)} %copy-done.8, bf16[512,512]{1,0:T(8,128)(2,1)S(1)} %copy-done.1, ...), custom_call_target="tpu_custom_call" | custom-call | flops 1000 | bytes 1000 | tf_op jit(solution)/shard_map/notes/pallas_call | solution.py:392
  18.1 2.5 %collective-permute-start.3 = (bf16[80,512]{1,0:T(8,128)(2,1)S(1)}, bf16[80,512]{1,0:T(8,128)(2,1)S(1)}, u32[]{:S(2)}, u32[]{:S(2)}) collective-permute-start(bf16[80,512]{1,0:T(8,128)(2,1)S(1)} %get-tuple-element.35), channel_id=1, source_target_pairs={{0,12},{12,0},{4,8},{8,4},{1,13},{13,1},{5,9},{9,5},{2,14},{14,2},... | collective-permute-start | bytes 245768 | tf_op jit(solution)/shard_map/ppermute | solution.py:839
  20.6 1.2 %early.1.near_ref = bf16[560,512]{1,0:T(8,128)(2,1)S(1)} custom-call(s32[2,8]{1,0:T(2,128)S(1)} %bitcast.9, bf16[512,512]{1,0:T(8,128)(2,1)S(1)} %copy-done.1, bf16[784,128]{1,0:T(8,128)(2,1)S(1)} %collective-permute-done.first_ref, bf16[784,128]{1,0:T(8,128)(2,1)S(1)} %collective-permute-done.1.second_ref, bf16[8,25]{1,0:T(8,128)(2,1)S(1)} %copy-done.5, ...), custom_call_target="tpu_custom_call" | custom-call | flops 1000 | bytes 1000 | tf_op jit(solution)/shard_map/early/pallas_call | solution.py:423
  21.8 3.9 %collective-permute-start.5 = (bf16[560,512]{1,0:T(8,128)(2,1)S(1)}, bf16[560,512]{1,0:T(8,128)(2,1)S(1)}, u32[]{:S(2)}, u32[]{:S(2)}) collective-permute-start(bf16[560,512]{1,0:T(8,128)(2,1)S(1)} %early.1.near_ref), channel_id=1, source_target_pairs={{0,4},{12,8},{1,5},{13,9},{2,6},{14,10},{3,7},{15,11},{16,20},{28,... | collective-permute-start | bytes 1720328 | tf_op jit(solution)/shard_map/ppermute | solution.py:838
  25.7 0.0 collective-permute-done.2.one_ref.more_1_
  25.7 0.0 copy-done.2
  25.7 0.2 merge.1
  25.9 0.0 collective-permute-done.3.more_5_
  25.9 0.0 collective-permute-done.4.more_2_
  25.9 4.4 %collective-permute-start.7 = (bf16[512,512]{1,0:T(8,128)(2,1)S(1)}, bf16[512,512]{1,0:T(8,128)(2,1)S(1)}, u32[]{:S(2)}, u32[]{:S(2)}) collective-permute-start(bf16[512,512]{1,0:T(8,128)(2,1)S(1)} %merge.1), channel_id=1, source_target_pairs={{0,8},{12,4},{4,12},{8,0},{1,9},{13,5},{5,13},{9,1},{2,10},{14,6},... | collective-permute-start | bytes 1572872 | tf_op jit(solution)/shard_map/ppermute | solution.py:842
  30.4 2.1 %finish.1 = (bf16[512,640]{1,0:T(8,128)(2,1)S(1)}, f32[16,640]{1,0:T(8,128)S(1)}, bf16[80,512]{1,0:T(8,128)(2,1)S(1)}, bf16[512,512]{1,0:T(8,128)(2,1)S(1)}) custom-call(s32[2,8]{1,0:T(2,128)S(1)} %bitcast.10, bf16[512,512]{1,0:T(8,128)(2,1)S(1)} %copy-done.1, s32[8,512]{1,0:T(8,128)S(1)} %copy-done.3, bf16[784,128]{1,0:T(8,128)(2,1)S(1)} %collective-permute-done.first_ref, ...), custom_call_target="tpu_custom_call" | custom-call | flops 1000 | bytes 1000 | tf_op jit(solution)/shard_map/finish/pallas_call | solution.py:490
  32.4 1.5 %collective-permute-start.6 = (bf16[80,512]{1,0:T(8,128)(2,1)S(1)}, bf16[80,512]{1,0:T(8,128)(2,1)S(1)}, u32[]{:S(2)}, u32[]{:S(2)}) collective-permute-start(bf16[80,512]{1,0:T(8,128)(2,1)S(1)} %get-tuple-element.42), channel_id=1, source_target_pairs={{4,0},{8,12},{5,1},{9,13},{6,2},{10,14},{7,3},{11,15},{20,16},{24,... | collective-permute-start | bytes 245768 | tf_op jit(solution)/shard_map/ppermute | solution.py:846
  33.9 8.9 %collective-permute-done.6.more_4_ = bf16[80,512]{1,0:T(8,128)(2,1)S(1)} collective-permute-done((bf16[80,512]{1,0:T(8,128)(2,1)S(1)}, bf16[80,512]{1,0:T(8,128)(2,1)S(1)}, u32[]{:S(2)}, u32[]{:S(2)}) %collective-permute-start.6) | collective-permute-done | bytes 81952 | tf_op jit(solution)/shard_map/ppermute | solution.py:846
  42.8 0.0 collective-permute-done.5.more_3_
  42.8 7.8 %model_term.1 = f32[512,512]{1,0:T(8,128)S(1)} custom-call(s32[4,4,8]{2,1,0:T(4,128)S(1)} %bitcast.5, s32[2,8]{1,0:T(2,128)S(1)} %bitcast.11, f32[8]{0:T(128)S(1)} %copy-done.8, bf16[512,640]{1,0:T(8,128)(2,1)S(1)} %get-tuple-element.38.wide_ref, f32[16,640]{1,0:T(8,128)S(1)} %get-tuple-element.39.good_ref, bf16[8,25]{1,0:T(8,128)(2,1)S(1)} %copy-done.7, ...), custom_call_target="tpu_custom_call" | custom-call | flops 1000 | bytes 1000 | tf_op jit(solution)/shard_map/model_term/pallas_call | solution.py:791
  50.7 0.0 collective-permute-done.7
  50.7 1.1 %convert_add_fusion = f32[512,512]{1,0:T(8,128)} fusion(f32[512,512]{1,0:T(8,128)S(1)} %model_term.1, bf16[512,512]{1,0:T(8,128)(2,1)S(1)} %collective-permute-done.7), kind=kLoop, calls=%fused_computation | loop fusion | flops 524288 | bytes 2621440 | tf_op jit(solution)/shard_map/add | solution.py:851
  (10 shorter events, 0.0 us)
Async XLA Ops:
  0.0 13.0 %copy-start.5 = (bf16[8,25]{1,0:T(8,128)(2,1)S(1)}, bf16[8,25]{1,0:T(8,128)(2,1)}, u32[]{:S(2)}) copy-start(bf16[8,25]{1,0:T(8,128)(2,1)} %psf_cols_ref.5) | copy-start | bytes 1204
  0.0 13.0 %copy-start.8 = (f32[8]{0:T(128)S(1)}, f32[8]{0:T(128)}, u32[]{:S(2)}) copy-start(f32[8]{0:T(128)} %weight_ref.3) | copy-start | bytes 100
  0.0 13.0 %copy-start.7 = (bf16[8,25]{1,0:T(8,128)(2,1)S(1)}, bf16[8,25]{1,0:T(8,128)(2,1)}, u32[]{:S(2)}) copy-start(bf16[8,25]{1,0:T(8,128)(2,1)} %psf_rows_ref.3) | copy-start | bytes 1204
  0.0 13.0 %copy-start.3 = (s32[8,512]{1,0:T(8,128)S(1)}, s32[8,512]{1,0:T(8,128)}, u32[]{:S(2)}) copy-start(s32[8,512]{1,0:T(8,128)} %mask_ref.1) | copy-start | bytes 49156
  0.0 13.0 %copy-start = (bf16[2,2048,512]{2,1,0:T(8,128)(2,1)S(1)}, bf16[2,2048,512]{2,1,0:T(8,128)(2,1)}, u32[]{:S(2)}) copy-start(bf16[2,2048,512]{2,1,0:T(8,128)(2,1)} %images_ref.3) | copy-start | bytes 12582916
  0.0 13.0 %copy-start.4 = (s32[8,4,4]{0,2,1:T(4,128)S(1)}, s32[8,4,4]{0,2,1:T(4,128)}, u32[]{:S(2)}) copy-start(s32[8,4,4]{0,2,1:T(4,128)} %param.15) | copy-start | bytes 1540
  0.0 13.0 %copy-start.6 = (s32[8,2]{0,1:T(2,128)S(1)}, s32[8,2]{0,1:T(2,128)}, u32[]{:S(2)}) copy-start(s32[8,2]{0,1:T(2,128)} %param.12) | copy-start | bytes 196
  0.0 16.2 %copy-start.1 = (bf16[512,512]{1,0:T(8,128)(2,1)S(1)}, bf16[512,512]{1,0:T(8,128)(2,1)}, u32[]{:S(2)}) copy-start(bf16[512,512]{1,0:T(8,128)(2,1)} %scene_ref.5) | copy-start | bytes 1572868
  5.7 20.1 %copy-start.2 = (bf16[512,512]{1,0:T(8,128)(2,1)S(1)}, bf16[512,512]{1,0:T(8,128)(2,1)}, u32[]{:S(2)}) copy-start(bf16[512,512]{1,0:T(8,128)(2,1)} %get-tuple-element.31.two_ref) | copy-start | bytes 1572868
  5.7 20.0 %collective-permute-start.2 = (bf16[512,512]{1,0:T(8,128)(2,1)}, bf16[512,512]{1,0:T(8,128)(2,1)S(1)}, u32[]{:S(2)}, u32[]{:S(2)}) collective-permute-start(bf16[512,512]{1,0:T(8,128)(2,1)} %get-tuple-element.27), channel_id=1, source_target_pairs={{0,4},{4,0},{8,12},{12,8},{1,5},{5,1},{9,13},{13,9},{2,6},{6,2},{1... | collective-permute-start | bytes 1572872 | tf_op jit(solution)/shard_map/ppermute | solution.py:829
  8.8 17.2 %collective-permute-start.4 = (bf16[512,512]{1,0:T(8,128)(2,1)}, bf16[512,512]{1,0:T(8,128)(2,1)S(1)}, u32[]{:S(2)}, u32[]{:S(2)}) collective-permute-start(bf16[512,512]{1,0:T(8,128)(2,1)} %get-tuple-element.31.two_ref), channel_id=1, source_target_pairs={{4,8},{8,4},{5,9},{9,5},{6,10},{10,6},{7,11},{11,7},{20,24},{24,20... | collective-permute-start | bytes 1572872 | tf_op jit(solution)/shard_map/ppermute | solution.py:830
  9.5 6.7 %collective-permute-start.1 = (bf16[784,128]{1,0:T(8,128)(2,1)}, bf16[784,128]{1,0:T(8,128)(2,1)S(1)}, u32[]{:S(2)}, u32[]{:S(2)}) collective-permute-start(bf16[784,128]{1,0:T(8,128)(2,1)} %get-tuple-element.26), channel_id=1, source_target_pairs={{1,2},{2,1},{5,6},{6,5},{9,10},{10,9},{13,14},{14,13},{17,18},{18,... | collective-permute-start | bytes 602120 | tf_op jit(solution)/shard_map/ppermute | solution.py:834
  10.1 6.1 %collective-permute-start = (bf16[784,128]{1,0:T(8,128)(2,1)}, bf16[784,128]{1,0:T(8,128)(2,1)S(1)}, u32[]{:S(2)}, u32[]{:S(2)}) collective-permute-start(bf16[784,128]{1,0:T(8,128)(2,1)} %get-tuple-element.25), channel_id=1, source_target_pairs={{0,1},{1,0},{2,3},{3,2},{4,5},{5,4},{6,7},{7,6},{8,9},{9,8},{10,11... | collective-permute-start | bytes 602120 | tf_op jit(solution)/shard_map/ppermute | solution.py:833
  18.1 7.8 %collective-permute-start.3 = (bf16[80,512]{1,0:T(8,128)(2,1)S(1)}, bf16[80,512]{1,0:T(8,128)(2,1)S(1)}, u32[]{:S(2)}, u32[]{:S(2)}) collective-permute-start(bf16[80,512]{1,0:T(8,128)(2,1)S(1)} %get-tuple-element.35), channel_id=1, source_target_pairs={{0,12},{12,0},{4,8},{8,4},{1,13},{13,1},{5,9},{9,5},{2,14},{14,2},... | collective-permute-start | bytes 245768 | tf_op jit(solution)/shard_map/ppermute | solution.py:839
  21.8 21.0 %collective-permute-start.5 = (bf16[560,512]{1,0:T(8,128)(2,1)S(1)}, bf16[560,512]{1,0:T(8,128)(2,1)S(1)}, u32[]{:S(2)}, u32[]{:S(2)}) collective-permute-start(bf16[560,512]{1,0:T(8,128)(2,1)S(1)} %early.1.near_ref), channel_id=1, source_target_pairs={{0,4},{12,8},{1,5},{13,9},{2,6},{14,10},{3,7},{15,11},{16,20},{28,... | collective-permute-start | bytes 1720328 | tf_op jit(solution)/shard_map/ppermute | solution.py:838
  25.9 24.8 %collective-permute-start.7 = (bf16[512,512]{1,0:T(8,128)(2,1)S(1)}, bf16[512,512]{1,0:T(8,128)(2,1)S(1)}, u32[]{:S(2)}, u32[]{:S(2)}) collective-permute-start(bf16[512,512]{1,0:T(8,128)(2,1)S(1)} %merge.1), channel_id=1, source_target_pairs={{0,8},{12,4},{4,12},{8,0},{1,9},{13,5},{5,13},{9,1},{2,10},{14,6},... | collective-permute-start | bytes 1572872 | tf_op jit(solution)/shard_map/ppermute | solution.py:842
  32.4 10.4 %collective-permute-start.6 = (bf16[80,512]{1,0:T(8,128)(2,1)S(1)}, bf16[80,512]{1,0:T(8,128)(2,1)S(1)}, u32[]{:S(2)}, u32[]{:S(2)}) collective-permute-start(bf16[80,512]{1,0:T(8,128)(2,1)S(1)} %get-tuple-element.42), channel_id=1, source_target_pairs={{4,0},{8,12},{5,1},{9,13},{6,2},{10,14},{7,3},{11,15},{20,16},{24,... | collective-permute-start | bytes 245768 | tf_op jit(solution)/shard_map/ppermute | solution.py:846

commit v7 on v6

--- a/solution.py
+++ b/solution.py
@@ -571,7 +571,10 @@
                 rim_parts[i] += part
     column_tile = column // TILE
     for i, target in enumerate(targets):
-        for copy in copies[3 * sz.local * i : 3 * sz.local * (i + 1)]:
+        wait = copies[3 * sz.local * i : 3 * sz.local * (i + 1)]
+        if not packs:
+            wait = copies if i == 0 else []
+        for copy in wait:
             copy.wait()
         for copy in edge_waits[0] + edge_waits[1] if packs and i == 0 else ():
             copy.start()

time: 52.2 us -> 52.2 us (level)
  no operation moved by 1% of the time
where the time goes in v7:
time: 52.2 us; the launch traced here: 51.8 us
  Pallas kernels  21.7 us (42%)
  starting transfers between devices  19.8 us (38%)
  waiting for transfers between devices  8.95 us (17%)
  other arithmetic  1.13 us (2%)
    ppermute x1, waiting for transfers between devices, on_device(): got_back = lax.ppermute(back, 'epoch', [(1, 0), (2, 3)])  8.93 us
    pallas_call x2, Pallas kernels, image_blocks(): pl.pallas_call(functools.partial(image_kernel, sz, slots, len(ends), pack...  8.57 us
    pallas_call x1, Pallas kernels, model_term(): pl.pallas_call(functools.partial(model_kernel, sz, batch), grid=(sz.epoch...  7.82 us
    ppermute x1, starting transfers between devices, on_device(): got_passed = lax.ppermute(passed, 'epoch', [(0, 2), (3, 1), (1, 3), (2, 0)])  4.56 us
    ppermute x1, starting transfers between devices, on_device(): got_three = lax.ppermute(near, 'epoch', [(0, 1), (3, 2)])  3.85 us
    ppermute x1, starting transfers between devices, on_device(): got_one = lax.ppermute(one, 'epoch', pairs(0, depth))  3.09 us
    ppermute x1, starting transfers between devices, on_device(): first = lax.ppermute(first, 'sky', pairs(0, peers))  2.9 us
    ppermute x1, starting transfers between devices, on_device(): got_far = lax.ppermute(far, 'epoch', [(0, 3), (3, 0), (1, 2), (2, 1)])  2.56 us
  transfers between devices with their start and end apart: 8, of which 1 were waited for; matrix products, arithmetic and copies ran while one was open for 0% of the time, Pallas kernels for 31%

profile of v7, /device:TPU:0, one launch (start us, length us, event | category | flops | bytes accessed | tf_op | source)
XLA Modules:
  0.0 51.8 jit_solution(7802716660855707420)
XLA Ops:
  0.0 0.0 copy-start.4
  0.0 0.0 copy-start.6
  0.0 0.0 copy-start.1
  0.0 5.6 %image_blocks.2 = (bf16[512,512]{1,0:T(8,128)(2,1)}, bf16[512,512]{1,0:T(8,128)(2,1)}, bf16[784,128]{1,0:T(8,128)(2,1)}, bf16[784,128]{1,0:T(8,128)(2,1)}) custom-call(bf16[2,2048,512]{2,1,0:T(8,128)(2,1)} %images_ref.3, s32[4,4,8]{2,1,0:T(4,128)} %bitcast.2, s32[2,8]{1,0:T(2,128)} %bitcast.6, f32[8]{0:T(128)} %weight_ref.3, s32[8,512]{1,0:T(8,128)} %mask_ref.1, ...), custom_call_target="tpu_custom_call" | custom-call | flops 1000 | bytes 1000 | tf_op jit(solution)/shard_map/image_blocks/pallas_call | solution.py:644
  5.7 0.0 copy-start.2
  5.7 3.1 %collective-permute-start.2 = (bf16[512,512]{1,0:T(8,128)(2,1)}, bf16[512,512]{1,0:T(8,128)(2,1)S(1)}, u32[]{:S(2)}, u32[]{:S(2)}) collective-permute-start(bf16[512,512]{1,0:T(8,128)(2,1)} %get-tuple-element.27), channel_id=1, source_target_pairs={{0,4},{4,0},{8,12},{12,8},{1,5},{5,1},{9,13},{13,9},{2,6},{6,2},{1... | collective-permute-start | bytes 1572872 | tf_op jit(solution)/shard_map/ppermute | solution.py:832
  8.8 0.7 %collective-permute-start.4 = (bf16[512,512]{1,0:T(8,128)(2,1)}, bf16[512,512]{1,0:T(8,128)(2,1)S(1)}, u32[]{:S(2)}, u32[]{:S(2)}) collective-permute-start(bf16[512,512]{1,0:T(8,128)(2,1)} %get-tuple-element.31.two_ref), channel_id=1, source_target_pairs={{4,8},{8,4},{5,9},{9,5},{6,10},{10,6},{7,11},{11,7},{20,24},{24,20... | collective-permute-start | bytes 1572872 | tf_op jit(solution)/shard_map/ppermute | solution.py:833
  9.5 0.7 %collective-permute-start.1 = (bf16[784,128]{1,0:T(8,128)(2,1)}, bf16[784,128]{1,0:T(8,128)(2,1)S(1)}, u32[]{:S(2)}, u32[]{:S(2)}) collective-permute-start(bf16[784,128]{1,0:T(8,128)(2,1)} %get-tuple-element.26), channel_id=1, source_target_pairs={{1,2},{2,1},{5,6},{6,5},{9,10},{10,9},{13,14},{14,13},{17,18},{18,... | collective-permute-start | bytes 602120 | tf_op jit(solution)/shard_map/ppermute | solution.py:837
  10.1 2.9 %collective-permute-start = (bf16[784,128]{1,0:T(8,128)(2,1)}, bf16[784,128]{1,0:T(8,128)(2,1)S(1)}, u32[]{:S(2)}, u32[]{:S(2)}) collective-permute-start(bf16[784,128]{1,0:T(8,128)(2,1)} %get-tuple-element.25), channel_id=1, source_target_pairs={{0,1},{1,0},{2,3},{3,2},{4,5},{5,4},{6,7},{7,6},{8,9},{9,8},{10,11... | collective-permute-start | bytes 602120 | tf_op jit(solution)/shard_map/ppermute | solution.py:836
  13.0 0.0 copy-done.5
  13.0 0.0 copy-done.8
  13.0 0.0 copy-done.7
  13.0 0.0 copy-done.3
  13.1 3.0 %image_blocks.3 = (bf16[512,512]{1,0:T(8,128)(2,1)S(1)}, bf16[512,512]{1,0:T(8,128)(2,1)S(1)}) custom-call(bf16[2,2048,512]{2,1,0:T(8,128)(2,1)S(1)} %copy-done, s32[4,4,8]{2,1,0:T(4,128)S(1)} %bitcast.3, s32[2,8]{1,0:T(2,128)S(1)} %bitcast.7, f32[8]{0:T(128)S(1)} %copy-done.8, s32[8,512]{1,0:T(8,128)S(1)} %copy-done.3, bf16[8,25]{1,0:T(8,128)(2,1)S(1)} %copy-done.7, ...), custom_call_target="tpu_custom_call" | custom-call | flops 1000 | bytes 1000 | tf_op jit(solution)/shard_map/image_blocks/pallas_call | solution.py:644
  16.1 0.0 collective-permute-done.1.second_ref
  16.1 0.0 collective-permute-done.first_ref
  16.1 1.8 %notes.1 = (bf16[80,512]{1,0:T(8,128)(2,1)S(1)}, bf16[2,256,256]{2,1,0:T(8,128)(2,1)S(1)}, bf16[512,256]{1,0:T(8,128)(2,1)S(1)}) custom-call(s32[4,4,8]{2,1,0:T(4,128)S(1)} %bitcast.4, s32[2,8]{1,0:T(2,128)S(1)} %bitcast.8, f32[8]{0:T(128)S(1)} %copy-done.8, bf16[512,512]{1,0:T(8,128)(2,1)S(1)} %copy-done.1, ...), custom_call_target="tpu_custom_call" | custom-call | flops 1000 | bytes 1000 | tf_op jit(solution)/shard_map/notes/pallas_call | solution.py:392
  17.9 2.6 %collective-permute-start.3 = (bf16[80,512]{1,0:T(8,128)(2,1)S(1)}, bf16[80,512]{1,0:T(8,128)(2,1)S(1)}, u32[]{:S(2)}, u32[]{:S(2)}) collective-permute-start(bf16[80,512]{1,0:T(8,128)(2,1)S(1)} %get-tuple-element.35), channel_id=1, source_target_pairs={{0,12},{12,0},{4,8},{8,4},{1,13},{13,1},{5,9},{9,5},{2,14},{14,2},... | collective-permute-start | bytes 245768 | tf_op jit(solution)/shard_map/ppermute | solution.py:842
  20.5 1.2 %early.1.near_ref = bf16[560,512]{1,0:T(8,128)(2,1)S(1)} custom-call(s32[2,8]{1,0:T(2,128)S(1)} %bitcast.9, bf16[512,512]{1,0:T(8,128)(2,1)S(1)} %copy-done.1, bf16[784,128]{1,0:T(8,128)(2,1)S(1)} %collective-permute-done.first_ref, bf16[784,128]{1,0:T(8,128)(2,1)S(1)} %collective-permute-done.1.second_ref, bf16[8,25]{1,0:T(8,128)(2,1)S(1)} %copy-done.5, ...), custom_call_target="tpu_custom_call" | custom-call | flops 1000 | bytes 1000 | tf_op jit(solution)/shard_map/early/pallas_call | solution.py:423
  21.7 3.8 %collective-permute-start.5 = (bf16[560,512]{1,0:T(8,128)(2,1)S(1)}, bf16[560,512]{1,0:T(8,128)(2,1)S(1)}, u32[]{:S(2)}, u32[]{:S(2)}) collective-permute-start(bf16[560,512]{1,0:T(8,128)(2,1)S(1)} %early.1.near_ref), channel_id=1, source_target_pairs={{0,4},{12,8},{1,5},{13,9},{2,6},{14,10},{3,7},{15,11},{16,20},{28,... | collective-permute-start | bytes 1720328 | tf_op jit(solution)/shard_map/ppermute | solution.py:841
  25.6 0.0 collective-permute-done.2.one_ref.more_1_
  25.6 0.2 merge.1
  25.8 0.0 collective-permute-done.3.more_5_
  25.8 0.0 collective-permute-done.4.more_2_
  25.8 4.6 %collective-permute-start.7 = (bf16[512,512]{1,0:T(8,128)(2,1)S(1)}, bf16[512,512]{1,0:T(8,128)(2,1)S(1)}, u32[]{:S(2)}, u32[]{:S(2)}) collective-permute-start(bf16[512,512]{1,0:T(8,128)(2,1)S(1)} %merge.1), channel_id=1, source_target_pairs={{0,8},{12,4},{4,12},{8,0},{1,9},{13,5},{5,13},{9,1},{2,10},{14,6},... | collective-permute-start | bytes 1572872 | tf_op jit(solution)/shard_map/ppermute | solution.py:845
  30.4 2.1 %finish.1 = (bf16[512,640]{1,0:T(8,128)(2,1)S(1)}, f32[16,640]{1,0:T(8,128)S(1)}, bf16[80,512]{1,0:T(8,128)(2,1)S(1)}, bf16[512,512]{1,0:T(8,128)(2,1)S(1)}) custom-call(s32[2,8]{1,0:T(2,128)S(1)} %bitcast.10, bf16[512,512]{1,0:T(8,128)(2,1)S(1)} %copy-done.1, s32[8,512]{1,0:T(8,128)S(1)} %copy-done.3, bf16[784,128]{1,0:T(8,128)(2,1)S(1)} %collective-permute-done.first_ref, ...), custom_call_target="tpu_custom_call" | custom-call | flops 1000 | bytes 1000 | tf_op jit(solution)/shard_map/finish/pallas_call | solution.py:490
  32.4 1.5 %collective-permute-start.6 = (bf16[80,512]{1,0:T(8,128)(2,1)S(1)}, bf16[80,512]{1,0:T(8,128)(2,1)S(1)}, u32[]{:S(2)}, u32[]{:S(2)}) collective-permute-start(bf16[80,512]{1,0:T(8,128)(2,1)S(1)} %get-tuple-element.42), channel_id=1, source_target_pairs={{4,0},{8,12},{5,1},{9,13},{6,2},{10,14},{7,3},{11,15},{20,16},{24,... | collective-permute-start | bytes 245768 | tf_op jit(solution)/shard_map/ppermute | solution.py:849
  33.9 8.9 %collective-permute-done.6.more_4_ = bf16[80,512]{1,0:T(8,128)(2,1)S(1)} collective-permute-done((bf16[80,512]{1,0:T(8,128)(2,1)S(1)}, bf16[80,512]{1,0:T(8,128)(2,1)S(1)}, u32[]{:S(2)}, u32[]{:S(2)}) %collective-permute-start.6) | collective-permute-done | bytes 81952 | tf_op jit(solution)/shard_map/ppermute | solution.py:849
  42.8 0.0 collective-permute-done.5.more_3_
  42.8 7.8 %model_term.1 = f32[512,512]{1,0:T(8,128)S(1)} custom-call(s32[4,4,8]{2,1,0:T(4,128)S(1)} %bitcast.5, s32[2,8]{1,0:T(2,128)S(1)} %bitcast.11, f32[8]{0:T(128)S(1)} %copy-done.8, bf16[512,640]{1,0:T(8,128)(2,1)S(1)} %get-tuple-element.38.wide_ref, f32[16,640]{1,0:T(8,128)S(1)} %get-tuple-element.39.good_ref, bf16[8,25]{1,0:T(8,128)(2,1)S(1)} %copy-done.7, ...), custom_call_target="tpu_custom_call" | custom-call | flops 1000 | bytes 1000 | tf_op jit(solution)/shard_map/model_term/pallas_call | solution.py:794
  50.7 0.0 collective-permute-done.7
  50.7 1.1 %convert_add_fusion = f32[512,512]{1,0:T(8,128)} fusion(f32[512,512]{1,0:T(8,128)S(1)} %model_term.1, bf16[512,512]{1,0:T(8,128)(2,1)S(1)} %collective-permute-done.7), kind=kLoop, calls=%fused_computation | loop fusion | flops 524288 | bytes 2621440 | tf_op jit(solution)/shard_map/add | solution.py:854
  (10 shorter events, 0.0 us)
Async XLA Ops:
  0.0 13.0 %copy-start.5 = (bf16[8,25]{1,0:T(8,128)(2,1)S(1)}, bf16[8,25]{1,0:T(8,128)(2,1)}, u32[]{:S(2)}) copy-start(bf16[8,25]{1,0:T(8,128)(2,1)} %psf_cols_ref.5) | copy-start | bytes 1204
  0.0 13.0 %copy-start.8 = (f32[8]{0:T(128)S(1)}, f32[8]{0:T(128)}, u32[]{:S(2)}) copy-start(f32[8]{0:T(128)} %weight_ref.3) | copy-start | bytes 100
  0.0 13.0 %copy-start.7 = (bf16[8,25]{1,0:T(8,128)(2,1)S(1)}, bf16[8,25]{1,0:T(8,128)(2,1)}, u32[]{:S(2)}) copy-start(bf16[8,25]{1,0:T(8,128)(2,1)} %psf_rows_ref.3) | copy-start | bytes 1204
  0.0 13.0 %copy-start.3 = (s32[8,512]{1,0:T(8,128)S(1)}, s32[8,512]{1,0:T(8,128)}, u32[]{:S(2)}) copy-start(s32[8,512]{1,0:T(8,128)} %mask_ref.1) | copy-start | bytes 49156
  0.0 13.0 %copy-start = (bf16[2,2048,512]{2,1,0:T(8,128)(2,1)S(1)}, bf16[2,2048,512]{2,1,0:T(8,128)(2,1)}, u32[]{:S(2)}) copy-start(bf16[2,2048,512]{2,1,0:T(8,128)(2,1)} %images_ref.3) | copy-start | bytes 12582916
  0.0 13.0 %copy-start.4 = (s32[8,4,4]{0,2,1:T(4,128)S(1)}, s32[8,4,4]{0,2,1:T(4,128)}, u32[]{:S(2)}) copy-start(s32[8,4,4]{0,2,1:T(4,128)} %param.15) | copy-start | bytes 1540
  0.0 13.0 %copy-start.6 = (s32[8,2]{0,1:T(2,128)S(1)}, s32[8,2]{0,1:T(2,128)}, u32[]{:S(2)}) copy-start(s32[8,2]{0,1:T(2,128)} %param.12) | copy-start | bytes 196
  0.0 16.0 %copy-start.1 = (bf16[512,512]{1,0:T(8,128)(2,1)S(1)}, bf16[512,512]{1,0:T(8,128)(2,1)}, u32[]{:S(2)}) copy-start(bf16[512,512]{1,0:T(8,128)(2,1)} %scene_ref.5) | copy-start | bytes 1572868
  5.7 19.9 %copy-start.2 = (bf16[512,512]{1,0:T(8,128)(2,1)S(1)}, bf16[512,512]{1,0:T(8,128)(2,1)}, u32[]{:S(2)}) copy-start(bf16[512,512]{1,0:T(8,128)(2,1)} %get-tuple-element.31.two_ref) | copy-start | bytes 1572868
  5.7 19.9 %collective-permute-start.2 = (bf16[512,512]{1,0:T(8,128)(2,1)}, bf16[512,512]{1,0:T(8,128)(2,1)S(1)}, u32[]{:S(2)}, u32[]{:S(2)}) collective-permute-start(bf16[512,512]{1,0:T(8,128)(2,1)} %get-tuple-element.27), channel_id=1, source_target_pairs={{0,4},{4,0},{8,12},{12,8},{1,5},{5,1},{9,13},{13,9},{2,6},{6,2},{1... | collective-permute-start | bytes 1572872 | tf_op jit(solution)/shard_map/ppermute | solution.py:832
  8.8 17.0 %collective-permute-start.4 = (bf16[512,512]{1,0:T(8,128)(2,1)}, bf16[512,512]{1,0:T(8,128)(2,1)S(1)}, u32[]{:S(2)}, u32[]{:S(2)}) collective-permute-start(bf16[512,512]{1,0:T(8,128)(2,1)} %get-tuple-element.31.two_ref), channel_id=1, source_target_pairs={{4,8},{8,4},{5,9},{9,5},{6,10},{10,6},{7,11},{11,7},{20,24},{24,20... | collective-permute-start | bytes 1572872 | tf_op jit(solution)/shard_map/ppermute | solution.py:833
  9.5 6.6 %collective-permute-start.1 = (bf16[784,128]{1,0:T(8,128)(2,1)}, bf16[784,128]{1,0:T(8,128)(2,1)S(1)}, u32[]{:S(2)}, u32[]{:S(2)}) collective-permute-start(bf16[784,128]{1,0:T(8,128)(2,1)} %get-tuple-element.26), channel_id=1, source_target_pairs={{1,2},{2,1},{5,6},{6,5},{9,10},{10,9},{13,14},{14,13},{17,18},{18,... | collective-permute-start | bytes 602120 | tf_op jit(solution)/shard_map/ppermute | solution.py:837
  10.1 5.9 %collective-permute-start = (bf16[784,128]{1,0:T(8,128)(2,1)}, bf16[784,128]{1,0:T(8,128)(2,1)S(1)}, u32[]{:S(2)}, u32[]{:S(2)}) collective-permute-start(bf16[784,128]{1,0:T(8,128)(2,1)} %get-tuple-element.25), channel_id=1, source_target_pairs={{0,1},{1,0},{2,3},{3,2},{4,5},{5,4},{6,7},{7,6},{8,9},{9,8},{10,11... | collective-permute-start | bytes 602120 | tf_op jit(solution)/shard_map/ppermute | solution.py:836
  17.9 7.8 %collective-permute-start.3 = (bf16[80,512]{1,0:T(8,128)(2,1)S(1)}, bf16[80,512]{1,0:T(8,128)(2,1)S(1)}, u32[]{:S(2)}, u32[]{:S(2)}) collective-permute-start(bf16[80,512]{1,0:T(8,128)(2,1)S(1)} %get-tuple-element.35), channel_id=1, source_target_pairs={{0,12},{12,0},{4,8},{8,4},{1,13},{13,1},{5,9},{9,5},{2,14},{14,2},... | collective-permute-start | bytes 245768 | tf_op jit(solution)/shard_map/ppermute | solution.py:842
  21.7 21.1 %collective-permute-start.5 = (bf16[560,512]{1,0:T(8,128)(2,1)S(1)}, bf16[560,512]{1,0:T(8,128)(2,1)S(1)}, u32[]{:S(2)}, u32[]{:S(2)}) collective-permute-start(bf16[560,512]{1,0:T(8,128)(2,1)S(1)} %early.1.near_ref), channel_id=1, source_target_pairs={{0,4},{12,8},{1,5},{13,9},{2,6},{14,10},{3,7},{15,11},{16,20},{28,... | collective-permute-start | bytes 1720328 | tf_op jit(solution)/shard_map/ppermute | solution.py:841
  25.8 24.9 %collective-permute-start.7 = (bf16[512,512]{1,0:T(8,128)(2,1)S(1)}, bf16[512,512]{1,0:T(8,128)(2,1)S(1)}, u32[]{:S(2)}, u32[]{:S(2)}) collective-permute-start(bf16[512,512]{1,0:T(8,128)(2,1)S(1)} %merge.1), channel_id=1, source_target_pairs={{0,8},{12,4},{4,12},{8,0},{1,9},{13,5},{5,13},{9,1},{2,10},{14,6},... | collective-permute-start | bytes 1572872 | tf_op jit(solution)/shard_map/ppermute | solution.py:845
  32.4 10.4 %collective-permute-start.6 = (bf16[80,512]{1,0:T(8,128)(2,1)S(1)}, bf16[80,512]{1,0:T(8,128)(2,1)S(1)}, u32[]{:S(2)}, u32[]{:S(2)}) collective-permute-start(bf16[80,512]{1,0:T(8,128)(2,1)S(1)} %get-tuple-element.42), channel_id=1, source_target_pairs={{4,0},{8,12},{5,1},{9,13},{6,2},{10,14},{7,3},{11,15},{20,16},{24,... | collective-permute-start | bytes 245768 | tf_op jit(solution)/shard_map/ppermute | solution.py:849
